TPU v7x, 512 devices: a whole 4x4x16 slice. The times are simulated.
512 devices in a mesh: texel: 32 (over x, y, core), light: 16 (over z).
Axes of the slice: x: 4, y: 4, z: 16, core: 2. Of those that a mesh axis runs over, the one named last changes fastest.
Arguments:
- tex_feat: bfloat16 [32768, 512], P('texel'), may hold values from -18 to 18
- light_feat: bfloat16 [24576, 512], P('light'), may hold values from -0.25 to 0.25
- sketch: bfloat16 [24576, 256], P('light'), may hold values from -0.0390625 to 0.0390625
- row_counts: int32 [32], replicated, may hold values from 1 to 1024, 16384 in all
Outputs:
- basis: float32 [32768, 256], P('texel')
- coeffs: float32 [256, 24576], P('texel', 'light')
Inputs may be any that keep to these rules, and one draw needn't show every extreme that they name: row_counts sums to 32 * 512; some entry equals 1024.
All inputs are finite; a program needn't handle non-finite values.
Results may differ from a plain program's by a relative error of at most 0.0034.
Values sent between devices are 32-bit elements; how exact they have to be, the bound alone decides.
No kernel may reach another device: no remote copies, remote signals or barrier semaphores. Data moves between devices by JAX's collectives and lax.ppermute only.
A program may use at most 64 MiB of HBM per device.

v0:
```python
import jax
import jax.numpy as jnp
from jax import lax
from jax.sharding import PartitionSpec as P


def rows_for(lines, count):
    spare = -lines.shape[0] % count
    if not spare:
        return lines
    return jnp.concatenate([lines, jnp.zeros((spare, *lines.shape[1:]), lines.dtype)])


def sent_to_all(shard, axis):
    copies = jnp.broadcast_to(shard, (lax.axis_size(axis), *shard.shape))
    return lax.all_to_all(copies, axis, split_axis=0, concat_axis=0, tiled=True)


def joined_along(parts, dim):
    shape = list(parts.shape[1:])
    shape[dim] *= parts.shape[0]
    return jnp.moveaxis(parts, 0, dim).reshape(shape)


def gather_directly(shard, axis, dim):
    parts = sent_to_all(shard, axis)
    return joined_along(parts, dim)


def in_blocks(shard, dim, count):
    shape = shard.shape
    parts = shard.reshape(*shape[:dim], count, shape[dim] // count, *shape[dim + 1 :])
    return jnp.moveaxis(parts, dim, 0)


def sum_at_owner(shard, axis, dim):
    count = lax.axis_size(axis)
    parts = lax.all_to_all(in_blocks(shard, dim, count), axis, 0, 0, tiled=True)
    return jnp.sum(parts, axis=0)


def total_of(shard, axes):
    lines = shard.reshape(-1, shard.shape[-1])
    padded = rows_for(lines, lax.axis_size(axes))
    whole = gather_directly(sum_at_owner(padded, axes, 0), axes, 0)
    return lax.slice_in_dim(whole, 0, len(lines)).reshape(shard.shape)


def on_device(tex_feat, light_feat, sketch, row_counts):
    capacity = tex_feat.shape[0]
    own_count = row_counts[lax.axis_index("texel")]
    valid_total = jnp.sum(row_counts).astype(jnp.float32)
    logits = lax.dot_general(
        tex_feat, light_feat, (((1,), (1,)), ((), ())), preferred_element_type=jnp.float32
    )
    tile_block = jnp.sin(logits).astype(jnp.bfloat16)
    row_valid = (lax.iota(jnp.int32, capacity) < own_count).astype(jnp.float32)
    partial_value = (
        jnp.dot(tile_block, sketch, preferred_element_type=jnp.float32) * row_valid[:, None]
    )
    sketched = total_of(partial_value, "light")
    gram_local = jnp.dot(sketched.T, sketched, precision=lax.Precision.HIGHEST)
    gram_matrix = total_of(gram_local, "texel") / valid_total
    factor = jnp.linalg.cholesky(gram_matrix)
    basis = jax.scipy.linalg.solve_triangular(factor, sketched.T, lower=True).T
    basis_half = basis.astype(jnp.bfloat16)
    coeffs = sum_at_owner(
        lax.dot_general(
            basis_half, tile_block, (((0,), (0,)), ((), ())), preferred_element_type=jnp.float32
        ),
        "texel",
        0,
    ) / jnp.sqrt(valid_total)
    return (basis, coeffs)


def solution(mesh):
    placed = (P("texel", None), P("light", None), P("light", None), P())
    return jax.shard_map(
        on_device,
        mesh=mesh,
        in_specs=placed,
        out_specs=(P("texel", None), P("texel", "light")),
        check_vma=False,
    )
```

profile of v0, /device:TPU:1, one launch (start us, length us, event | category | flops | bytes accessed | tf_op | source)
XLA Modules:
  0.0 281.7 jit_solution(17492901387551761789)
XLA Ops:
  0.6 1.4 dynamic_slice.3
  2.0 0.6 fusion.11
  2.7 23.0 %sine_convert_fusion = bf16[1024,1536]{1,0:T(8,128)(2,1)S(1)} fusion(bf16[1024,512]{1,0:T(8,128)(2,1)} %param.4, bf16[1536,512]{1,0:T(8,128)(2,1)S(1)} %copy-done), kind=kOutput, calls=%fused_computation.2 | convolution fusion | flops 1612185600 | bytes 5767168 | tf_op jit(solution)/shard_map/dot_general | solution.py:53
  25.7 1.0 convolution_multiply_fusion
  26.7 0.7 copy-done.1
  27.4 60.8 %all_to_all.25 = f32[16,64,256]{2,1,0:T(8,128)S(1)} all-to-all(f32[16,64,256]{2,1,0:T(8,128)S(1)} %bitcast.62), channel_id=1, replica_groups=mesh['texel'=32,'light'=16] {'light'}, dimensions={0} | all-to-all | bytes 2097152 | tf_op jit(solution)/shard_map/all_to_all | solution.py:38
  88.3 57.7 %all_to_all.26 = f32[16,64,256]{2,1,0:T(8,128)S(1)} all-to-all(f32[16,64,256]{2,1,0:T(8,128)S(1)} %broadcast_in_dim.9), channel_id=1, replica_groups=mesh['texel'=32,'light'=16] {'light'}, dimensions={0} | all-to-all | bytes 2097152 | tf_op jit(solution)/shard_map/all_to_all | solution.py:16
  146.0 1.3 copy.9
  147.4 2.2 fusion
  149.6 23.0 %all_to_all.27 = f32[32,8,256]{2,1,0:T(8,128)S(1)} all-to-all(f32[32,8,256]{2,1,0:T(8,128)S(1)} %fusion), channel_id=1, replica_groups=mesh['texel'=32,'light'=16] {'texel'}, dimensions={0} | all-to-all | bytes 524288 | tf_op jit(solution)/shard_map/all_to_all | solution.py:38
  172.7 0.7 broadcast_in_dim.10
  173.4 3.8 %all-to-all-start.3 = ((f32[32,8,256]{2,1,0:T(8,128)}), f32[32,8,256]{2,1,0:T(8,128)S(1)}, u32[]{:S(2)}, u32[]{:S(2)}) async-start(f32[32,8,256]{2,1,0:T(8,128)} %broadcast_in_dim.10), calls=%async_computation.3 | async-start | bytes 524288 | tf_op jit(solution)/shard_map/all_to_all | solution.py:16
  177.3 0.6 reduce_sum.38
  178.5 7.7 %all-to-all-done.3 = f32[32,8,256]{2,1,0:T(8,128)S(1)} async-done(((f32[32,8,256]{2,1,0:T(8,128)}), f32[32,8,256]{2,1,0:T(8,128)S(1)}, u32[]{:S(2)}, u32[]{:S(2)}) %all-to-all-start.3) | async-done | bytes 262176 | tf_op jit(solution)/shard_map/all_to_all | solution.py:16
  186.4 11.7 %cholesky.50 = f32[128,128]{1,0:T(8,128)S(1)} custom-call(f32[128,128]{1,0:T(8,128)S(1)} %cholesky.118), custom_call_target="Cholesky" | custom-call | tf_op jit(solution)/shard_map/jit(cholesky)/cholesky | solution.py:64
  198.2 9.8 %custom-call.15 = f32[1,128,128]{1,2,0:T(8,128)S(1)} custom-call(f32[1,128,128]{2,1,0:T(8,128)S(1)} %get-tuple-element.27), custom_call_target="InvertDiagBlocksLowerTriangular" | custom-call | tf_op jit(solution)/shard_map/jit(cholesky)/cholesky | solution.py:64
  208.5 11.7 %cholesky.105 = f32[128,128]{1,0:T(8,128)S(1)} custom-call(f32[128,128]{1,0:T(8,128)S(1)} %convolution_subtract_fusion.1), custom_call_target="Cholesky" | custom-call | tf_op jit(solution)/shard_map/jit(cholesky)/cholesky | solution.py:64
  220.3 0.6 compare_reduce_fusion
  222.2 5.0 %while.1 = (s32[]{:T(128)}, f32[256,256]{1,0:T(8,128)S(1)}, s32[2,2]{1,0:T(2,128)S(1)}, f32[2,128,128]{2,1,0:T(8,128)}, s32[]{:T(128)}) while((s32[]{:T(128)}, f32[256,256]{1,0:T(8,128)S(1)}, s32[2,2]{1,0:T(2,128)S(1)}, f32[2,128,128]{2,1,0:T(8,128)}, s32[]{:T(128)}) %tuple.29), condition=%wide.while_cond, body=%wide.while_body.sunk | while | flops 2 | bytes 132205 | solution.py:65
  222.8 1.9 bitcast_dynamic-update-slice_fusion.2
  225.3 1.9 bitcast_dynamic-update-slice_fusion.2
  227.3 20.5 %custom-call.16 = f32[2,128,128]{1,2,0:T(8,128)S(1)} custom-call(f32[2,128,128]{2,1,0:T(8,128)} %get-tuple-element.9), custom_call_target="InvertDiagBlocksLowerTriangular" | custom-call | tf_op jit(solution)/shard_map/jit(_solve_triangular)/triangular_solve | solution.py:65
  247.8 0.6 fusion.2
  248.4 1.0 convolution_subtract_fusion
  249.4 0.6 fusion.7
  250.1 2.2 convolution_bitcast_fusion
  252.2 4.5 %all-to-all-start.4 = ((f32[32,8,1536]{2,1,0:T(8,128)}), f32[32,8,1536]{2,1,0:T(8,128)}, u32[]{:S(2)}, u32[]{:S(2)}) async-start(f32[32,8,1536]{2,1,0:T(8,128)} %convolution_bitcast_fusion), calls=%async_computation.4 | async-start | bytes 3145728 | tf_op jit(solution)/shard_map/all_to_all | solution.py:38
  256.8 1.1 maximum_bitcast_fusion
  257.8 2.5 copy.11
  260.4 19.2 %all-to-all-done.4 = f32[32,8,1536]{2,1,0:T(8,128)} async-done(((f32[32,8,1536]{2,1,0:T(8,128)}), f32[32,8,1536]{2,1,0:T(8,128)}, u32[]{:S(2)}, u32[]{:S(2)}) %all-to-all-start.4) | async-done | bytes 1572896 | tf_op jit(solution)/shard_map/all_to_all | solution.py:38
  279.5 1.5 reduce_sum.39
  281.0 0.6 broadcast_divide_fusion
  (29 shorter events, 2.3 us)
Async XLA Ops:
  0.6 2.0 copy-start
  2.7 23.0 %copy-start.3 = (bf16[1536,256]{1,0:T(8,128)(2,1)S(1)}, bf16[1536,256]{1,0:T(8,128)(2,1)}, u32[]{:S(2)}) copy-start(bf16[1536,256]{1,0:T(8,128)(2,1)} %param.6) | copy-start | bytes 2359300
  25.7 1.7 copy-start.1
  146.0 31.2 %copy-start.4 = (s32[32]{0:T(128)S(1)}, s32[32]{0:T(128)}, u32[]{:S(2)}) copy-start(s32[32]{0:T(128)} %param.7) | copy-start | bytes 388
  173.4 12.8 %all-to-all-start.3 = ((f32[32,8,256]{2,1,0:T(8,128)}), f32[32,8,256]{2,1,0:T(8,128)S(1)}, u32[]{:S(2)}, u32[]{:S(2)}) async-start(f32[32,8,256]{2,1,0:T(8,128)} %broadcast_in_dim.10), calls=%async_computation.3 | async-start | bytes 524288 | tf_op jit(solution)/shard_map/all_to_all | solution.py:16
  247.8 2.3 copy-start.2
  252.2 27.3 %all-to-all-start.4 = ((f32[32,8,1536]{2,1,0:T(8,128)}), f32[32,8,1536]{2,1,0:T(8,128)}, u32[]{:S(2)}, u32[]{:S(2)}) async-start(f32[32,8,1536]{2,1,0:T(8,128)} %convolution_bitcast_fusion), calls=%async_computation.4 | async-start | bytes 3145728 | tf_op jit(solution)/shard_map/all_to_all | solution.py:38
where the time goes:
time: 282 us
  blocking collectives  142 us (50%)
  other arithmetic  59.1 us (21%)
  matrix products  31.1 us (11%)
  waiting for transfers between devices  26.9 us (10%)
  local copies, waits for them, and re-layouts  12 us (4%)
  starting transfers between devices  8.33 us (3%)
    all_to_all x2, blocking collectives, sum_at_owner(): parts = lax.all_to_all(in_blocks(shard, dim, count), axis, 0, 0, tiled=True)  83.8 us
    all_to_all x1, blocking collectives, sent_to_all(): return lax.all_to_all(copies, axis, split_axis=0, concat_axis=0, tiled=True)  57.7 us
    another operation x6, other arithmetic, on_device(): factor = jnp.linalg.cholesky(gram_matrix)  34 us
    dot_general x1, matrix products, on_device(): lax.dot_general(tex_feat, light_feat, (((1,), (1,)), ((), ())), preferred...  23 us
    another operation x3, other arithmetic, on_device(): basis = jax.scipy.linalg.solve_triangular(factor, sketched.T, lower=True).T  20.5 us
    all_to_all x1, waiting for transfers between devices, sum_at_owner(): parts = lax.all_to_all(in_blocks(shard, dim, count), axis, 0, 0, tiled=True)  19.2 us
    all_to_all x1, waiting for transfers between devices, sent_to_all(): return lax.all_to_all(copies, axis, split_axis=0, concat_axis=0, tiled=True)  7.75 us
  transfers between devices with their start and end apart: 2, of which 2 were waited for; matrix products, arithmetic and copies ran while one was open for 1% of the time, Pallas kernels for 0%

commit v1 on v0

v1 whole, which is shorter than its diff:
```python
import math

import jax
import jax.numpy as jnp
import numpy as np
from jax import lax
from jax.experimental import pallas as pl
from jax.experimental.pallas import tpu as pltpu
from jax.sharding import Mesh, PartitionSpec as P

F32 = jnp.float32
BF16 = jnp.bfloat16
TEXEL = ("x", "y", "core")
FAR = ("z3", "z2", "z1")
LIGHT = FAR + ("z0",)
HIGHEST = lax.Precision.HIGHEST
VMEM_LIMIT = 48 * 2**20


def sine_coefficients():
    angle = (np.arange(4000) + 0.5) * math.pi / 4000
    u = 0.125 * (1 + np.cos(angle)) + 1e-9
    w = 1.0
    basis = np.stack([u ** (2 * i + 1) for i in range(5)], axis=1)
    fit, *_ = np.linalg.lstsq(basis / w, np.sin(2 * math.pi * u) / w, rcond=None)
    return [float(c) for c in fit]


SINE = sine_coefficients()
ROUNDER = float(1.5 * 2**23)


def sine(x):
    turns = x * F32(1 / (2 * math.pi))
    part = turns - ((turns + F32(ROUNDER)) - F32(ROUNDER))
    part = jnp.maximum(jnp.minimum(part, F32(0.5) - part), F32(-0.5) - part)
    sq = part * part
    value = F32(SINE[4])
    for c in SINE[3::-1]:
        value = value * sq + F32(c)
    return value * part


def dot(a, b, contract, precision=None):
    return lax.dot_general(
        a, b, ((contract[0:1], contract[1:2]), ((), ())), precision=precision, preferred_element_type=F32
    )


def tile_kernel(where_ref, counts_ref, tex_ref, light_ref, sketch_ref, tile_ref, part_ref, *, half, rows, blocks):
    first = (half + where_ref[1]) % 2 * (blocks * rows) + pl.program_id(0) * rows
    tile = sine(dot(tex_ref[...], light_ref[...], (1, 1))).astype(BF16)
    tile_ref[...] = tile
    part = dot(tile, sketch_ref[...], (1, 0))
    row = first + lax.broadcasted_iota(jnp.int32, part.shape, 0)
    part_ref[...] = jnp.where(row < counts_ref[where_ref[0]], part, 0.0)


def tile_call(half, where, counts, tex, light, sketch, rows=128):
    capacity, features = tex.shape
    lights, width = sketch.shape
    blocks = capacity // 2 // rows

    def tex_at(i, where_ref, counts_ref):
        return ((half + where_ref[1]) % 2 * blocks + i, 0)

    return pl.pallas_call(
        lambda *refs: tile_kernel(*refs, half=half, rows=rows, blocks=blocks),
        out_shape=(
            jax.ShapeDtypeStruct((capacity // 2, lights), BF16),
            jax.ShapeDtypeStruct((capacity // 2, width), F32),
        ),
        grid_spec=pltpu.PrefetchScalarGridSpec(
            num_scalar_prefetch=2,
            grid=(blocks,),
            in_specs=[
                pl.BlockSpec((rows, features), tex_at),
                pl.BlockSpec((lights, features), lambda i, *_: (0, 0)),
                pl.BlockSpec((lights, width), lambda i, *_: (0, 0)),
            ],
            out_specs=(
                pl.BlockSpec((rows, lights), lambda i, *_: (i, 0)),
                pl.BlockSpec((rows, width), lambda i, *_: (i, 0)),
            ),
        ),
        compiler_params=pltpu.CompilerParams(vmem_limit_bytes=VMEM_LIMIT),
        cost_estimate=pl.CostEstimate(
            flops=capacity * lights * (features + width), bytes_accessed=4 * 2**20, transcendentals=0
        ),
        name="tile_half",
    )(where, counts, tex, light, sketch)


def gram_kernel(own_ref, other_ref, gram_ref):
    gram_ref[...] = dot(own_ref[...], own_ref[...], (0, 0), HIGHEST) + dot(
        other_ref[...], other_ref[...], (0, 0), HIGHEST
    )


def invert_factor(gram, y_ref, a_ref, w_ref):
    size = gram.shape[0]
    row = lax.broadcasted_iota(jnp.int32, (size, size), 0)
    col = lax.broadcasted_iota(jnp.int32, (size, size), 1)
    diagonal = jnp.sum(jnp.where(row == col, gram, 0.0), axis=0, keepdims=True)
    a_ref[...] = gram
    y_ref[...] = jnp.where(row == col, lax.rsqrt(diagonal), 0.0)

    def refine(exact):
        precision = HIGHEST if exact else None
        cast = (lambda v: v) if exact else (lambda v: v.astype(BF16))
        y = cast(y_ref[...])
        product = dot(dot(y, cast(a_ref[...]), (1, 0), precision).astype(y.dtype), y, (1, 1), precision)
        off = product - jnp.where(row == col, F32(1), F32(0))
        step = jnp.where(row > col, off, jnp.where(row == col, 0.5 * off, 0.0))
        y_ref[...] = y_ref[...] - dot(cast(step), y, (1, 0), precision)
        return jnp.sum(off * off)

    def coarse(state):
        count, _ = state
        return count + 1, refine(False)

    def fine(state):
        count, _ = state
        return count + 1, refine(True)

    lax.while_loop(lambda s: (s[0] < 8) & (s[1] > 2e-2), coarse, (jnp.int32(0), F32(1)))
    _, rest = lax.while_loop(lambda s: (s[0] < 8) & (s[1] > 4e-6), fine, (jnp.int32(0), F32(1)))

    @pl.when(jnp.logical_not(rest <= 4e-6))
    def _():
        y_ref[...] = jnp.where(row == col, F32(1), F32(0))
        line = lax.broadcasted_iota(jnp.int32, (size, 1), 0)
        w_ref[...] = gram

        def eliminate(j, carry):
            work = w_ref[...]
            column = jnp.sum(jnp.where(col == j, work, 0.0), axis=1, keepdims=True)
            pivot = lax.rsqrt(jnp.sum(jnp.where(line == j, column, 0.0), axis=0, keepdims=True))
            top = w_ref[pl.ds(j, 1), :] * pivot
            top_y = y_ref[pl.ds(j, 1), :] * pivot
            factor = jnp.where(line > j, column * pivot, 0.0)
            w_ref[...] = work - factor * top
            y_ref[...] = jnp.where(line == j, top_y, y_ref[...] - factor * top_y)
            return carry

        lax.fori_loop(0, size, eliminate, 0)


def basis_kernel(
    where_ref, counts_ref, gram_ref, own_ref, other_ref, tile_own_ref, tile_other_ref,
    basis_ref, keep_ref, send_ref, y_ref, a_ref, w_ref, coeff_ref,
):
    total = F32(0)
    for i in range(counts_ref.shape[0]):
        total = total + counts_ref[i].astype(F32)
    gram = gram_ref[...] / total
    invert_factor(gram, y_ref, a_ref, w_ref)
    inverse = y_ref[...]
    half = own_ref.shape[0]
    own = dot(own_ref[...], inverse, (1, 1), HIGHEST)
    other = dot(other_ref[...], inverse, (1, 1), HIGHEST)
    parity = where_ref[1]
    basis_ref[pl.ds(pl.multiple_of(parity * half, half), half), :] = own
    basis_ref[pl.ds(pl.multiple_of((1 - parity) * half, half), half), :] = other
    coeffs = dot(own.astype(BF16), tile_own_ref[...], (0, 0)) + dot(other.astype(BF16), tile_other_ref[...], (0, 0))
    scale = 1.0 / jnp.sqrt(jnp.full((1, 1), total, F32))
    coeff_ref[...] = (coeffs * scale).reshape(coeff_ref.shape)
    core = where_ref[2]
    for i in range(keep_ref.shape[0]):
        keep_ref[i] = coeff_ref[2 * i + core]
        send_ref[i] = coeff_ref[2 * i + 1 - core]


def core_pairs():
    return [(i, i ^ 1) for i in range(2)]


def light_pairs(count):
    pairs = []
    for core in range(2):
        for z in range(count):
            other = z ^ 1 if core == 0 else ((((z - 1) % count) ^ 1) + 1) % count
            pairs.append((core * count + z, core * count + other))
    return pairs


def with_neighbour(value):
    return lax.ppermute(value, ("core", *LIGHT), light_pairs(lax.axis_size(LIGHT)))


def each_to_each(parts, axes):
    return lax.all_to_all(parts, axes, 0, 0, tiled=True)


def on_device(tex_feat, light_feat, sketch, row_counts):
    capacity, width = tex_feat.shape[0], sketch.shape[1]
    lights = light_feat.shape[0]
    half = capacity // 2
    texels, far = lax.axis_size(TEXEL), lax.axis_size(FAR)
    where = jnp.stack([lax.axis_index(TEXEL), lax.axis_index("z0"), lax.axis_index("core")]).astype(jnp.int32)

    tile_other, part_other = tile_call(1, where, row_counts, tex_feat, light_feat, sketch)
    arrived = with_neighbour(part_other)
    tile_own, part_own = tile_call(0, where, row_counts, tex_feat, light_feat, sketch)
    shares = each_to_each((part_own + arrived).reshape(far, half // far, width), FAR)
    share = jnp.sum(shares, axis=0)
    sketched_own = lax.all_gather(share, FAR, axis=0, tiled=True)
    sketched_other = with_neighbour(sketched_own)

    gram_part = pl.pallas_call(
        gram_kernel,
        out_shape=jax.ShapeDtypeStruct((width, width), F32),
        compiler_params=pltpu.CompilerParams(vmem_limit_bytes=VMEM_LIMIT),
        name="gram_part",
    )(sketched_own, sketched_other)
    gram_rows = jnp.sum(each_to_each(gram_part.reshape(texels, width // texels, width), TEXEL), axis=0)
    gram = each_to_each(jnp.broadcast_to(gram_rows, (texels, *gram_rows.shape)), TEXEL).reshape(width, width)

    lines = width // texels
    smem, vmem = pl.BlockSpec(memory_space=pltpu.SMEM), pl.BlockSpec(memory_space=pltpu.VMEM)
    basis, keep, send = pl.pallas_call(
        basis_kernel,
        out_shape=(
            jax.ShapeDtypeStruct((capacity, width), F32),
            jax.ShapeDtypeStruct((texels // 2, lines, lights), F32),
            jax.ShapeDtypeStruct((texels // 2, lines, lights), F32),
        ),
        in_specs=[smem, smem] + [vmem] * 5,
        out_specs=(vmem, vmem, vmem),
        scratch_shapes=[pltpu.VMEM((width, width), F32)] * 3 + [pltpu.VMEM((texels, lines, lights), F32)],
        compiler_params=pltpu.CompilerParams(vmem_limit_bytes=VMEM_LIMIT),
        name="basis_and_coeffs",
    )(where, row_counts, gram, sketched_own, sketched_other, tile_own, tile_other)
    mine = keep + lax.ppermute(send, "core", core_pairs())
    coeffs = jnp.sum(each_to_each(mine, ("x", "y")), axis=0)
    return basis, coeffs


def solution(mesh):
    fine = Mesh(np.asarray(mesh.devices).reshape(4, 4, 2, 2, 2, 2, 2), (*TEXEL, *LIGHT))
    placed = (P(TEXEL, None), P(LIGHT, None), P(LIGHT, None), P())
    return jax.shard_map(
        on_device, mesh=fine, in_specs=placed, out_specs=(P(TEXEL, None), P(TEXEL, LIGHT)), check_vma=False
    )
```

time: 282 us -> 228 us (0.81)
  Pallas kernels: 0 us -> 75.1 us
  other arithmetic: 59.1 us -> 0.99 us
  matrix products: 31.1 us -> 0 us
  blocking collectives: 142 us -> 115 us
  waiting for transfers between devices: 26.9 us -> 12.6 us
  starting transfers between devices: 8.33 us -> 16.1 us
  local copies, waits for them, and re-layouts: 12 us -> 7.01 us
    pallas_call x0 -> x4, Pallas kernels: none -> 75.1 us  [the longest x1 65 us: on_device(): pl.pallas_call(basis_kernel, out_shape=(jax.ShapeDtypeStruct((capacity, w...]
    another operation x9 -> x1, other arithmetic: 54.5 us -> 0.08 us  [on_device(): jnp.stack([lax.axis_index(TEXEL), lax.axis_index('z0'), lax.axis_index('c...]
    all_to_all x3 -> x4, blocking collectives: 142 us -> 90.3 us  [each_to_each(): return lax.all_to_all(parts, axes, 0, 0, tiled=True)]
    dot_general x4 -> x0, matrix products: 28.4 us -> none  [the longest x1 23 us: on_device(): lax.dot_general(tex_feat, light_feat, (((1,), (1,)), ((), ())), preferred...]
    all_to_all x2 -> x0, waiting for transfers between devices: 26.9 us -> none  [the longest x1 19.2 us: sum_at_owner(): parts = lax.all_to_all(in_blocks(shard, dim, count), axis, 0, 0, tiled=True)]
    all_gather x0 -> x1, blocking collectives: none -> 24.9 us  [on_device(): sketched_own = lax.all_gather(share, FAR, axis=0, tiled=True)]
    ppermute x0 -> x3, starting transfers between devices: none -> 16.1 us  [the longest x2 14 us: with_neighbour(): lax.ppermute(value, ('core', *LIGHT), light_pairs(lax.axis_size(LIGHT)))]
    ppermute x0 -> x3, waiting for transfers between devices: none -> 12.6 us  [the longest x2 10.5 us: with_neighbour(): lax.ppermute(value, ('core', *LIGHT), light_pairs(lax.axis_size(LIGHT)))]
  transfers between devices with their start and end apart: 2 -> 3, of which waited for: 2 -> 3; matrix products, arithmetic and copies ran while one was open for 1% -> 0% of each run, Pallas kernels for 0% -> 2%
where the time goes in v1:
time: 228 us
  blocking collectives  115 us (50%)
  Pallas kernels  75.1 us (33%)
  starting transfers between devices  16.1 us (7%)
  waiting for transfers between devices  12.6 us (6%)
  local copies, waits for them, and re-layouts  7.01 us (3%)
    all_to_all x4, blocking collectives, each_to_each(): return lax.all_to_all(parts, axes, 0, 0, tiled=True)  90.3 us
    pallas_call x1, Pallas kernels, on_device(): pl.pallas_call(basis_kernel, out_shape=(jax.ShapeDtypeStruct((capacity, w...  65 us
    all_gather x1, blocking collectives, on_device(): sketched_own = lax.all_gather(share, FAR, axis=0, tiled=True)  24.9 us
    ppermute x2, starting transfers between devices, with_neighbour(): lax.ppermute(value, ('core', *LIGHT), light_pairs(lax.axis_size(LIGHT)))  14 us
    ppermute x2, waiting for transfers between devices, with_neighbour(): lax.ppermute(value, ('core', *LIGHT), light_pairs(lax.axis_size(LIGHT)))  10.5 us
    pallas_call x2, Pallas kernels, tile_call(): pl.pallas_call(lambda *refs: tile_kernel(*refs, half=half, rows=rows, blo...  8.87 us
    unnamed x14, local copies, waits for them, and re-layouts  6.99 us
  transfers between devices with their start and end apart: 3, of which 3 were waited for; matrix products, arithmetic and copies ran while one was open for 0% of the time, Pallas kernels for 2%

profile of v1, /device:TPU:1, one launch (start us, length us, event | category | flops | bytes accessed | tf_op | source)
XLA Modules:
  0.0 227.6 jit_solution(2745464304866403022)
XLA Ops:
  0.6 0.1 pad_add_fusion.refs_0_.where_ref
  0.7 0.0 copy-start.2
  0.7 0.7 copy-done.2
  1.4 0.0 copy-start.4
  1.4 1.4 copy-done.4
  2.8 0.0 copy-start.5
  2.8 1.2 copy-done.5
  4.0 0.0 copy-start.6
  4.0 1.1 copy-done.6
  5.1 4.4 %tile_half.3 = (bf16[512,1536]{1,0:T(8,128)(2,1)S(1)}, f32[512,256]{1,0:T(8,128)S(1)}) custom-call(s32[3]{0:T(128)S(1)} %pad_add_fusion.refs_0_.where_ref, s32[32]{0:T(128)S(1)} %copy-done.2, bf16[1024,512]{1,0:T(8,128)(2,1)S(1)} %copy-done.5, bf16[1536,512]{1,0:T(8,128)(2,1)S(1)} %copy-done.4, bf16[1536,256]{1,0:T(8,128)(2,1)S(1)} %copy-done.6), custom_call_target="tpu_custom_call" | custom-call | flops 1207959552 | bytes 4194304 | tf_op jit(solution)/shard_map/tile_half/pallas_call | solution.py:67
  9.6 12.0 %collective-permute-start = (f32[512,256]{1,0:T(8,128)S(1)}, f32[512,256]{1,0:T(8,128)S(1)}, u32[]{:S(2)}, u32[]{:S(2)}) collective-permute-start(f32[512,256]{1,0:T(8,128)S(1)} %get-tuple-element.10), channel_id=1, source_target_pairs={{0,1},{1,0},{2,3},{3,2},{4,5},{5,4},{6,7},{7,6},{8,9},{9,8},{10,11... | collective-permute-start | bytes 1572872 | tf_op jit(solution)/shard_map/ppermute | solution.py:188
  21.5 4.4 %tile_half.2 = (bf16[512,1536]{1,0:T(8,128)(2,1)S(1)}, f32[512,256]{1,0:T(8,128)S(1)}) custom-call(s32[3]{0:T(128)S(1)} %pad_add_fusion.refs_0_.where_ref, s32[32]{0:T(128)S(1)} %copy-done.2, bf16[1024,512]{1,0:T(8,128)(2,1)S(1)} %copy-done.5, bf16[1536,512]{1,0:T(8,128)(2,1)S(1)} %copy-done.4, bf16[1536,256]{1,0:T(8,128)(2,1)S(1)} %copy-done.6), custom_call_target="tpu_custom_call" | custom-call | flops 1207959552 | bytes 4194304 | tf_op jit(solution)/shard_map/tile_half/pallas_call | solution.py:67
  26.0 0.0 copy-start
  26.0 1.2 copy-done
  27.1 0.9 collective-permute-done
  28.1 0.1 add.14
  28.2 37.8 %all_to_all.20 = f32[8,64,256]{2,1,0:T(8,128)S(1)} all-to-all(f32[8,64,256]{2,1,0:T(8,128)S(1)} %bitcast.8), channel_id=1, replica_groups=mesh['x'=4,'y'=4,'core'=2,'z3'=2,'z2'=2,'z1'=2,'z0'=2] {'z3','z2','z1'}, dimensions={0} | all-to-all | bytes 1048576 | tf_op jit(solution)/shard_map/all_to_all | solution.py:192
  66.0 24.9 %all_gather.3.own_ref = f32[512,256]{1,0:T(8,128)S(1)} all-gather(f32[64,256]{1,0:T(8,128)S(1)} %reduce_sum.27), channel_id=1, replica_groups=mesh['x'=4,'y'=4,'core'=2,'z3'=2,'z2'=2,'z1'=2,'z0'=2] {'z3','z2','z1'}, dimensions={0}, use_global_device_ids=true | all-gather | bytes 589824 | tf_op jit(solution)/shard_map/all_gather | solution.py:207
  90.8 0.0 copy-start.3
  90.8 2.0 collective-permute-start.1
  92.9 9.6 %collective-permute-done.1.other_ref = f32[512,256]{1,0:T(8,128)S(1)} collective-permute-done((f32[512,256]{1,0:T(8,128)S(1)}, f32[512,256]{1,0:T(8,128)S(1)}, u32[]{:S(2)}, u32[]{:S(2)}) %collective-permute-start.1) | collective-permute-done | bytes 524320 | tf_op jit(solution)/shard_map/ppermute | solution.py:188
  102.5 1.2 gram_part.1
  103.6 24.0 %all_to_all.21 = f32[32,8,256]{2,1,0:T(8,128)S(1)} all-to-all(f32[32,8,256]{2,1,0:T(8,128)S(1)} %bitcast.7), channel_id=1, replica_groups=mesh['x'=4,'y'=4,'core'=2,'z3'=2,'z2'=2,'z1'=2,'z0'=2] {'x','y','core'}, dimensions={0} | all-to-all | bytes 524288 | tf_op jit(solution)/shard_map/all_to_all | solution.py:192
  127.7 12.5 %all_to_all.22 = f32[32,8,256]{2,1,0:T(8,128)S(1)} all-to-all(f32[32,8,256]{2,1,0:T(8,128)S(1)} %broadcast_in_dim.3), channel_id=1, replica_groups=mesh['x'=4,'y'=4,'core'=2,'z3'=2,'z2'=2,'z1'=2,'z0'=2] {'x','y','core'}, dimensions={0} | all-to-all | bytes 524288 | tf_op jit(solution)/shard_map/all_to_all | solution.py:192
  140.2 0.0 copy-done.3
  140.2 1.4 copy-done.1
  141.6 65.0 %basis_and_coeffs.1 = (f32[1024,256]{1,0:T(8,128)}, f32[16,8,1536]{2,1,0:T(8,128)S(1)}, f32[16,8,1536]{2,1,0:T(8,128)S(1)}) custom-call(s32[3]{0:T(128)S(1)} %pad_add_fusion.refs_0_.where_ref, s32[32]{0:T(128)S(1)} %copy-done.3, f32[256,256]{1,0:T(8,128)S(1)} %bitcast.6, f32[512,256]{1,0:T(8,128)S(1)} %all_gather.3.own_ref, ...), custom_call_target="tpu_custom_call" | custom-call | tf_op jit(solution)/shard_map/basis_and_coeffs/pallas_call | solution.py:221
  206.6 2.1 collective-permute-start.2
  208.7 2.1 collective-permute-done.2
  210.8 0.1 add.15
  210.9 16.1 %all_to_all.23 = f32[16,8,1536]{2,1,0:T(8,128)S(1)} all-to-all(f32[16,8,1536]{2,1,0:T(8,128)S(1)} %add.15), channel_id=1, replica_groups=mesh['x'=4,'y'=4,'core'=2,'z3'=2,'z2'=2,'z1'=2,'z0'=2] {'x','y'}, dimensions={0} | all-to-all | bytes 1572864 | tf_op jit(solution)/shard_map/all_to_all | solution.py:192
  226.9 0.7 reduce_sum.29
  (4 shorter events, 0.1 us)
Async XLA Ops:
  0.7 0.7 copy-start.2
  1.4 1.4 copy-start.4
  2.8 1.2 copy-start.5
  4.0 1.1 copy-start.6
  9.6 18.5 %collective-permute-start = (f32[512,256]{1,0:T(8,128)S(1)}, f32[512,256]{1,0:T(8,128)S(1)}, u32[]{:S(2)}, u32[]{:S(2)}) collective-permute-start(f32[512,256]{1,0:T(8,128)S(1)} %get-tuple-element.10), channel_id=1, source_target_pairs={{0,1},{1,0},{2,3},{3,2},{4,5},{5,4},{6,7},{7,6},{8,9},{9,8},{10,11... | collective-permute-start | bytes 1572872 | tf_op jit(solution)/shard_map/ppermute | solution.py:188
  26.0 1.2 copy-start
  90.8 49.3 %copy-start.3 = (s32[32]{0:T(128)S(1)}, s32[32]{0:T(128)}, u32[]{:S(2)}) copy-start(s32[32]{0:T(128)} %counts_ref.1) | copy-start | bytes 388
  90.8 11.6 %collective-permute-start.1 = (f32[512,256]{1,0:T(8,128)S(1)}, f32[512,256]{1,0:T(8,128)S(1)}, u32[]{:S(2)}, u32[]{:S(2)}) collective-permute-start(f32[512,256]{1,0:T(8,128)S(1)} %all_gather.3.own_ref), channel_id=1, source_target_pairs={{0,1},{1,0},{2,3},{3,2},{4,5},{5,4},{6,7},{7,6},{8,9},{9,8},{10,11... | collective-permute-start | bytes 1572872 | tf_op jit(solution)/shard_map/ppermute | solution.py:188
  140.2 1.4 copy-start.1
  206.6 4.2 %collective-permute-start.2 = (f32[16,8,1536]{2,1,0:T(8,128)S(1)}, f32[16,8,1536]{2,1,0:T(8,128)S(1)}, u32[]{:S(2)}, u32[]{:S(2)}) collective-permute-start(f32[16,8,1536]{2,1,0:T(8,128)S(1)} %get-tuple-element.15), channel_id=1, source_target_pairs={{0,16},{16,0},{1,17},{17,1},{2,18},{18,2},{3,19},{19,3},{4,20},{20... | collective-permute-start | bytes 2359304 | tf_op jit(solution)/shard_map/ppermute | solution.py:234

commit v2 on v1

--- a/solution.py
+++ b/solution.py
@@ -47,16 +47,26 @@
     )
 
 
-def tile_kernel(where_ref, counts_ref, tex_ref, light_ref, sketch_ref, tile_ref, part_ref, *, half, rows, blocks):
-    first = (half + where_ref[1]) % 2 * (blocks * rows) + pl.program_id(0) * rows
+def tile_kernel(
+    where_ref, counts_ref, tex_ref, light_ref, sketch_ref, tile_ref, part_ref, *, half, rows, blocks, share
+):
+    parity, core, far = where_ref[1], where_ref[2], where_ref[3]
+    step = pl.program_id(0)
+    first = (half + parity) % 2 * (blocks * rows) + step * rows
     tile = sine(dot(tex_ref[...], light_ref[...], (1, 1))).astype(BF16)
     tile_ref[...] = tile
     part = dot(tile, sketch_ref[...], (1, 0))
     row = first + lax.broadcasted_iota(jnp.int32, part.shape, 0)
-    part_ref[...] = jnp.where(row < counts_ref[where_ref[0]], part, 0.0)
-
-
-def tile_call(half, where, counts, tex, light, sketch, rows=128):
+    part = jnp.where(row < counts_ref[where_ref[0]], part, 0.0)
+    reference = (far + core * half) % 2
+    shares = blocks * rows // share
+    for i in range(rows // share):
+        owner = step * (rows // share) + i
+        place = (owner + reference) % 2 * (shares // 2) + owner // 2
+        part_ref[pl.ds(pl.multiple_of(place * share, share), share), :] = part[i * share : (i + 1) * share, :]
+
+
+def tile_call(half, where, counts, tex, light, sketch, share, rows=128):
     capacity, features = tex.shape
     lights, width = sketch.shape
     blocks = capacity // 2 // rows
@@ -65,7 +75,7 @@
         return ((half + where_ref[1]) % 2 * blocks + i, 0)
 
     return pl.pallas_call(
-        lambda *refs: tile_kernel(*refs, half=half, rows=rows, blocks=blocks),
+        lambda *refs: tile_kernel(*refs, half=half, rows=rows, blocks=blocks, share=share),
         out_shape=(
             jax.ShapeDtypeStruct((capacity // 2, lights), BF16),
             jax.ShapeDtypeStruct((capacity // 2, width), F32),
@@ -80,7 +90,7 @@
             ],
             out_specs=(
                 pl.BlockSpec((rows, lights), lambda i, *_: (i, 0)),
-                pl.BlockSpec((rows, width), lambda i, *_: (i, 0)),
+                pl.BlockSpec((capacity // 2, width), lambda i, *_: (0, 0)),
             ),
         ),
         compiler_params=pltpu.CompilerParams(vmem_limit_bytes=VMEM_LIMIT),
@@ -91,10 +101,10 @@
     )(where, counts, tex, light, sketch)
 
 
-def gram_kernel(own_ref, other_ref, gram_ref):
-    gram_ref[...] = dot(own_ref[...], own_ref[...], (0, 0), HIGHEST) + dot(
-        other_ref[...], other_ref[...], (0, 0), HIGHEST
-    )
+def gram_kernel(shares_ref, share_ref, gram_ref):
+    share = jnp.sum(shares_ref[...], axis=0)
+    share_ref[...] = share
+    gram_ref[...] = dot(share, share, (0, 0), HIGHEST)
 
 
 def invert_factor(gram, y_ref, a_ref, w_ref):
@@ -146,26 +156,40 @@
         lax.fori_loop(0, size, eliminate, 0)
 
 
+def inverse_kernel(counts_ref, gram_ref, inverse_ref, a_ref, w_ref):
+    total = F32(0)
+    for i in range(counts_ref.shape[0]):
+        total = total + counts_ref[i].astype(F32)
+    invert_factor(gram_ref[...] / total, inverse_ref, a_ref, w_ref)
+
+
 def basis_kernel(
-    where_ref, counts_ref, gram_ref, own_ref, other_ref, tile_own_ref, tile_other_ref,
-    basis_ref, keep_ref, send_ref, y_ref, a_ref, w_ref, coeff_ref,
+    where_ref, counts_ref, inverse_ref, own_ref, other_ref, tile_own_ref, tile_other_ref,
+    basis_ref, keep_ref, send_ref, coeff_ref,
 ):
     total = F32(0)
     for i in range(counts_ref.shape[0]):
         total = total + counts_ref[i].astype(F32)
-    gram = gram_ref[...] / total
-    invert_factor(gram, y_ref, a_ref, w_ref)
-    inverse = y_ref[...]
-    half = own_ref.shape[0]
-    own = dot(own_ref[...], inverse, (1, 1), HIGHEST)
-    other = dot(other_ref[...], inverse, (1, 1), HIGHEST)
-    parity = where_ref[1]
-    basis_ref[pl.ds(pl.multiple_of(parity * half, half), half), :] = own
-    basis_ref[pl.ds(pl.multiple_of((1 - parity) * half, half), half), :] = other
-    coeffs = dot(own.astype(BF16), tile_own_ref[...], (0, 0)) + dot(other.astype(BF16), tile_other_ref[...], (0, 0))
+    inverse = inverse_ref[...]
+    shares, share = own_ref.shape[0], own_ref.shape[1]
+    half = shares * share
+    parity, core, far = where_ref[1], where_ref[2], where_ref[3]
+    near = (far + core * (2 * parity - 1) + shares) % shares
+    coeffs = None
+    for source_ref, tile_ref, side, place in (
+        (own_ref, tile_own_ref, parity, far), (other_ref, tile_other_ref, 1 - parity, near)
+    ):
+        basis = dot(source_ref[...].reshape(half, source_ref.shape[2]), inverse, (1, 1), HIGHEST)
+        for i in range(shares):
+            apart = (i & 1) << 2 | i & 2 | i >> 2
+            owner = ((((place + shares - core) % shares) ^ apart) + core) % shares
+            at = pl.multiple_of(side * half + owner * share, share)
+            basis_ref[pl.ds(at, share), :] = basis[i * share : (i + 1) * share, :]
+        ordered = basis_ref[pl.ds(pl.multiple_of(side * half, half), half), :].astype(BF16)
+        product = dot(ordered, tile_ref[...], (0, 0))
+        coeffs = product if coeffs is None else coeffs + product
     scale = 1.0 / jnp.sqrt(jnp.full((1, 1), total, F32))
     coeff_ref[...] = (coeffs * scale).reshape(coeff_ref.shape)
-    core = where_ref[2]
     for i in range(keep_ref.shape[0]):
         keep_ref[i] = coeff_ref[2 * i + core]
         send_ref[i] = coeff_ref[2 * i + 1 - core]
@@ -175,21 +199,29 @@
     return [(i, i ^ 1) for i in range(2)]
 
 
-def light_pairs(count):
+def light_pairs(count, reach):
     pairs = []
     for core in range(2):
+        shift = core * min(reach, 2)
         for z in range(count):
-            other = z ^ 1 if core == 0 else ((((z - 1) % count) ^ 1) + 1) % count
-            pairs.append((core * count + z, core * count + other))
+            pairs.append((core * count + z, core * count + ((((z - shift) % count) ^ reach) + shift) % count))
     return pairs
 
 
-def with_neighbour(value):
-    return lax.ppermute(value, ("core", *LIGHT), light_pairs(lax.axis_size(LIGHT)))
+def across(value, reach):
+    return lax.ppermute(value, ("core", *LIGHT), light_pairs(lax.axis_size(LIGHT), reach))
 
 
 def each_to_each(parts, axes):
     return lax.all_to_all(parts, axes, 0, 0, tiled=True)
+
+
+def to_each(value, axes):
+    return each_to_each(jnp.broadcast_to(value, (lax.axis_size(axes), *value.shape)), axes)
+
+
+def after(value, *others):
+    return lax.optimization_barrier((value, *others))[0]
 
 
 def on_device(tex_feat, light_feat, sketch, row_counts):
@@ -197,27 +229,50 @@
     lights = light_feat.shape[0]
     half = capacity // 2
     texels, far = lax.axis_size(TEXEL), lax.axis_size(FAR)
-    where = jnp.stack([lax.axis_index(TEXEL), lax.axis_index("z0"), lax.axis_index("core")]).astype(jnp.int32)
-
-    tile_other, part_other = tile_call(1, where, row_counts, tex_feat, light_feat, sketch)
-    arrived = with_neighbour(part_other)
-    tile_own, part_own = tile_call(0, where, row_counts, tex_feat, light_feat, sketch)
-    shares = each_to_each((part_own + arrived).reshape(far, half // far, width), FAR)
-    share = jnp.sum(shares, axis=0)
-    sketched_own = lax.all_gather(share, FAR, axis=0, tiled=True)
-    sketched_other = with_neighbour(sketched_own)
-
-    gram_part = pl.pallas_call(
+    share_rows = half // far
+    places = [lax.axis_index(axes) for axes in (TEXEL, "z0", "core", FAR)]
+    where = jnp.stack(places).astype(jnp.int32)
+
+    inputs = (where, row_counts, tex_feat, light_feat, sketch, share_rows)
+    tile_other, part_other = tile_call(1, *inputs)
+    arrived = across(part_other, 1)
+    tile_own, part_own = tile_call(0, *inputs)
+    quarter = part_own[: half // 2] + arrived[: half // 2]
+    quarter = quarter + across(part_own[half // 2 :] + arrived[half // 2 :], 2)
+    shares = each_to_each(quarter.reshape(far // 2, share_rows, width), ("z3", "z2"))
+
+    share, gram_part = pl.pallas_call(
         gram_kernel,
+        out_shape=(jax.ShapeDtypeStruct((share_rows, width), F32), jax.ShapeDtypeStruct((width, width), F32)),
+        compiler_params=pltpu.CompilerParams(vmem_limit_bytes=VMEM_LIMIT),
+        name="gram_part",
+    )(shares)
+
+    held = share[None]
+    held = jnp.concatenate([held, across(held, 8)])
+    gram_rows = jnp.sum(each_to_each(gram_part.reshape(texels, width // texels, width), TEXEL), axis=0)
+    held, gram_rows = lax.optimization_barrier((held, gram_rows))
+    held = jnp.concatenate([held, across(held, 4)])
+    gram_rows = jnp.sum(to_each(gram_rows, LIGHT), axis=0)
+    held, gram_rows = lax.optimization_barrier((held, gram_rows))
+    sketched_own = jnp.concatenate([held, across(held, 2)])
+    gram = to_each(gram_rows, TEXEL).reshape(width, width)
+    sketched_own, gram = lax.optimization_barrier((sketched_own, gram))
+    sketched_other = across(sketched_own, 1)
+
+    smem, vmem = pl.BlockSpec(memory_space=pltpu.SMEM), pl.BlockSpec(memory_space=pltpu.VMEM)
+    inverse = pl.pallas_call(
+        inverse_kernel,
         out_shape=jax.ShapeDtypeStruct((width, width), F32),
-        compiler_params=pltpu.CompilerParams(vmem_limit_bytes=VMEM_LIMIT),
-        name="gram_part",
-    )(sketched_own, sketched_other)
-    gram_rows = jnp.sum(each_to_each(gram_part.reshape(texels, width // texels, width), TEXEL), axis=0)
-    gram = each_to_each(jnp.broadcast_to(gram_rows, (texels, *gram_rows.shape)), TEXEL).reshape(width, width)
+        in_specs=[smem, vmem],
+        out_specs=vmem,
+        scratch_shapes=[pltpu.VMEM((width, width), F32)] * 2,
+        compiler_params=pltpu.CompilerParams(vmem_limit_bytes=VMEM_LIMIT),
+        cost_estimate=pl.CostEstimate(flops=10**10, bytes_accessed=2**20, transcendentals=0),
+        name="inverse_factor",
+    )(row_counts, gram)
 
     lines = width // texels
-    smem, vmem = pl.BlockSpec(memory_space=pltpu.SMEM), pl.BlockSpec(memory_space=pltpu.VMEM)
     basis, keep, send = pl.pallas_call(
         basis_kernel,
         out_shape=(
@@ -227,10 +282,10 @@
         ),
         in_specs=[smem, smem] + [vmem] * 5,
         out_specs=(vmem, vmem, vmem),
-        scratch_shapes=[pltpu.VMEM((width, width), F32)] * 3 + [pltpu.VMEM((texels, lines, lights), F32)],
+        scratch_shapes=[pltpu.VMEM((texels, lines, lights), F32)],
         compiler_params=pltpu.CompilerParams(vmem_limit_bytes=VMEM_LIMIT),
         name="basis_and_coeffs",
-    )(where, row_counts, gram, sketched_own, sketched_other, tile_own, tile_other)
+    )(where, row_counts, inverse, sketched_own, sketched_other, tile_own, tile_other)
     mine = keep + lax.ppermute(send, "core", core_pairs())
     coeffs = jnp.sum(each_to_each(mine, ("x", "y")), axis=0)
     return basis, coeffs

time: 228 us -> 232 us (1.018)
  blocking collectives: 115 us -> 43.6 us
  starting transfers between devices: 16.1 us -> 63.9 us
  waiting for transfers between devices: 12.6 us -> 37.9 us
    pallas_call x1 -> x2, Pallas kernels: 1.18 us -> 64.4 us  [the longest x1 63.3 us: on_device(): pl.pallas_call(inverse_kernel, out_shape=jax.ShapeDtypeStruct((width, wid...]
    pallas_call x1, Pallas kernels: 65 us -> 3.77 us  [on_device(): pl.pallas_call(basis_kernel, out_shape=(jax.ShapeDtypeStruct((capacity, w...]
    all_to_all x4 -> x2, blocking collectives: 90.3 us -> 43.6 us  [each_to_each(): return lax.all_to_all(parts, axes, 0, 0, tiled=True)]
    all_gather x1 -> x0, blocking collectives: 24.9 us -> none  [on_device(): sketched_own = lax.all_gather(share, FAR, axis=0, tiled=True)]
    ppermute x2 -> x6, starting transfers between devices: 14 us -> 37.7 us  [across(): lax.ppermute(value, ('core', *LIGHT), light_pairs(lax.axis_size(LIGHT), r...]
    all_to_all x0 -> x3, starting transfers between devices: none -> 23.3 us  [each_to_each(): return lax.all_to_all(parts, axes, 0, 0, tiled=True)]
    ppermute x2 -> x6, waiting for transfers between devices: 10.5 us -> 27.1 us  [across(): lax.ppermute(value, ('core', *LIGHT), light_pairs(lax.axis_size(LIGHT), r...]
    all_to_all x0 -> x3, waiting for transfers between devices: none -> 8.93 us  [each_to_each(): return lax.all_to_all(parts, axes, 0, 0, tiled=True)]
  transfers between devices with their start and end apart: 3 -> 10, of which waited for: 3 -> 6; matrix products, arithmetic and copies ran while one was open for 0% -> 0% of each run, Pallas kernels for 2% -> 29%
where the time goes in v2:
time: 232 us; the launch traced here: 231 us
  Pallas kernels  77.1 us (33%)
  starting transfers between devices  63.9 us (28%)
  blocking collectives  43.6 us (19%)
  waiting for transfers between devices  37.9 us (16%)
  local copies, waits for them, and re-layouts  6.97 us (3%)
    pallas_call x1, Pallas kernels, on_device(): pl.pallas_call(inverse_kernel, out_shape=jax.ShapeDtypeStruct((width, wid...  63.3 us
    all_to_all x2, blocking collectives, each_to_each(): return lax.all_to_all(parts, axes, 0, 0, tiled=True)  43.6 us
    ppermute x6, starting transfers between devices, across(): lax.ppermute(value, ('core', *LIGHT), light_pairs(lax.axis_size(LIGHT), r...  37.7 us
    ppermute x6, waiting for transfers between devices, across(): lax.ppermute(value, ('core', *LIGHT), light_pairs(lax.axis_size(LIGHT), r...  27.1 us
    all_to_all x3, starting transfers between devices, each_to_each(): return lax.all_to_all(parts, axes, 0, 0, tiled=True)  23.3 us
    all_to_all x3, waiting for transfers between devices, each_to_each(): return lax.all_to_all(parts, axes, 0, 0, tiled=True)  8.93 us
    pallas_call x2, Pallas kernels, tile_call(): pl.pallas_call(lambda *refs: tile_kernel(*refs, half=half, rows=rows, blo...  8.87 us
    unnamed x14, local copies, waits for them, and re-layouts  5.59 us
  transfers between devices with their start and end apart: 10, of which 6 were waited for; matrix products, arithmetic and copies ran while one was open for 0% of the time, Pallas kernels for 29%

profile of v2, /device:TPU:1, one launch (start us, length us, event | category | flops | bytes accessed | tf_op | source)
XLA Modules:
  0.0 231.4 jit_solution(5064409915241994228)
XLA Ops:
  0.7 0.7 copy-done.2
  1.4 1.4 copy-done.4
  2.8 1.2 copy-done.5
  4.0 1.1 copy-done.6
  5.1 4.4 %tile_half.3 = (bf16[512,1536]{1,0:T(8,128)(2,1)S(1)}, f32[512,256]{1,0:T(8,128)S(1)}) custom-call(s32[4]{0:T(128)S(1)} %pad_add_fusion.refs_0_.where_ref, s32[32]{0:T(128)S(1)} %copy-done.2, bf16[1024,512]{1,0:T(8,128)(2,1)S(1)} %copy-done.5, bf16[1536,512]{1,0:T(8,128)(2,1)S(1)} %copy-done.4, bf16[1536,256]{1,0:T(8,128)(2,1)S(1)} %copy-done.6), custom_call_target="tpu_custom_call" | custom-call | flops 1207959552 | bytes 4194304 | tf_op jit(solution)/shard_map/tile_half/pallas_call | solution.py:77
  9.6 12.0 %collective-permute-start = (f32[512,256]{1,0:T(8,128)S(1)}, f32[512,256]{1,0:T(8,128)S(1)}, u32[]{:S(2)}, u32[]{:S(2)}) collective-permute-start(f32[512,256]{1,0:T(8,128)S(1)} %get-tuple-element.18), channel_id=1, source_target_pairs={{0,1},{1,0},{2,3},{3,2},{4,5},{5,4},{6,7},{7,6},{8,9},{9,8},{10,11... | collective-permute-start | bytes 1572872 | tf_op jit(solution)/shard_map/ppermute | solution.py:212
  21.6 4.4 %tile_half.2 = (bf16[512,1536]{1,0:T(8,128)(2,1)S(1)}, f32[512,256]{1,0:T(8,128)S(1)}) custom-call(s32[4]{0:T(128)S(1)} %pad_add_fusion.refs_0_.where_ref, s32[32]{0:T(128)S(1)} %copy-done.2, bf16[1024,512]{1,0:T(8,128)(2,1)S(1)} %copy-done.5, bf16[1536,512]{1,0:T(8,128)(2,1)S(1)} %copy-done.4, bf16[1536,256]{1,0:T(8,128)(2,1)S(1)} %copy-done.6), custom_call_target="tpu_custom_call" | custom-call | flops 1207959552 | bytes 4194304 | tf_op jit(solution)/shard_map/tile_half/pallas_call | solution.py:77
  26.0 1.2 copy-done
  27.2 0.9 collective-permute-done
  28.1 4.1 %collective-permute-start.1 = (f32[256,256]{1,0:T(8,128)S(1)}, f32[256,256]{1,0:T(8,128)S(1)}, u32[]{:S(2)}, u32[]{:S(2)}) collective-permute-start(f32[256,256]{1,0:T(8,128)S(1)} %slice_add_fusion), channel_id=1, source_target_pairs={{0,2},{1,3},{2,0},{3,1},{4,6},{5,7},{6,4},{7,5},{8,10},{9,11},{10,... | collective-permute-start | bytes 786440 | tf_op jit(solution)/shard_map/ppermute | solution.py:212
  32.2 6.8 %collective-permute-done.1 = f32[256,256]{1,0:T(8,128)S(1)} collective-permute-done((f32[256,256]{1,0:T(8,128)S(1)}, f32[256,256]{1,0:T(8,128)S(1)}, u32[]{:S(2)}, u32[]{:S(2)}) %collective-permute-start.1) | collective-permute-done | bytes 262176 | tf_op jit(solution)/shard_map/ppermute | solution.py:212
  39.1 27.4 %all_to_all.25.shares_ref = f32[4,64,256]{2,1,0:T(8,128)S(1)} all-to-all(f32[4,64,256]{2,1,0:T(8,128)S(1)} %bitcast.11), channel_id=1, replica_groups=mesh['x'=4,'y'=4,'core'=2,'z3'=2,'z2'=2,'z1'=2,'z0'=2] {'z3','z2'}, dimensions={0} | all-to-all | bytes 524288 | tf_op jit(solution)/shard_map/all_to_all | solution.py:216
  66.5 1.1 gram_part.1
  67.6 8.1 %all-to-all-start.1 = ((f32[32,8,256]{2,1,0:T(8,128)}), f32[32,8,256]{2,1,0:T(8,128)S(1)}, u32[]{:S(2)}, u32[]{:S(2)}) async-start(f32[32,8,256]{2,1,0:T(8,128)} %bitcast.6), calls=%async_computation.1 | async-start | bytes 524288 | tf_op jit(solution)/shard_map/all_to_all | solution.py:216
  75.7 3.0 %collective-permute-start.2 = (f32[1,64,256]{2,1,0:T(8,128)S(1)}, f32[1,64,256]{2,1,0:T(8,128)S(1)}, u32[]{:S(2)}, u32[]{:S(2)}) collective-permute-start(f32[1,64,256]{2,1,0:T(8,128)S(1)} %bitcast.9), channel_id=1, source_target_pairs={{0,8},{1,9},{2,10},{3,11},{4,12},{5,13},{6,14},{7,15},{8,0},{9,1},... | collective-permute-start | bytes 196616 | tf_op jit(solution)/shard_map/ppermute | solution.py:212
  78.7 12.8 %collective-permute-done.2 = f32[1,64,256]{2,1,0:T(8,128)S(1)} collective-permute-done((f32[1,64,256]{2,1,0:T(8,128)S(1)}, f32[1,64,256]{2,1,0:T(8,128)S(1)}, u32[]{:S(2)}, u32[]{:S(2)}) %collective-permute-start.2) | collective-permute-done | bytes 65568 | tf_op jit(solution)/shard_map/ppermute | solution.py:212
  91.5 0.7 broadcast_in_dim.10
  92.2 5.6 %all-to-all-start.2 = ((f32[16,8,256]{2,1,0:T(8,128)}), f32[16,8,256]{2,1,0:T(8,128)S(1)}, u32[]{:S(2)}, u32[]{:S(2)}) async-start(f32[16,8,256]{2,1,0:T(8,128)} %broadcast_in_dim.10), calls=%async_computation.2 | async-start | bytes 262144 | tf_op jit(solution)/shard_map/all_to_all | solution.py:216
  97.8 7.2 %collective-permute-start.3 = (f32[2,64,256]{2,1,0:T(8,128)S(1)}, f32[2,64,256]{2,1,0:T(8,128)S(1)}, u32[]{:S(2)}, u32[]{:S(2)}) collective-permute-start(f32[2,64,256]{2,1,0:T(8,128)S(1)} %pad_maximum_fusion.2), channel_id=1, source_target_pairs={{0,4},{1,5},{2,6},{3,7},{4,0},{5,1},{6,2},{7,3},{8,12},{9,13},{10,... | collective-permute-start | bytes 393224 | tf_op jit(solution)/shard_map/ppermute | solution.py:212
  105.0 6.6 %collective-permute-done.3 = f32[2,64,256]{2,1,0:T(8,128)S(1)} collective-permute-done((f32[2,64,256]{2,1,0:T(8,128)S(1)}, f32[2,64,256]{2,1,0:T(8,128)S(1)}, u32[]{:S(2)}, u32[]{:S(2)}) %collective-permute-start.3) | collective-permute-done | bytes 131104 | tf_op jit(solution)/shard_map/ppermute | solution.py:212
  111.6 9.3 %collective-permute-start.4 = (f32[4,64,256]{2,1,0:T(8,128)S(1)}, f32[4,64,256]{2,1,0:T(8,128)S(1)}, u32[]{:S(2)}, u32[]{:S(2)}) collective-permute-start(f32[4,64,256]{2,1,0:T(8,128)S(1)} %pad_maximum_fusion.1), channel_id=1, source_target_pairs={{0,2},{1,3},{2,0},{3,1},{4,6},{5,7},{6,4},{7,5},{8,10},{9,11},{10,... | collective-permute-start | bytes 786440 | tf_op jit(solution)/shard_map/ppermute | solution.py:212
  121.0 0.7 broadcast_in_dim.11
  121.7 9.6 %all-to-all-start.3 = ((f32[32,8,256]{2,1,0:T(8,128)}), f32[32,8,256]{2,1,0:T(8,128)S(1)}, u32[]{:S(2)}, u32[]{:S(2)}) async-start(f32[32,8,256]{2,1,0:T(8,128)} %broadcast_in_dim.11), calls=%async_computation.3 | async-start | bytes 524288 | tf_op jit(solution)/shard_map/all_to_all | solution.py:216
  131.4 8.9 %all-to-all-done.3 = f32[32,8,256]{2,1,0:T(8,128)S(1)} async-done(((f32[32,8,256]{2,1,0:T(8,128)}), f32[32,8,256]{2,1,0:T(8,128)S(1)}, u32[]{:S(2)}, u32[]{:S(2)}) %all-to-all-start.3) | async-done | bytes 262176 | tf_op jit(solution)/shard_map/all_to_all | solution.py:216
  140.3 2.2 collective-permute-start.5
  142.5 63.3 %inverse_factor.1.inverse_ref = f32[256,256]{1,0:T(8,128)S(1)} custom-call(s32[32]{0:T(128)S(1)} %copy-done.3, f32[256,256]{1,0:T(8,128)S(1)} %bitcast.8), custom_call_target="tpu_custom_call" | custom-call | flops 10000000000 | bytes 1048576 | tf_op jit(solution)/shard_map/inverse_factor/pallas_call | solution.py:264
  205.8 3.8 %basis_and_coeffs.1 = (f32[1024,256]{1,0:T(8,128)}, f32[16,8,1536]{2,1,0:T(8,128)S(1)}, f32[16,8,1536]{2,1,0:T(8,128)S(1)}) custom-call(s32[4]{0:T(128)S(1)} %pad_add_fusion.refs_0_.where_ref, s32[32]{0:T(128)S(1)} %copy-done.3, f32[256,256]{1,0:T(8,128)S(1)} %inverse_factor.1.inverse_ref, f32[8,64,256]{2,1,0:T(8,128)S(1)} %pad_maximum_fusion.own_ref, ...), custom_call_target="tpu_custom_call" | custom-call | tf_op jit(solution)/shard_map/basis_and_coeffs/pallas_call | solution.py:276
  209.6 2.8 %collective-permute-start.6 = (f32[16,8,1536]{2,1,0:T(8,128)S(1)}, f32[16,8,1536]{2,1,0:T(8,128)S(1)}, u32[]{:S(2)}, u32[]{:S(2)}) collective-permute-start(f32[16,8,1536]{2,1,0:T(8,128)S(1)} %get-tuple-element.31), channel_id=1, source_target_pairs={{0,16},{16,0},{1,17},{17,1},{2,18},{18,2},{3,19},{19,3},{4,20},{20... | collective-permute-start | bytes 2359304 | tf_op jit(solution)/shard_map/ppermute | solution.py:289
  212.5 1.9 collective-permute-done.6
  214.3 0.1 add.31
  214.5 16.2 %all_to_all.26 = f32[16,8,1536]{2,1,0:T(8,128)S(1)} all-to-all(f32[16,8,1536]{2,1,0:T(8,128)S(1)} %add.31), channel_id=1, replica_groups=mesh['x'=4,'y'=4,'core'=2,'z3'=2,'z2'=2,'z1'=2,'z0'=2] {'x','y'}, dimensions={0} | all-to-all | bytes 1572864 | tf_op jit(solution)/shard_map/all_to_all | solution.py:216
  230.7 0.7 reduce_sum.29
  (21 shorter events, 0.3 us)
Async XLA Ops:
  0.7 0.7 copy-start.2
  1.4 1.4 copy-start.4
  2.8 1.2 copy-start.5
  4.0 1.1 copy-start.6
  9.6 18.5 %collective-permute-start = (f32[512,256]{1,0:T(8,128)S(1)}, f32[512,256]{1,0:T(8,128)S(1)}, u32[]{:S(2)}, u32[]{:S(2)}) collective-permute-start(f32[512,256]{1,0:T(8,128)S(1)} %get-tuple-element.18), channel_id=1, source_target_pairs={{0,1},{1,0},{2,3},{3,2},{4,5},{5,4},{6,7},{7,6},{8,9},{9,8},{10,11... | collective-permute-start | bytes 1572872 | tf_op jit(solution)/shard_map/ppermute | solution.py:212
  26.0 1.2 copy-start
  28.1 10.9 %collective-permute-start.1 = (f32[256,256]{1,0:T(8,128)S(1)}, f32[256,256]{1,0:T(8,128)S(1)}, u32[]{:S(2)}, u32[]{:S(2)}) collective-permute-start(f32[256,256]{1,0:T(8,128)S(1)} %slice_add_fusion), channel_id=1, source_target_pairs={{0,2},{1,3},{2,0},{3,1},{4,6},{5,7},{6,4},{7,5},{8,10},{9,11},{10,... | collective-permute-start | bytes 786440 | tf_op jit(solution)/shard_map/ppermute | solution.py:212
  67.6 23.8 %all-to-all-start.1 = ((f32[32,8,256]{2,1,0:T(8,128)}), f32[32,8,256]{2,1,0:T(8,128)S(1)}, u32[]{:S(2)}, u32[]{:S(2)}) async-start(f32[32,8,256]{2,1,0:T(8,128)} %bitcast.6), calls=%async_computation.1 | async-start | bytes 524288 | tf_op jit(solution)/shard_map/all_to_all | solution.py:216
  75.7 15.7 %collective-permute-start.2 = (f32[1,64,256]{2,1,0:T(8,128)S(1)}, f32[1,64,256]{2,1,0:T(8,128)S(1)}, u32[]{:S(2)}, u32[]{:S(2)}) collective-permute-start(f32[1,64,256]{2,1,0:T(8,128)S(1)} %bitcast.9), channel_id=1, source_target_pairs={{0,8},{1,9},{2,10},{3,11},{4,12},{5,13},{6,14},{7,15},{8,0},{9,1},... | collective-permute-start | bytes 196616 | tf_op jit(solution)/shard_map/ppermute | solution.py:212
  91.5 51.0 %copy-start.3 = (s32[32]{0:T(128)S(1)}, s32[32]{0:T(128)}, u32[]{:S(2)}) copy-start(s32[32]{0:T(128)} %counts_ref.3) | copy-start | bytes 388
  92.2 19.4 %all-to-all-start.2 = ((f32[16,8,256]{2,1,0:T(8,128)}), f32[16,8,256]{2,1,0:T(8,128)S(1)}, u32[]{:S(2)}, u32[]{:S(2)}) async-start(f32[16,8,256]{2,1,0:T(8,128)} %broadcast_in_dim.10), calls=%async_computation.2 | async-start | bytes 262144 | tf_op jit(solution)/shard_map/all_to_all | solution.py:216
  97.8 13.8 %collective-permute-start.3 = (f32[2,64,256]{2,1,0:T(8,128)S(1)}, f32[2,64,256]{2,1,0:T(8,128)S(1)}, u32[]{:S(2)}, u32[]{:S(2)}) collective-permute-start(f32[2,64,256]{2,1,0:T(8,128)S(1)} %pad_maximum_fusion.2), channel_id=1, source_target_pairs={{0,4},{1,5},{2,6},{3,7},{4,0},{5,1},{6,2},{7,3},{8,12},{9,13},{10,... | collective-permute-start | bytes 393224 | tf_op jit(solution)/shard_map/ppermute | solution.py:212
  111.6 19.7 %collective-permute-start.4 = (f32[4,64,256]{2,1,0:T(8,128)S(1)}, f32[4,64,256]{2,1,0:T(8,128)S(1)}, u32[]{:S(2)}, u32[]{:S(2)}) collective-permute-start(f32[4,64,256]{2,1,0:T(8,128)S(1)} %pad_maximum_fusion.1), channel_id=1, source_target_pairs={{0,2},{1,3},{2,0},{3,1},{4,6},{5,7},{6,4},{7,5},{8,10},{9,11},{10,... | collective-permute-start | bytes 786440 | tf_op jit(solution)/shard_map/ppermute | solution.py:212
  121.7 18.6 %all-to-all-start.3 = ((f32[32,8,256]{2,1,0:T(8,128)}), f32[32,8,256]{2,1,0:T(8,128)S(1)}, u32[]{:S(2)}, u32[]{:S(2)}) async-start(f32[32,8,256]{2,1,0:T(8,128)} %broadcast_in_dim.11), calls=%async_computation.3 | async-start | bytes 524288 | tf_op jit(solution)/shard_map/all_to_all | solution.py:216
  140.3 65.5 %copy-start.1 = (bf16[512,1536]{1,0:T(8,128)(2,1)S(1)}, bf16[512,1536]{1,0:T(8,128)(2,1)}, u32[]{:S(2)}) copy-start(bf16[512,1536]{1,0:T(8,128)(2,1)} %copy-done) | copy-start | bytes 4718596
  140.3 65.5 %collective-permute-start.5 = (f32[8,64,256]{2,1,0:T(8,128)S(1)}, f32[8,64,256]{2,1,0:T(8,128)S(1)}, u32[]{:S(2)}, u32[]{:S(2)}) collective-permute-start(f32[8,64,256]{2,1,0:T(8,128)S(1)} %pad_maximum_fusion.own_ref), channel_id=1, source_target_pairs={{0,1},{1,0},{2,3},{3,2},{4,5},{5,4},{6,7},{7,6},{8,9},{9,8},{10,11... | collective-permute-start | bytes 1572872 | tf_op jit(solution)/shard_map/ppermute | solution.py:212
  209.6 4.7 %collective-permute-start.6 = (f32[16,8,1536]{2,1,0:T(8,128)S(1)}, f32[16,8,1536]{2,1,0:T(8,128)S(1)}, u32[]{:S(2)}, u32[]{:S(2)}) collective-permute-start(f32[16,8,1536]{2,1,0:T(8,128)S(1)} %get-tuple-element.31), channel_id=1, source_target_pairs={{0,16},{16,0},{1,17},{17,1},{2,18},{18,2},{3,19},{19,3},{4,20},{20... | collective-permute-start | bytes 2359304 | tf_op jit(solution)/shard_map/ppermute | solution.py:289

commit v3 on v1

v3 whole, which is shorter than its diff:
```python
import math

import jax
import jax.numpy as jnp
import numpy as np
from jax import lax
from jax.experimental import pallas as pl
from jax.experimental.pallas import tpu as pltpu
from jax.sharding import Mesh, PartitionSpec as P

F32 = jnp.float32
BF16 = jnp.bfloat16
CHIP = ("x", "y")
TEXEL = CHIP + ("core",)
LIGHT = ("z3", "z2", "z1", "z0")
HIGHEST = lax.Precision.HIGHEST
VMEM_LIMIT = 24 * 2**20


def sine_coefficients():
    angle = (np.arange(4000) + 0.5) * math.pi / 4000
    u = 0.125 * (1 + np.cos(angle)) + 1e-9
    w = 1.0
    basis = np.stack([u ** (2 * i + 1) for i in range(5)], axis=1)
    fit, *_ = np.linalg.lstsq(basis / w, np.sin(2 * math.pi * u) / w, rcond=None)
    return [float(c) for c in fit]


SINE = sine_coefficients()
ROUNDER = float(1.5 * 2**23)


def sine(x):
    turns = x * F32(1 / (2 * math.pi))
    part = turns - ((turns + F32(ROUNDER)) - F32(ROUNDER))
    part = jnp.maximum(jnp.minimum(part, F32(0.5) - part), F32(-0.5) - part)
    sq = part * part
    value = F32(SINE[4])
    for c in SINE[3::-1]:
        value = value * sq + F32(c)
    return value * part


def dot(a, b, contract, precision=None):
    return lax.dot_general(
        a, b, ((contract[0:1], contract[1:2]), ((), ())), precision=precision, preferred_element_type=F32
    )


def on_core(kernel, out_shape, in_specs, name, scratch=(), flops=10**9):
    vmem = pl.BlockSpec(memory_space=pltpu.VMEM)
    smem = pl.BlockSpec(memory_space=pltpu.SMEM)
    return pl.pallas_call(
        kernel,
        out_shape=out_shape,
        in_specs=[smem if spec else vmem for spec in in_specs],
        out_specs=jax.tree.map(lambda _: vmem, out_shape),
        scratch_shapes=scratch,
        compiler_params=pltpu.CompilerParams(vmem_limit_bytes=VMEM_LIMIT),
        cost_estimate=pl.CostEstimate(flops=flops, bytes_accessed=2**20, transcendentals=0),
        name=name,
    )


def quarter_of(order, where):
    low, second, core = where[1], where[2], where[3]
    if order < 2:
        return 2 * (1 - low) + (second + core + 1 - order) % 2
    return 2 * low + (second + 1 - (order - 2)) % 2


def tile_kernel(where_ref, counts_ref, tex_ref, light_ref, sketch_ref, tile_ref, part_ref, *, order, step=128):
    first = quarter_of(order, where_ref) * tile_ref.shape[0]
    count = counts_ref[where_ref[0]]
    for at in range(0, tile_ref.shape[0], step):
        tex = tex_ref[pl.ds(pl.multiple_of(first + at, step), step), :]
        tile = sine(dot(tex, light_ref[...], (1, 1))).astype(BF16)
        tile_ref[at : at + step, :] = tile
        part = dot(tile, sketch_ref[...], (1, 0))
        row = first + at + lax.broadcasted_iota(jnp.int32, part.shape, 0)
        part_ref[at : at + step, :] = jnp.where(row < count, part, 0.0)


def tile_call(order, where, counts, tex, light, sketch):
    rows = tex.shape[0] // 4
    return on_core(
        lambda *refs: tile_kernel(*refs, order=order),
        (
            jax.ShapeDtypeStruct((rows, light.shape[0]), BF16),
            jax.ShapeDtypeStruct((rows, sketch.shape[1]), F32),
        ),
        (True, True, False, False, False),
        "tile_quarter",
        flops=2 * rows * light.shape[0] * (tex.shape[1] + sketch.shape[1]),
    )(where, counts, tex, light, sketch)


def gram_kernel(most_ref, rest_ref, gram_ref):
    gram = None
    for ref in (most_ref, rest_ref):
        rows = ref[...].reshape(-1, ref.shape[-1])
        product = dot(rows, rows, (0, 0), HIGHEST)
        gram = product if gram is None else gram + product
    gram_ref[...] = gram


def invert_factor(gram, y_ref, a_ref, w_ref):
    size = gram.shape[0]
    row = lax.broadcasted_iota(jnp.int32, (size, size), 0)
    col = lax.broadcasted_iota(jnp.int32, (size, size), 1)
    diagonal = jnp.sum(jnp.where(row == col, gram, 0.0), axis=0, keepdims=True)
    a_ref[...] = gram
    y_ref[...] = jnp.where(row == col, lax.rsqrt(diagonal), 0.0)

    def refine(exact):
        precision = HIGHEST if exact else None
        cast = (lambda v: v) if exact else (lambda v: v.astype(BF16))
        y = cast(y_ref[...])
        product = dot(dot(y, cast(a_ref[...]), (1, 0), precision).astype(y.dtype), y, (1, 1), precision)
        off = product - jnp.where(row == col, F32(1), F32(0))
        step = jnp.where(row > col, off, jnp.where(row == col, 0.5 * off, 0.0))
        y_ref[...] = y_ref[...] - dot(cast(step), y, (1, 0), precision)
        return jnp.sum(off * off)

    def coarse(state):
        count, _ = state
        return count + 1, refine(False)

    def fine(state):
        count, _ = state
        return count + 1, refine(True)

    lax.while_loop(lambda s: (s[0] < 8) & (s[1] > 2e-2), coarse, (jnp.int32(0), F32(1)))
    _, rest = lax.while_loop(lambda s: (s[0] < 8) & (s[1] > 4e-6), fine, (jnp.int32(0), F32(1)))

    @pl.when(jnp.logical_not(rest <= 4e-6))
    def _():
        y_ref[...] = jnp.where(row == col, F32(1), F32(0))
        line = lax.broadcasted_iota(jnp.int32, (size, 1), 0)
        w_ref[...] = gram

        def eliminate(j, carry):
            work = w_ref[...]
            column = jnp.sum(jnp.where(col == j, work, 0.0), axis=1, keepdims=True)
            pivot = lax.rsqrt(jnp.sum(jnp.where(line == j, column, 0.0), axis=0, keepdims=True))
            top = w_ref[pl.ds(j, 1), :] * pivot
            top_y = y_ref[pl.ds(j, 1), :] * pivot
            factor = jnp.where(line > j, column * pivot, 0.0)
            w_ref[...] = work - factor * top
            y_ref[...] = jnp.where(line == j, top_y, y_ref[...] - factor * top_y)
            return carry

        lax.fori_loop(0, size, eliminate, 0)


def basis_kernel(
    where_ref, counts_ref, gram_ref, most_ref, rest_ref, *refs
):
    tile_refs, (basis_ref, keep_ref, send_ref, y_ref, a_ref, w_ref, coeff_ref) = refs[:4], refs[4:]
    total = F32(0)
    for i in range(counts_ref.shape[0]):
        total = total + counts_ref[i].astype(F32)
    invert_factor(gram_ref[...] / total, y_ref, a_ref, w_ref)
    inverse = y_ref[...]
    owners = most_ref.shape[0]
    share = most_ref.shape[1] + rest_ref.shape[1]
    quarter = owners * share // 4
    offset = 0
    for ref in (most_ref, rest_ref):
        lines = ref.shape[1]
        basis = dot(ref[...].reshape(owners * lines, ref.shape[2]), inverse, (1, 1), HIGHEST)
        for z in range(owners):
            start = (2 * (z & 1) + (z >> 1 & 1)) * quarter + (z >> 2) * share + offset
            basis_ref[start : start + lines, :] = basis[z * lines : (z + 1) * lines, :]
        offset += lines
    coeffs = None
    for order, tile_ref in enumerate(tile_refs):
        start = pl.multiple_of(quarter_of(order, where_ref) * quarter, quarter)
        product = dot(basis_ref[pl.ds(start, quarter), :].astype(BF16), tile_ref[...], (0, 0))
        coeffs = product if coeffs is None else coeffs + product
    scale = 1.0 / jnp.sqrt(jnp.full((1, 1), total, F32))
    coeff_ref[...] = (coeffs * scale).reshape(coeff_ref.shape)
    core = where_ref[3]
    for i in range(keep_ref.shape[0]):
        keep_ref[i] = coeff_ref[2 * i + core]
        send_ref[i] = coeff_ref[2 * i + 1 - core]


def light_pairs(count, reach):
    pairs = []
    for core in range(2):
        shift = core * reach
        for z in range(count):
            pairs.append((core * count + z, core * count + ((((z - shift) % count) ^ reach) + shift) % count))
    return pairs


def across(value, reach):
    return lax.ppermute(value, ("core", *LIGHT), light_pairs(lax.axis_size(LIGHT), reach))


def across_cores(value):
    return lax.ppermute(value, "core", [(0, 1), (1, 0)])


def each_to_each(parts, axes):
    return lax.all_to_all(parts, axes, 0, 0, tiled=True)


def to_each(value, axes):
    return each_to_each(jnp.broadcast_to(value, (lax.axis_size(axes), *value.shape)), axes)


def on_device(tex_feat, light_feat, sketch, row_counts):
    capacity, width = tex_feat.shape[0], sketch.shape[1]
    lights = light_feat.shape[0]
    texels, places = lax.axis_size(TEXEL), lax.axis_size(LIGHT)
    share = capacity // places
    most = share - 8
    where = jnp.stack([lax.axis_index(axes) for axes in (TEXEL, "z0", "z1", "core")]).astype(jnp.int32)

    inputs = (where, row_counts, tex_feat, light_feat, sketch)
    tiles, parts = [None] * 4, [None] * 4
    tiles[0], parts[0] = tile_call(0, *inputs)
    passing = across(parts[0], 1)
    tiles[1], parts[1] = tile_call(1, *inputs)
    staying = across(parts[1], 1)
    tiles[2], parts[2] = tile_call(2, *inputs)
    passed = across(parts[2] + passing, 2)
    tiles[3], parts[3] = tile_call(3, *inputs)
    quarter = parts[3] + staying + passed
    shares = each_to_each(quarter.reshape(places // 4, share, width), ("z3", "z2"))
    own = jnp.sum(shares, axis=0)

    rest_rows = to_each(own[most:], LIGHT)
    most_rows = lax.all_gather(own[:most], LIGHT, axis=0)
    rest_rows = rest_rows.reshape(places, share - most, width)

    gram = on_core(gram_kernel, jax.ShapeDtypeStruct((width, width), F32), (False, False), "gram_part")(
        most_rows, rest_rows
    )
    gram = gram + across_cores(gram)
    chips = lax.axis_size(CHIP)
    gram_rows = jnp.sum(each_to_each(gram.reshape(chips, width // chips, width), CHIP), axis=0)
    gram = to_each(gram_rows, CHIP).reshape(width, width)

    lines = width // texels
    basis, keep, send = on_core(
        basis_kernel,
        (
            jax.ShapeDtypeStruct((capacity, width), F32),
            jax.ShapeDtypeStruct((chips, lines, lights), F32),
            jax.ShapeDtypeStruct((chips, lines, lights), F32),
        ),
        (True, True) + (False,) * 7,
        "basis_and_coeffs",
        scratch=[pltpu.VMEM((width, width), F32)] * 3 + [pltpu.VMEM((texels, lines, lights), F32)],
    )(where, row_counts, gram, most_rows, rest_rows, *tiles)
    mine = keep + across_cores(send)
    coeffs = jnp.sum(each_to_each(mine, CHIP), axis=0)
    return basis, coeffs


def solution(mesh):
    fine = Mesh(np.asarray(mesh.devices).reshape(4, 4, 2, 2, 2, 2, 2), (*TEXEL, *LIGHT))
    placed = (P(TEXEL, None), P(LIGHT, None), P(LIGHT, None), P())
    return jax.shard_map(
        on_device, mesh=fine, in_specs=placed, out_specs=(P(TEXEL, None), P(TEXEL, LIGHT)), check_vma=False
    )
```

time: 228 us -> 230 us (level)
  starting transfers between devices: 16.1 us -> 35.8 us
  blocking collectives: 115 us -> 99.5 us
  waiting for transfers between devices: 12.6 us -> 7.77 us
    all_to_all x4, blocking collectives: 90.3 us -> 67.6 us  [each_to_each(): return lax.all_to_all(parts, axes, 0, 0, tiled=True)]
    ppermute x3 -> x5, starting transfers between devices: 16.1 us -> 31.2 us  [the longest x3 17.7 us: across(): lax.ppermute(value, ('core', *LIGHT), light_pairs(lax.axis_size(LIGHT), r...]
    all_gather x1, blocking collectives: 24.9 us -> 31.9 us  [on_device(): most_rows = lax.all_gather(own[:most], LIGHT, axis=0)]
    ppermute x3 -> x5, waiting for transfers between devices: 12.6 us -> 7.77 us  [the longest x3 4.74 us: across(): lax.ppermute(value, ('core', *LIGHT), light_pairs(lax.axis_size(LIGHT), r...]
    all_to_all x0 -> x1, starting transfers between devices: none -> 4.55 us  [each_to_each(): return lax.all_to_all(parts, axes, 0, 0, tiled=True)]
    pallas_call x4 -> x6, Pallas kernels: 75.1 us -> 76 us  [the longest x1 66.3 us: on_device(): on_core(basis_kernel, (jax.ShapeDtypeStruct((capacity, width), F32), jax....]
  transfers between devices with their start and end apart: 3 -> 6, of which waited for: 3 -> 3; matrix products, arithmetic and copies ran while one was open for 0% -> 0% of each run, Pallas kernels for 2% -> 3%
where the time goes in v3:
time: 230 us; the launch traced here: 229 us
  blocking collectives  99.5 us (43%)
  Pallas kernels  76 us (33%)
  starting transfers between devices  35.8 us (16%)
  waiting for transfers between devices  7.77 us (3%)
  local copies, waits for them, and re-layouts  7.12 us (3%)
    all_to_all x4, blocking collectives, each_to_each(): return lax.all_to_all(parts, axes, 0, 0, tiled=True)  67.6 us
    pallas_call x1, Pallas kernels, on_device(): on_core(basis_kernel, (jax.ShapeDtypeStruct((capacity, width), F32), jax....  66.3 us
    all_gather x1, blocking collectives, on_device(): most_rows = lax.all_gather(own[:most], LIGHT, axis=0)  31.9 us
    ppermute x3, starting transfers between devices, across(): lax.ppermute(value, ('core', *LIGHT), light_pairs(lax.axis_size(LIGHT), r...  17.7 us
    ppermute x2, starting transfers between devices, across_cores(): return lax.ppermute(value, 'core', [(0, 1), (1, 0)])  13.6 us
    pallas_call x4, Pallas kernels, tile_call(): on_core(lambda *refs: tile_kernel(*refs, order=order), (jax.ShapeDtypeStr...  8.4 us
    unnamed x14, local copies, waits for them, and re-layouts  6.44 us
    ppermute x3, waiting for transfers between devices, across(): lax.ppermute(value, ('core', *LIGHT), light_pairs(lax.axis_size(LIGHT), r...  4.74 us
  transfers between devices with their start and end apart: 6, of which 3 were waited for; matrix products, arithmetic and copies ran while one was open for 0% of the time, Pallas kernels for 3%

profile of v3, /device:TPU:1, one launch (start us, length us, event | category | flops | bytes accessed | tf_op | source)
XLA Modules:
  0.0 228.9 jit_solution(1324899913947411788)
XLA Ops:
  0.6 0.1 pad_add_fusion.refs_0_.where_ref
  0.7 1.4 copy-done
  2.1 1.2 copy-done.1
  3.4 1.1 copy-done.2
  4.5 0.7 copy-done.5
  5.1 2.1 tile_quarter.7
  7.2 11.9 %collective-permute-start.1 = (f32[256,256]{1,0:T(8,128)S(1)}, f32[256,256]{1,0:T(8,128)S(1)}, u32[]{:S(2)}, u32[]{:S(2)}) collective-permute-start(f32[256,256]{1,0:T(8,128)S(1)} %get-tuple-element.16), channel_id=1, source_target_pairs={{0,1},{1,0},{2,3},{3,2},{4,5},{5,4},{6,7},{7,6},{8,9},{9,8},{10,11... | collective-permute-start | bytes 786440 | tf_op jit(solution)/shard_map/ppermute | solution.py:199
  19.2 2.1 tile_quarter.5
  21.3 1.9 collective-permute-start
  23.2 2.1 tile_quarter.6
  25.4 3.8 %collective-permute-start.2 = (f32[256,256]{1,0:T(8,128)S(1)}, f32[256,256]{1,0:T(8,128)S(1)}, u32[]{:S(2)}, u32[]{:S(2)}) collective-permute-start(f32[256,256]{1,0:T(8,128)S(1)} %add.24), channel_id=1, source_target_pairs={{0,2},{1,3},{2,0},{3,1},{4,6},{5,7},{6,4},{7,5},{8,10},{9,11},{10,... | collective-permute-start | bytes 786440 | tf_op jit(solution)/shard_map/ppermute | solution.py:199
  29.2 2.1 tile_quarter.4
  31.3 0.9 copy-done.3
  32.2 4.7 %collective-permute-done.2 = f32[256,256]{1,0:T(8,128)S(1)} collective-permute-done((f32[256,256]{1,0:T(8,128)S(1)}, f32[256,256]{1,0:T(8,128)S(1)}, u32[]{:S(2)}, u32[]{:S(2)}) %collective-permute-start.2) | collective-permute-done | bytes 262176 | tf_op jit(solution)/shard_map/ppermute | solution.py:199
  36.9 0.1 add_add_fusion
  37.0 26.2 %all_to_all.25 = f32[4,64,256]{2,1,0:T(8,128)S(1)} all-to-all(f32[4,64,256]{2,1,0:T(8,128)S(1)} %bitcast.12), channel_id=1, replica_groups=mesh['x'=4,'y'=4,'core'=2,'z3'=2,'z2'=2,'z1'=2,'z0'=2] {'z3','z2'}, dimensions={0} | all-to-all | bytes 524288 | tf_op jit(solution)/shard_map/all_to_all | solution.py:207
  63.3 0.7 broadcast_in_dim.6
  63.9 4.6 %all-to-all-start.1 = ((f32[16,8,256]{2,1,0:T(8,128)}), f32[16,8,256]{2,1,0:T(8,128)S(1)}, u32[]{:S(2)}, u32[]{:S(2)}) async-start(f32[16,8,256]{2,1,0:T(8,128)} %broadcast_in_dim.6), calls=%async_computation.1 | async-start | bytes 262144 | tf_op jit(solution)/shard_map/all_to_all | solution.py:207
  68.5 31.9 %all-gather = f32[896,256]{1,0:T(8,128)S(1)} all-gather(f32[56,256]{1,0:T(8,128)S(1)} %slice.8), channel_id=2, replica_groups=mesh['x'=4,'y'=4,'core'=2,'z3'=2,'z2'=2,'z1'=2,'z0'=2] {'z3','z2','z1','..., dimensions={0}, use_global_device_ids=true | all-gather | bytes 974848 | tf_op jit(solution)/shard_map/all_gather | solution.py:236
  100.4 1.3 gram_part.1
  101.6 8.7 %collective-permute-start.3 = (f32[256,256]{1,0:T(8,128)S(1)}, f32[256,256]{1,0:T(8,128)S(1)}, u32[]{:S(2)}, u32[]{:S(2)}) collective-permute-start(f32[256,256]{1,0:T(8,128)S(1)} %gram_part.1), channel_id=1, source_target_pairs={{0,16},{16,0},{1,17},{17,1},{2,18},{18,2},{3,19},{19,3},{4,20},{20... | collective-permute-start | bytes 786440 | tf_op jit(solution)/shard_map/ppermute | solution.py:203
  110.4 1.1 collective-permute-done.3
  111.5 14.0 %all_to_all.26 = f32[16,16,256]{2,1,0:T(8,128)} all-to-all(f32[16,16,256]{2,1,0:T(8,128)S(1)} %bitcast.11), channel_id=1, replica_groups=mesh['x'=4,'y'=4,'core'=2,'z3'=2,'z2'=2,'z1'=2,'z0'=2] {'x','y'}, dimensions={0} | all-to-all | bytes 524288 | tf_op jit(solution)/shard_map/all_to_all | solution.py:207
  125.6 1.0 reduce_sum.28
  126.6 10.8 %all_to_all.27 = f32[16,16,256]{2,1,0:T(8,128)S(1)} all-to-all(f32[16,16,256]{2,1,0:T(8,128)S(1)} %broadcast_in_dim.7), channel_id=1, replica_groups=mesh['x'=4,'y'=4,'core'=2,'z3'=2,'z2'=2,'z1'=2,'z0'=2] {'x','y'}, dimensions={0} | all-to-all | bytes 524288 | tf_op jit(solution)/shard_map/all_to_all | solution.py:207
  137.4 1.1 copy-done.4
  138.6 66.3 %basis_and_coeffs.1 = (f32[1024,256]{1,0:T(8,128)}, f32[16,8,1536]{2,1,0:T(8,128)S(1)}, f32[16,8,1536]{2,1,0:T(8,128)S(1)}) custom-call(s32[4]{0:T(128)S(1)} %pad_add_fusion.refs_0_.where_ref, s32[32]{0:T(128)S(1)} %copy-done.6, f32[256,256]{1,0:T(8,128)S(1)} %bitcast.10, f32[16,56,256]{2,1,0:T(8,128)S(1)} %bitcast.9, ...), custom_call_target="tpu_custom_call" | custom-call | flops 1000000000 | bytes 1048576 | tf_op jit(solution)/shard_map/basis_and_coeffs/pallas_call | solution.py:248
  204.9 4.9 %collective-permute-start.4 = (f32[16,8,1536]{2,1,0:T(8,128)S(1)}, f32[16,8,1536]{2,1,0:T(8,128)S(1)}, u32[]{:S(2)}, u32[]{:S(2)}) collective-permute-start(f32[16,8,1536]{2,1,0:T(8,128)S(1)} %get-tuple-element.23), channel_id=1, source_target_pairs={{0,16},{16,0},{1,17},{17,1},{2,18},{18,2},{3,19},{19,3},{4,20},{20... | collective-permute-start | bytes 2359304 | tf_op jit(solution)/shard_map/ppermute | solution.py:203
  209.8 1.9 collective-permute-done.4
  211.7 0.1 add.27
  211.8 16.5 %all_to_all.28 = f32[16,8,1536]{2,1,0:T(8,128)S(1)} all-to-all(f32[16,8,1536]{2,1,0:T(8,128)S(1)} %add.27), channel_id=1, replica_groups=mesh['x'=4,'y'=4,'core'=2,'z3'=2,'z2'=2,'z1'=2,'z0'=2] {'x','y'}, dimensions={0} | all-to-all | bytes 1572864 | tf_op jit(solution)/shard_map/all_to_all | solution.py:207
  228.2 0.7 reduce_sum.29
  (17 shorter events, 0.1 us)
Async XLA Ops:
  0.7 1.4 copy-start
  2.1 1.2 copy-start.1
  3.4 1.1 copy-start.2
  4.5 0.7 copy-start.5
  7.2 18.1 %collective-permute-start.1 = (f32[256,256]{1,0:T(8,128)S(1)}, f32[256,256]{1,0:T(8,128)S(1)}, u32[]{:S(2)}, u32[]{:S(2)}) collective-permute-start(f32[256,256]{1,0:T(8,128)S(1)} %get-tuple-element.16), channel_id=1, source_target_pairs={{0,1},{1,0},{2,3},{3,2},{4,5},{5,4},{6,7},{7,6},{8,9},{9,8},{10,11... | collective-permute-start | bytes 786440 | tf_op jit(solution)/shard_map/ppermute | solution.py:199
  21.3 10.9 %collective-permute-start = (f32[256,256]{1,0:T(8,128)S(1)}, f32[256,256]{1,0:T(8,128)S(1)}, u32[]{:S(2)}, u32[]{:S(2)}) collective-permute-start(f32[256,256]{1,0:T(8,128)S(1)} %get-tuple-element.14), channel_id=1, source_target_pairs={{0,1},{1,0},{2,3},{3,2},{4,5},{5,4},{6,7},{7,6},{8,9},{9,8},{10,11... | collective-permute-start | bytes 786440 | tf_op jit(solution)/shard_map/ppermute | solution.py:199
  25.4 11.5 %collective-permute-start.2 = (f32[256,256]{1,0:T(8,128)S(1)}, f32[256,256]{1,0:T(8,128)S(1)}, u32[]{:S(2)}, u32[]{:S(2)}) collective-permute-start(f32[256,256]{1,0:T(8,128)S(1)} %add.24), channel_id=1, source_target_pairs={{0,2},{1,3},{2,0},{3,1},{4,6},{5,7},{6,4},{7,5},{8,10},{9,11},{10,... | collective-permute-start | bytes 786440 | tf_op jit(solution)/shard_map/ppermute | solution.py:199
  31.3 0.9 copy-start.3
  63.9 36.5 %all-to-all-start.1 = ((f32[16,8,256]{2,1,0:T(8,128)}), f32[16,8,256]{2,1,0:T(8,128)S(1)}, u32[]{:S(2)}, u32[]{:S(2)}) async-start(f32[16,8,256]{2,1,0:T(8,128)} %broadcast_in_dim.6), calls=%async_computation.1 | async-start | bytes 262144 | tf_op jit(solution)/shard_map/all_to_all | solution.py:207
  101.6 35.8 %copy-start.6 = (s32[32]{0:T(128)S(1)}, s32[32]{0:T(128)}, u32[]{:S(2)}) copy-start(s32[32]{0:T(128)} %counts_ref.1) | copy-start | bytes 388
  101.6 9.9 %collective-permute-start.3 = (f32[256,256]{1,0:T(8,128)S(1)}, f32[256,256]{1,0:T(8,128)S(1)}, u32[]{:S(2)}, u32[]{:S(2)}) collective-permute-start(f32[256,256]{1,0:T(8,128)S(1)} %gram_part.1), channel_id=1, source_target_pairs={{0,16},{16,0},{1,17},{17,1},{2,18},{18,2},{3,19},{19,3},{4,20},{20... | collective-permute-start | bytes 786440 | tf_op jit(solution)/shard_map/ppermute | solution.py:203
  137.4 1.1 copy-start.4
  204.9 6.8 %collective-permute-start.4 = (f32[16,8,1536]{2,1,0:T(8,128)S(1)}, f32[16,8,1536]{2,1,0:T(8,128)S(1)}, u32[]{:S(2)}, u32[]{:S(2)}) collective-permute-start(f32[16,8,1536]{2,1,0:T(8,128)S(1)} %get-tuple-element.23), channel_id=1, source_target_pairs={{0,16},{16,0},{1,17},{17,1},{2,18},{18,2},{3,19},{19,3},{4,20},{20... | collective-permute-start | bytes 2359304 | tf_op jit(solution)/shard_map/ppermute | solution.py:203

commit v4 on v3

v4 whole, which is shorter than its diff:
```python
import functools
import math

import jax
import jax.numpy as jnp
import numpy as np
from jax import lax
from jax.experimental import pallas as pl
from jax.experimental.pallas import tpu as pltpu
from jax.sharding import Mesh, PartitionSpec as P

F32 = jnp.float32
BF16 = jnp.bfloat16
CHIP = ("x", "y")
TEXEL = CHIP + ("core",)
FAR = ("z3", "z2")
LIGHT = FAR + ("z1", "z0")
HIGHEST = lax.Precision.HIGHEST
VMEM_LIMIT = 24 * 2**20
COUNTS = 5


def sine_coefficients():
    angle = (np.arange(4000) + 0.5) * math.pi / 4000
    u = 0.125 * (1 + np.cos(angle)) + 1e-9
    w = 1.0
    basis = np.stack([u ** (2 * i + 1) for i in range(5)], axis=1)
    fit, *_ = np.linalg.lstsq(basis / w, np.sin(2 * math.pi * u) / w, rcond=None)
    return [float(c) for c in fit]


SINE = sine_coefficients()
ROUNDER = float(1.5 * 2**23)


def sine(x):
    turns = x * F32(1 / (2 * math.pi))
    part = turns - ((turns + F32(ROUNDER)) - F32(ROUNDER))
    part = jnp.maximum(jnp.minimum(part, F32(0.5) - part), F32(-0.5) - part)
    sq = part * part
    value = F32(SINE[4])
    for c in SINE[3::-1]:
        value = value * sq + F32(c)
    return value * part


def dot(a, b, contract, precision=None):
    return lax.dot_general(
        a, b, ((contract[0:1], contract[1:2]), ((), ())), precision=precision, preferred_element_type=F32
    )


VMEM = pl.BlockSpec(memory_space=pltpu.VMEM)
SMEM = pl.BlockSpec(memory_space=pltpu.SMEM)


def on_core(kernel, out_shape, in_specs, name, scratch=(), flops=10**9, aliases=None):
    return pl.pallas_call(
        kernel,
        out_shape=out_shape,
        in_specs=in_specs,
        out_specs=jax.tree.map(lambda _: VMEM, out_shape),
        scratch_shapes=scratch,
        input_output_aliases=aliases or {},
        compiler_params=pltpu.CompilerParams(vmem_limit_bytes=VMEM_LIMIT),
        cost_estimate=pl.CostEstimate(flops=flops, bytes_accessed=2**20, transcendentals=0),
        name=name,
    )


def quarter_of(order, where):
    low, second, core = where[1], where[2], where[3]
    if order < 2:
        return 2 * (1 - low) + (second + core + 1 - order) % 2
    return 2 * low + (second + 1 - (order - 2)) % 2


def tile_kernel(where_ref, tex_ref, light_ref, sketch_ref, *refs, order, step=128):
    tile_ref, part_ref = refs[-2:]
    rows = part_ref.shape[0]
    first = quarter_of(order, where_ref) * rows
    count = where_ref[COUNTS + where_ref[0]]
    for at in range(0, rows, step):
        tex = tex_ref[pl.ds(pl.multiple_of(first + at, step), step), :]
        tile = sine(dot(tex, light_ref[...], (1, 1))).astype(BF16)
        tile_ref[order * rows + at : order * rows + at + step, :] = tile
        part = dot(tile, sketch_ref[...], (1, 0))
        row = first + at + lax.broadcasted_iota(jnp.int32, part.shape, 0)
        part_ref[at : at + step, :] = jnp.where(row < count, part, 0.0)


def tile_call(order, where, tex, light, sketch, *tiles):
    rows, lights, width = tex.shape[0] // 4, light.shape[0], sketch.shape[1]
    return on_core(
        lambda *refs: tile_kernel(*refs, order=order),
        (jax.ShapeDtypeStruct((tex.shape[0], lights), BF16), jax.ShapeDtypeStruct((rows, width), F32)),
        [SMEM] + [VMEM] * (3 + len(tiles)),
        "tile_quarter",
        flops=2 * rows * lights * (tex.shape[1] + width),
        aliases={4: 0} if tiles else None,
    )(where, tex, light, sketch, *tiles)


def gram_kernel(share_ref, gram_ref):
    gram_ref[...] = dot(share_ref[...], share_ref[...], (0, 0), HIGHEST)


def invert_factor(gram, y_ref, a_ref, w_ref):
    size = gram.shape[0]
    row = lax.broadcasted_iota(jnp.int32, (size, size), 0)
    col = lax.broadcasted_iota(jnp.int32, (size, size), 1)
    diagonal = jnp.sum(jnp.where(row == col, gram, 0.0), axis=0, keepdims=True)
    a_ref[...] = gram
    y_ref[...] = jnp.where(row == col, lax.rsqrt(diagonal), 0.0)

    def refine(exact):
        precision = HIGHEST if exact else None
        cast = (lambda v: v) if exact else (lambda v: v.astype(BF16))
        y = cast(y_ref[...])
        product = dot(dot(y, cast(a_ref[...]), (1, 0), precision).astype(y.dtype), y, (1, 1), precision)
        off = product - jnp.where(row == col, F32(1), F32(0))
        step = jnp.where(row > col, off, jnp.where(row == col, 0.5 * off, 0.0))
        y_ref[...] = y_ref[...] - dot(cast(step), y, (1, 0), precision)
        return jnp.sum(off * off)

    def coarse(state):
        count, _ = state
        return count + 1, refine(False)

    def fine(state):
        count, _ = state
        return count + 1, refine(True)

    lax.while_loop(lambda s: (s[0] < 8) & (s[1] > 2e-2), coarse, (jnp.int32(0), F32(1)))
    _, rest = lax.while_loop(lambda s: (s[0] < 8) & (s[1] > 4e-6), fine, (jnp.int32(0), F32(1)))

    @pl.when(jnp.logical_not(rest <= 4e-6))
    def _():
        y_ref[...] = jnp.where(row == col, F32(1), F32(0))
        line = lax.broadcasted_iota(jnp.int32, (size, 1), 0)
        w_ref[...] = gram

        def eliminate(j, carry):
            work = w_ref[...]
            column = jnp.sum(jnp.where(col == j, work, 0.0), axis=1, keepdims=True)
            pivot = lax.rsqrt(jnp.sum(jnp.where(line == j, column, 0.0), axis=0, keepdims=True))
            top = w_ref[pl.ds(j, 1), :] * pivot
            top_y = y_ref[pl.ds(j, 1), :] * pivot
            factor = jnp.where(line > j, column * pivot, 0.0)
            w_ref[...] = work - factor * top
            y_ref[...] = jnp.where(line == j, top_y, y_ref[...] - factor * top_y)
            return carry

        lax.fori_loop(0, size, eliminate, 0)


def total_of(where_ref):
    total = F32(0)
    for i in range(COUNTS, where_ref.shape[0]):
        total = total + where_ref[i].astype(F32)
    return total


def inverse_kernel(where_ref, gram_ref, inverse_ref, a_ref, w_ref):
    invert_factor(gram_ref[...] / total_of(where_ref), inverse_ref, a_ref, w_ref)


def basis_kernel(
    where_ref, inverse_ref, own_ref, other_ref, tile_ref,
    basis_ref, keep_ref, send_ref, half_ref, coeff_ref, *, share, places,
):
    inverse = inverse_ref[...]
    rows = basis_ref.shape[0] // 4
    groups = rows // share
    own, core = where_ref[4], where_ref[3]

    def partner(z, reach):
        shift = core * reach
        return (((z - shift + places) % places ^ reach) + shift) % places

    for ref, owner, orders in ((own_ref, own, (3, 2)), (other_ref, partner(own, 1), (1, 0))):
        basis = dot(ref[...], inverse, (1, 1), HIGHEST)
        for i, order in enumerate(orders):
            group = (owner if i == 0 else partner(owner, 2)) // (places // groups)
            start = quarter_of(order, where_ref) * rows
            for j, turn in enumerate((0, groups - 1, 1, 2)):
                at = (group + turn) % groups * share
                part = basis[i * rows + j * share : i * rows + (j + 1) * share, :]
                basis_ref[pl.ds(pl.multiple_of(start + at, share), share), :] = part
                half_ref[pl.ds(pl.multiple_of(order * rows + at, share), share), :] = part.astype(BF16)
    coeffs = dot(half_ref[...], tile_ref[...], (0, 0))
    scale = 1.0 / jnp.sqrt(jnp.full((1, 1), total_of(where_ref), F32))
    coeff_ref[...] = (coeffs * scale).reshape(coeff_ref.shape)
    for i in range(keep_ref.shape[0]):
        keep_ref[i] = coeff_ref[2 * i + core]
        send_ref[i] = coeff_ref[2 * i + 1 - core]


def light_pairs(count, reach):
    pairs = []
    for core in range(2):
        shift = core * reach
        for z in range(count):
            pairs.append((core * count + z, core * count + ((((z - shift) % count) ^ reach) + shift) % count))
    return pairs


def across(value, reach):
    return lax.ppermute(value, ("core", *LIGHT), light_pairs(lax.axis_size(LIGHT), reach))


def across_cores(value):
    return lax.ppermute(value, "core", [(0, 1), (1, 0)])


def each_to_each(parts, axes):
    return lax.all_to_all(parts, axes, 0, 0, tiled=True)


def to_each(value, axes):
    return each_to_each(jnp.broadcast_to(value, (lax.axis_size(axes), *value.shape)), axes)


def around(value, turn):
    places = lax.axis_size(LIGHT)
    return lax.ppermute(value, LIGHT, [(z, (z + 4 * turn) % places) for z in range(places)])


def on_device(tex_feat, light_feat, sketch, row_counts):
    capacity, width = tex_feat.shape[0], sketch.shape[1]
    lights = light_feat.shape[0]
    texels, places = lax.axis_size(TEXEL), lax.axis_size(LIGHT)
    share_rows = capacity // places
    marks = [lax.axis_index(axes) for axes in (TEXEL, "z0", "z1", "core", LIGHT)]
    where = jnp.concatenate([jnp.stack(marks).astype(jnp.int32), row_counts])

    inputs = (where, tex_feat, light_feat, sketch)
    tiles, part = tile_call(0, *inputs)
    passing = across(part, 1)
    tiles, part = tile_call(1, *inputs, tiles)
    staying = across(part, 1)
    tiles, part = tile_call(2, *inputs, tiles)
    passed = across(part + passing, 2)
    tiles, part = tile_call(3, *inputs, tiles)
    quarter = part + staying + passed
    share = jnp.sum(each_to_each(quarter.reshape(places // 4, share_rows, width), FAR), axis=0)

    before, behind = around(share, 1), around(share, -1)
    gram = on_core(gram_kernel, jax.ShapeDtypeStruct((width, width), F32), [VMEM], "gram_part")(share)
    gram_rows = jnp.sum(each_to_each(gram.reshape(texels, width // texels, width), TEXEL), axis=0)
    gram_rows, before, behind = lax.optimization_barrier((gram_rows, before, behind))
    opposite = around(before, 1)
    gram_rows = jnp.sum(to_each(gram_rows, LIGHT), axis=0)
    gram_rows, opposite = lax.optimization_barrier((gram_rows, opposite))
    quarter = jnp.concatenate([share, before, behind, opposite])
    own = jnp.concatenate([quarter, across(quarter, 2)])
    gram = to_each(gram_rows, TEXEL).reshape(width, width)
    gram, own = lax.optimization_barrier((gram, own))
    other = across(own, 1)
    inverse = on_core(
        inverse_kernel,
        jax.ShapeDtypeStruct((width, width), F32),
        [SMEM, VMEM],
        "inverse_factor",
        [pltpu.VMEM((width, width), F32)] * 2,
        10**10,
    )(where, gram)

    lines, chips = width // texels, lax.axis_size(CHIP)
    basis, keep, send = on_core(
        functools.partial(basis_kernel, share=share_rows, places=places),
        (
            jax.ShapeDtypeStruct((capacity, width), F32),
            jax.ShapeDtypeStruct((chips, lines, lights), F32),
            jax.ShapeDtypeStruct((chips, lines, lights), F32),
        ),
        [SMEM] + [VMEM] * 4,
        "basis_and_coeffs",
        [pltpu.VMEM((capacity, width), BF16), pltpu.VMEM((texels, lines, lights), F32)],
    )(where, inverse, own, other, tiles)
    mine = keep + across_cores(send)
    coeffs = jnp.sum(each_to_each(mine, CHIP), axis=0)
    return basis, coeffs


def solution(mesh):
    fine = Mesh(np.asarray(mesh.devices).reshape(4, 4, 2, 2, 2, 2, 2), (*TEXEL, *LIGHT))
    placed = (P(TEXEL, None), P(LIGHT, None), P(LIGHT, None), P())
    return jax.shard_map(
        on_device, mesh=fine, in_specs=placed, out_specs=(P(TEXEL, None), P(TEXEL, LIGHT)), check_vma=False
    )
```

time: 230 us -> 230 us (level)
  blocking collectives: 99.5 us -> 42.5 us
  starting transfers between devices: 35.8 us -> 70.7 us
  waiting for transfers between devices: 7.77 us -> 24.4 us
  local copies, waits for them, and re-layouts: 7.12 us -> 10.9 us
    all_gather x1 -> x0, blocking collectives: 31.9 us -> none  [on_device(): most_rows = lax.all_gather(own[:most], LIGHT, axis=0)]
    all_to_all x4 -> x2, blocking collectives: 67.6 us -> 42.5 us  [each_to_each(): return lax.all_to_all(parts, axes, 0, 0, tiled=True)]
    all_to_all x1 -> x3, starting transfers between devices: 4.55 us -> 24 us  [each_to_each(): return lax.all_to_all(parts, axes, 0, 0, tiled=True)]
    ppermute x0 -> x3, starting transfers between devices: none -> 16.4 us  [around(): lax.ppermute(value, LIGHT, [(z, (z + 4 * turn) % places) for z in range(p...]
    ppermute x2 -> x1, starting transfers between devices: 13.6 us -> 1.91 us  [across_cores(): return lax.ppermute(value, 'core', [(0, 1), (1, 0)])]
    ppermute x3 -> x5, starting transfers between devices: 17.7 us -> 28.4 us  [across(): lax.ppermute(value, ('core', *LIGHT), light_pairs(lax.axis_size(LIGHT), r...]
    all_to_all x1 -> x3, waiting for transfers between devices: 0.01 us -> 10.2 us  [each_to_each(): return lax.all_to_all(parts, axes, 0, 0, tiled=True)]
    ppermute x0 -> x3, waiting for transfers between devices: none -> 6.36 us  [around(): lax.ppermute(value, LIGHT, [(z, (z + 4 * turn) % places) for z in range(p...]
  transfers between devices with their start and end apart: 6 -> 12, of which waited for: 3 -> 6; matrix products, arithmetic and copies ran while one was open for 0% -> 3% of each run, Pallas kernels for 3% -> 31%
where the time goes in v4:
time: 230 us; the launch traced here: 229 us
  Pallas kernels  77 us (33%)
  starting transfers between devices  70.7 us (31%)
  blocking collectives  42.5 us (18%)
  waiting for transfers between devices  24.4 us (11%)
  local copies, waits for them, and re-layouts  10.9 us (5%)
  other arithmetic  2.49 us (1%)
    pallas_call x1, Pallas kernels, on_device(): on_core(inverse_kernel, jax.ShapeDtypeStruct((width, width), F32), [SMEM,...  63.6 us
    all_to_all x2, blocking collectives, each_to_each(): return lax.all_to_all(parts, axes, 0, 0, tiled=True)  42.5 us
    ppermute x5, starting transfers between devices, across(): lax.ppermute(value, ('core', *LIGHT), light_pairs(lax.axis_size(LIGHT), r...  28.4 us
    all_to_all x3, starting transfers between devices, each_to_each(): return lax.all_to_all(parts, axes, 0, 0, tiled=True)  24 us
    ppermute x3, starting transfers between devices, around(): lax.ppermute(value, LIGHT, [(z, (z + 4 * turn) % places) for z in range(p...  16.4 us
    all_to_all x3, waiting for transfers between devices, each_to_each(): return lax.all_to_all(parts, axes, 0, 0, tiled=True)  10.2 us
    pallas_call x4, Pallas kernels, tile_call(): on_core(lambda *refs: tile_kernel(*refs, order=order), (jax.ShapeDtypeStr...  8.57 us
    unnamed x12, local copies, waits for them, and re-layouts  7.15 us
  transfers between devices with their start and end apart: 12, of which 6 were waited for; matrix products, arithmetic and copies ran while one was open for 3% of the time, Pallas kernels for 31%

profile of v4, /device:TPU:1, one launch (start us, length us, event | category | flops | bytes accessed | tf_op | source)
XLA Modules:
  0.0 228.9 jit_solution(2279748773275693215)
XLA Ops:
  1.4 1.4 copy-done
  2.8 1.2 copy-done.1
  4.0 1.1 copy-done.2
  5.1 2.1 tile_quarter.4
  7.3 12.0 %collective-permute-start.1 = (f32[256,256]{1,0:T(8,128)S(1)}, f32[256,256]{1,0:T(8,128)S(1)}, u32[]{:S(2)}, u32[]{:S(2)}) collective-permute-start(f32[256,256]{1,0:T(8,128)S(1)} %get-tuple-element.26), channel_id=1, source_target_pairs={{0,1},{1,0},{2,3},{3,2},{4,5},{5,4},{6,7},{7,6},{8,9},{9,8},{10,11... | collective-permute-start | bytes 786440 | tf_op jit(solution)/shard_map/ppermute | solution.py:209
  19.3 2.1 tile_quarter.5
  21.4 1.9 collective-permute-start
  23.3 2.1 tile_quarter.6
  25.5 3.8 %collective-permute-start.2 = (f32[256,256]{1,0:T(8,128)S(1)}, f32[256,256]{1,0:T(8,128)S(1)}, u32[]{:S(2)}, u32[]{:S(2)}) collective-permute-start(f32[256,256]{1,0:T(8,128)S(1)} %add.33), channel_id=1, source_target_pairs={{0,2},{1,3},{2,0},{3,1},{4,6},{5,7},{6,4},{7,5},{8,10},{9,11},{10,... | collective-permute-start | bytes 786440 | tf_op jit(solution)/shard_map/ppermute | solution.py:209
  29.3 2.1 tile_quarter.7
  31.5 5.6 %collective-permute-done.2 = f32[256,256]{1,0:T(8,128)S(1)} collective-permute-done((f32[256,256]{1,0:T(8,128)S(1)}, f32[256,256]{1,0:T(8,128)S(1)}, u32[]{:S(2)}, u32[]{:S(2)}) %collective-permute-start.2) | collective-permute-done | bytes 262176 | tf_op jit(solution)/shard_map/ppermute | solution.py:209
  37.1 26.2 %all_to_all.25 = f32[4,64,256]{2,1,0:T(8,128)S(1)} all-to-all(f32[4,64,256]{2,1,0:T(8,128)S(1)} %bitcast.9), channel_id=1, replica_groups=mesh['x'=4,'y'=4,'core'=2,'z3'=2,'z2'=2,'z1'=2,'z0'=2] {'z3','z2'}, dimensions={0} | all-to-all | bytes 524288 | tf_op jit(solution)/shard_map/all_to_all | solution.py:217
  64.5 8.4 %all-to-all-start.1 = ((f32[32,8,256]{2,1,0:T(8,128)}), f32[32,8,256]{2,1,0:T(8,128)S(1)}, u32[]{:S(2)}, u32[]{:S(2)}) async-start(f32[32,8,256]{2,1,0:T(8,128)} %bitcast.6), calls=%async_computation.1 | async-start | bytes 524288 | tf_op jit(solution)/shard_map/all_to_all | solution.py:217
  72.9 2.3 collective-permute-start.3
  75.2 6.9 %collective-permute-start.4 = (f32[64,256]{1,0:T(8,128)S(1)}, f32[64,256]{1,0:T(8,128)S(1)}, u32[]{:S(2)}, u32[]{:S(2)}) collective-permute-start(f32[64,256]{1,0:T(8,128)S(1)} %reduce_sum.36.share_ref), channel_id=1, source_target_pairs={{0,12},{1,13},{2,14},{3,15},{4,0},{5,1},{6,2},{7,3},{8,4},{9,5},{1... | collective-permute-start | bytes 196616 | tf_op jit(solution)/shard_map/ppermute | solution.py:226
  82.2 4.5 %collective-permute-done.3 = f32[64,256]{1,0:T(8,128)} collective-permute-done((f32[64,256]{1,0:T(8,128)S(1)}, f32[64,256]{1,0:T(8,128)}, u32[]{:S(2)}, u32[]{:S(2)}) %collective-permute-start.3) | collective-permute-done | bytes 65568 | tf_op jit(solution)/shard_map/ppermute | solution.py:226
  87.3 8.2 %all-to-all-start.2 = ((f32[16,8,256]{2,1,0:T(8,128)}), f32[16,8,256]{2,1,0:T(8,128)S(1)}, u32[]{:S(2)}, u32[]{:S(2)}) async-start(f32[16,8,256]{2,1,0:T(8,128)} %broadcast_in_dim.6), calls=%async_computation.2 | async-start | bytes 262144 | tf_op jit(solution)/shard_map/all_to_all | solution.py:217
  95.5 7.2 %collective-permute-start.5 = (f32[64,256]{1,0:T(8,128)}, f32[64,256]{1,0:T(8,128)S(1)}, u32[]{:S(2)}, u32[]{:S(2)}) collective-permute-start(f32[64,256]{1,0:T(8,128)} %collective-permute-done.3), channel_id=1, source_target_pairs={{0,4},{1,5},{2,6},{3,7},{4,8},{5,9},{6,10},{7,11},{8,12},{9,13},{1... | collective-permute-start | bytes 196616 | tf_op jit(solution)/shard_map/ppermute | solution.py:226
  103.3 4.2 %all-to-all-done.2 = f32[16,8,256]{2,1,0:T(8,128)S(1)} async-done(((f32[16,8,256]{2,1,0:T(8,128)}), f32[16,8,256]{2,1,0:T(8,128)S(1)}, u32[]{:S(2)}, u32[]{:S(2)}) %all-to-all-start.2) | async-done | bytes 131104 | tf_op jit(solution)/shard_map/all_to_all | solution.py:217
  107.5 1.9 collective-permute-done.5
  109.4 1.6 pad_maximum_fusion
  110.9 5.6 %collective-permute-start.6 = (f32[256,256]{1,0:T(8,128)}, f32[256,256]{1,0:T(8,128)}, u32[]{:S(2)}, u32[]{:S(2)}) collective-permute-start(f32[256,256]{1,0:T(8,128)} %pad_maximum_fusion), channel_id=1, source_target_pairs={{0,2},{1,3},{2,0},{3,1},{4,6},{5,7},{6,4},{7,5},{8,10},{9,11},{10,... | collective-permute-start | bytes 786440 | tf_op jit(solution)/shard_map/ppermute | solution.py:209
  116.5 1.5 constant_dynamic-update-slice_fusion.3
  118.7 7.4 %all-to-all-start.3 = ((f32[32,8,256]{2,1,0:T(8,128)}), f32[32,8,256]{2,1,0:T(8,128)S(1)}, u32[]{:S(2)}, u32[]{:S(2)}) async-start(f32[32,8,256]{2,1,0:T(8,128)} %broadcast_in_dim.7), calls=%async_computation.3 | async-start | bytes 524288 | tf_op jit(solution)/shard_map/all_to_all | solution.py:217
  127.4 1.7 constant_dynamic-update-slice_fusion.own_ref
  129.1 6.0 %all-to-all-done.3 = f32[32,8,256]{2,1,0:T(8,128)S(1)} async-done(((f32[32,8,256]{2,1,0:T(8,128)}), f32[32,8,256]{2,1,0:T(8,128)S(1)}, u32[]{:S(2)}, u32[]{:S(2)}) %all-to-all-start.3) | async-done | bytes 262176 | tf_op jit(solution)/shard_map/all_to_all | solution.py:217
  135.1 5.2 %collective-permute-start.7 = (f32[512,256]{1,0:T(8,128)}, f32[512,256]{1,0:T(8,128)S(1)}, u32[]{:S(2)}, u32[]{:S(2)}) collective-permute-start(f32[512,256]{1,0:T(8,128)} %constant_dynamic-update-slice_fusion.own_ref), channel_id=1, source_target_pairs={{0,1},{1,0},{2,3},{3,2},{4,5},{5,4},{6,7},{7,6},{8,9},{9,8},{10,11... | collective-permute-start | bytes 1572872 | tf_op jit(solution)/shard_map/ppermute | solution.py:209
  140.3 63.6 %inverse_factor.1.inverse_ref = f32[256,256]{1,0:T(8,128)S(1)} custom-call(s32[37]{0:T(128)S(1)} %concatenate.10.refs_0_.where_ref, f32[256,256]{1,0:T(8,128)S(1)} %bitcast.8), custom_call_target="tpu_custom_call" | custom-call | flops 10000000000 | bytes 1048576 | tf_op jit(solution)/shard_map/inverse_factor/pallas_call | solution.py:260
  203.9 3.7 %basis_and_coeffs.1 = (f32[1024,256]{1,0:T(8,128)}, f32[16,8,1536]{2,1,0:T(8,128)S(1)}, f32[16,8,1536]{2,1,0:T(8,128)S(1)}) custom-call(s32[37]{0:T(128)S(1)} %concatenate.10.refs_0_.where_ref, f32[256,256]{1,0:T(8,128)S(1)} %inverse_factor.1.inverse_ref, f32[512,256]{1,0:T(8,128)S(1)} %copy-done.3, f32[512,256]{1,0:T(8,128)S(1)} %collective-permute-done.7.other_ref, ...), custom_call_target="tpu_custom_call" | custom-call | flops 1000000000 | bytes 1048576 | tf_op jit(solution)/shard_map/basis_and_coeffs/pallas_call | solution.py:270
  207.6 1.9 collective-permute-start.8
  209.5 2.3 collective-permute-done.8
  211.9 16.3 %all_to_all.26 = f32[16,8,1536]{2,1,0:T(8,128)S(1)} all-to-all(f32[16,8,1536]{2,1,0:T(8,128)S(1)} %add.35), channel_id=1, replica_groups=mesh['x'=4,'y'=4,'core'=2,'z3'=2,'z2'=2,'z1'=2,'z0'=2] {'x','y'}, dimensions={0} | all-to-all | bytes 1572864 | tf_op jit(solution)/shard_map/all_to_all | solution.py:217
  (25 shorter events, 6.1 us)
Async XLA Ops:
  1.4 1.4 copy-start
  2.8 1.2 copy-start.1
  4.0 1.1 copy-start.2
  7.3 18.2 %collective-permute-start.1 = (f32[256,256]{1,0:T(8,128)S(1)}, f32[256,256]{1,0:T(8,128)S(1)}, u32[]{:S(2)}, u32[]{:S(2)}) collective-permute-start(f32[256,256]{1,0:T(8,128)S(1)} %get-tuple-element.26), channel_id=1, source_target_pairs={{0,1},{1,0},{2,3},{3,2},{4,5},{5,4},{6,7},{7,6},{8,9},{9,8},{10,11... | collective-permute-start | bytes 786440 | tf_op jit(solution)/shard_map/ppermute | solution.py:209
  21.4 10.1 %collective-permute-start = (f32[256,256]{1,0:T(8,128)S(1)}, f32[256,256]{1,0:T(8,128)S(1)}, u32[]{:S(2)}, u32[]{:S(2)}) collective-permute-start(f32[256,256]{1,0:T(8,128)S(1)} %get-tuple-element.24), channel_id=1, source_target_pairs={{0,1},{1,0},{2,3},{3,2},{4,5},{5,4},{6,7},{7,6},{8,9},{9,8},{10,11... | collective-permute-start | bytes 786440 | tf_op jit(solution)/shard_map/ppermute | solution.py:209
  25.5 11.6 %collective-permute-start.2 = (f32[256,256]{1,0:T(8,128)S(1)}, f32[256,256]{1,0:T(8,128)S(1)}, u32[]{:S(2)}, u32[]{:S(2)}) collective-permute-start(f32[256,256]{1,0:T(8,128)S(1)} %add.33), channel_id=1, source_target_pairs={{0,2},{1,3},{2,0},{3,1},{4,6},{5,7},{6,4},{7,5},{8,10},{9,11},{10,... | collective-permute-start | bytes 786440 | tf_op jit(solution)/shard_map/ppermute | solution.py:209
  64.5 17.6 %all-to-all-start.1 = ((f32[32,8,256]{2,1,0:T(8,128)}), f32[32,8,256]{2,1,0:T(8,128)S(1)}, u32[]{:S(2)}, u32[]{:S(2)}) async-start(f32[32,8,256]{2,1,0:T(8,128)} %bitcast.6), calls=%async_computation.1 | async-start | bytes 524288 | tf_op jit(solution)/shard_map/all_to_all | solution.py:217
  72.9 13.8 %collective-permute-start.3 = (f32[64,256]{1,0:T(8,128)S(1)}, f32[64,256]{1,0:T(8,128)}, u32[]{:S(2)}, u32[]{:S(2)}) collective-permute-start(f32[64,256]{1,0:T(8,128)S(1)} %reduce_sum.36.share_ref), channel_id=1, source_target_pairs={{0,4},{1,5},{2,6},{3,7},{4,8},{5,9},{6,10},{7,11},{8,12},{9,13},{1... | collective-permute-start | bytes 196616 | tf_op jit(solution)/shard_map/ppermute | solution.py:226
  75.2 11.5 %collective-permute-start.4 = (f32[64,256]{1,0:T(8,128)S(1)}, f32[64,256]{1,0:T(8,128)S(1)}, u32[]{:S(2)}, u32[]{:S(2)}) collective-permute-start(f32[64,256]{1,0:T(8,128)S(1)} %reduce_sum.36.share_ref), channel_id=1, source_target_pairs={{0,12},{1,13},{2,14},{3,15},{4,0},{5,1},{6,2},{7,3},{8,4},{9,5},{1... | collective-permute-start | bytes 196616 | tf_op jit(solution)/shard_map/ppermute | solution.py:226
  87.3 20.2 %all-to-all-start.2 = ((f32[16,8,256]{2,1,0:T(8,128)}), f32[16,8,256]{2,1,0:T(8,128)S(1)}, u32[]{:S(2)}, u32[]{:S(2)}) async-start(f32[16,8,256]{2,1,0:T(8,128)} %broadcast_in_dim.6), calls=%async_computation.2 | async-start | bytes 262144 | tf_op jit(solution)/shard_map/all_to_all | solution.py:217
  95.5 13.9 %collective-permute-start.5 = (f32[64,256]{1,0:T(8,128)}, f32[64,256]{1,0:T(8,128)S(1)}, u32[]{:S(2)}, u32[]{:S(2)}) collective-permute-start(f32[64,256]{1,0:T(8,128)} %collective-permute-done.3), channel_id=1, source_target_pairs={{0,4},{1,5},{2,6},{3,7},{4,8},{5,9},{6,10},{7,11},{8,12},{9,13},{1... | collective-permute-start | bytes 196616 | tf_op jit(solution)/shard_map/ppermute | solution.py:226
  110.9 16.5 %collective-permute-start.6 = (f32[256,256]{1,0:T(8,128)}, f32[256,256]{1,0:T(8,128)}, u32[]{:S(2)}, u32[]{:S(2)}) collective-permute-start(f32[256,256]{1,0:T(8,128)} %pad_maximum_fusion), channel_id=1, source_target_pairs={{0,2},{1,3},{2,0},{3,1},{4,6},{5,7},{6,4},{7,5},{8,10},{9,11},{10,... | collective-permute-start | bytes 786440 | tf_op jit(solution)/shard_map/ppermute | solution.py:209
  118.7 16.4 %all-to-all-start.3 = ((f32[32,8,256]{2,1,0:T(8,128)}), f32[32,8,256]{2,1,0:T(8,128)S(1)}, u32[]{:S(2)}, u32[]{:S(2)}) async-start(f32[32,8,256]{2,1,0:T(8,128)} %broadcast_in_dim.7), calls=%async_computation.3 | async-start | bytes 524288 | tf_op jit(solution)/shard_map/all_to_all | solution.py:217
  135.1 68.7 %copy-start.3 = (f32[512,256]{1,0:T(8,128)S(1)}, f32[512,256]{1,0:T(8,128)}, u32[]{:S(2)}) copy-start(f32[512,256]{1,0:T(8,128)} %constant_dynamic-update-slice_fusion.own_ref) | copy-start | bytes 1572868
  135.1 68.7 %collective-permute-start.7 = (f32[512,256]{1,0:T(8,128)}, f32[512,256]{1,0:T(8,128)S(1)}, u32[]{:S(2)}, u32[]{:S(2)}) collective-permute-start(f32[512,256]{1,0:T(8,128)} %constant_dynamic-update-slice_fusion.own_ref), channel_id=1, source_target_pairs={{0,1},{1,0},{2,3},{3,2},{4,5},{5,4},{6,7},{7,6},{8,9},{9,8},{10,11... | collective-permute-start | bytes 1572872 | tf_op jit(solution)/shard_map/ppermute | solution.py:209
  207.6 4.2 %collective-permute-start.8 = (f32[16,8,1536]{2,1,0:T(8,128)S(1)}, f32[16,8,1536]{2,1,0:T(8,128)S(1)}, u32[]{:S(2)}, u32[]{:S(2)}) collective-permute-start(f32[16,8,1536]{2,1,0:T(8,128)S(1)} %get-tuple-element.37), channel_id=1, source_target_pairs={{0,16},{16,0},{1,17},{17,1},{2,18},{18,2},{3,19},{19,3},{4,20},{20... | collective-permute-start | bytes 2359304 | tf_op jit(solution)/shard_map/ppermute | solution.py:213

commit v5 on v4

--- a/solution.py
+++ b/solution.py
@@ -1,4 +1,3 @@
-import functools
 import math
 
 import jax
@@ -17,7 +16,7 @@
 LIGHT = FAR + ("z1", "z0")
 HIGHEST = lax.Precision.HIGHEST
 VMEM_LIMIT = 24 * 2**20
-COUNTS = 5
+COUNTS = 4
 
 
 def sine_coefficients():
@@ -166,28 +165,20 @@
 
 
 def basis_kernel(
-    where_ref, inverse_ref, own_ref, other_ref, tile_ref,
-    basis_ref, keep_ref, send_ref, half_ref, coeff_ref, *, share, places,
+    where_ref, inverse_ref, gathered_ref, tile_ref, basis_ref, keep_ref, send_ref, half_ref, coeff_ref
 ):
-    inverse = inverse_ref[...]
+    pairs, two, share = gathered_ref.shape[:3]
+    low, second, core = where_ref[1], where_ref[2], where_ref[3]
     rows = basis_ref.shape[0] // 4
-    groups = rows // share
-    own, core = where_ref[4], where_ref[3]
-
-    def partner(z, reach):
-        shift = core * reach
-        return (((z - shift + places) % places ^ reach) + shift) % places
-
-    for ref, owner, orders in ((own_ref, own, (3, 2)), (other_ref, partner(own, 1), (1, 0))):
-        basis = dot(ref[...], inverse, (1, 1), HIGHEST)
-        for i, order in enumerate(orders):
-            group = (owner if i == 0 else partner(owner, 2)) // (places // groups)
-            start = quarter_of(order, where_ref) * rows
-            for j, turn in enumerate((0, groups - 1, 1, 2)):
-                at = (group + turn) % groups * share
-                part = basis[i * rows + j * share : i * rows + (j + 1) * share, :]
-                basis_ref[pl.ds(pl.multiple_of(start + at, share), share), :] = part
-                half_ref[pl.ds(pl.multiple_of(order * rows + at, share), share), :] = part.astype(BF16)
+    basis = dot(gathered_ref[...].reshape(pairs * two * share, gathered_ref.shape[3]), inverse_ref[...], (1, 1), HIGHEST)
+    for k in range(pairs):
+        for j in range(two):
+            quarter = 2 * ((low + j) % 2) + k % 2
+            order = 2 - 2 * j + (second + j * core + k + 1) % 2
+            part = basis[(k * two + j) * share : (k * two + j + 1) * share, :]
+            at = k // 2 * share
+            basis_ref[pl.ds(pl.multiple_of(quarter * rows + at, share), share), :] = part
+            half_ref[pl.ds(pl.multiple_of(order * rows + at, share), share), :] = part.astype(BF16)
     coeffs = dot(half_ref[...], tile_ref[...], (0, 0))
     scale = 1.0 / jnp.sqrt(jnp.full((1, 1), total_of(where_ref), F32))
     coeff_ref[...] = (coeffs * scale).reshape(coeff_ref.shape)
@@ -221,17 +212,12 @@
     return each_to_each(jnp.broadcast_to(value, (lax.axis_size(axes), *value.shape)), axes)
 
 
-def around(value, turn):
-    places = lax.axis_size(LIGHT)
-    return lax.ppermute(value, LIGHT, [(z, (z + 4 * turn) % places) for z in range(places)])
-
-
 def on_device(tex_feat, light_feat, sketch, row_counts):
     capacity, width = tex_feat.shape[0], sketch.shape[1]
     lights = light_feat.shape[0]
     texels, places = lax.axis_size(TEXEL), lax.axis_size(LIGHT)
     share_rows = capacity // places
-    marks = [lax.axis_index(axes) for axes in (TEXEL, "z0", "z1", "core", LIGHT)]
+    marks = [lax.axis_index(axes) for axes in (TEXEL, "z0", "z1", "core")]
     where = jnp.concatenate([jnp.stack(marks).astype(jnp.int32), row_counts])
 
     inputs = (where, tex_feat, light_feat, sketch)
@@ -245,18 +231,13 @@
     quarter = part + staying + passed
     share = jnp.sum(each_to_each(quarter.reshape(places // 4, share_rows, width), FAR), axis=0)
 
-    before, behind = around(share, 1), around(share, -1)
+    both = jnp.stack([share, lax.ppermute(share, "z0", [(0, 1), (1, 0)])])
     gram = on_core(gram_kernel, jax.ShapeDtypeStruct((width, width), F32), [VMEM], "gram_part")(share)
+    gram, both = lax.optimization_barrier((gram, both))
+    gathered = lax.all_gather(both, FAR + ("z1",), axis=0)
     gram_rows = jnp.sum(each_to_each(gram.reshape(texels, width // texels, width), TEXEL), axis=0)
-    gram_rows, before, behind = lax.optimization_barrier((gram_rows, before, behind))
-    opposite = around(before, 1)
     gram_rows = jnp.sum(to_each(gram_rows, LIGHT), axis=0)
-    gram_rows, opposite = lax.optimization_barrier((gram_rows, opposite))
-    quarter = jnp.concatenate([share, before, behind, opposite])
-    own = jnp.concatenate([quarter, across(quarter, 2)])
     gram = to_each(gram_rows, TEXEL).reshape(width, width)
-    gram, own = lax.optimization_barrier((gram, own))
-    other = across(own, 1)
     inverse = on_core(
         inverse_kernel,
         jax.ShapeDtypeStruct((width, width), F32),
@@ -268,16 +249,16 @@
 
     lines, chips = width // texels, lax.axis_size(CHIP)
     basis, keep, send = on_core(
-        functools.partial(basis_kernel, share=share_rows, places=places),
+        basis_kernel,
         (
             jax.ShapeDtypeStruct((capacity, width), F32),
             jax.ShapeDtypeStruct((chips, lines, lights), F32),
             jax.ShapeDtypeStruct((chips, lines, lights), F32),
         ),
-        [SMEM] + [VMEM] * 4,
+        [SMEM] + [VMEM] * 3,
         "basis_and_coeffs",
         [pltpu.VMEM((capacity, width), BF16), pltpu.VMEM((texels, lines, lights), F32)],
-    )(where, inverse, own, other, tiles)
+    )(where, inverse, gathered, tiles)
     mine = keep + across_cores(send)
     coeffs = jnp.sum(each_to_each(mine, CHIP), axis=0)
     return basis, coeffs

time: 230 us -> 225 us (0.978)
  starting transfers between devices: 70.7 us -> 30.8 us
  blocking collectives: 42.5 us -> 76 us
  between operations: 0.83 us -> 14.2 us
  waiting for transfers between devices: 24.4 us -> 18.5 us
  local copies, waits for them, and re-layouts: 10.9 us -> 5.75 us
    all_to_all x2 -> x4, blocking collectives: 42.5 us -> 76 us  [each_to_each(): return lax.all_to_all(parts, axes, 0, 0, tiled=True)]
    all_to_all x3 -> x1, starting transfers between devices: 24 us -> 9.02 us  [each_to_each(): return lax.all_to_all(parts, axes, 0, 0, tiled=True)]
    ppermute x3 -> x1, starting transfers between devices: 16.4 us -> 1.92 us  [on_device(): both = jnp.stack([share, lax.ppermute(share, 'z0', [(0, 1), (1, 0)])])]
    ppermute x5 -> x3, starting transfers between devices: 28.4 us -> 17.7 us  [across(): lax.ppermute(value, ('core', *LIGHT), light_pairs(lax.axis_size(LIGHT), r...]
    ppermute x3 -> x1, waiting for transfers between devices: 6.36 us -> 1.97 us  [on_device(): both = jnp.stack([share, lax.ppermute(share, 'z0', [(0, 1), (1, 0)])])]
    unnamed x12 -> x8, local copies, waits for them, and re-layouts: 7.15 us -> 4.98 us
    all_to_all x3 -> x1, waiting for transfers between devices: 10.2 us -> 8.25 us  [each_to_each(): return lax.all_to_all(parts, axes, 0, 0, tiled=True)]
    ppermute x5 -> x3, waiting for transfers between devices: 5.6 us -> 5.57 us  [across(): lax.ppermute(value, ('core', *LIGHT), light_pairs(lax.axis_size(LIGHT), r...]
  transfers between devices with their start and end apart: 12 -> 7, of which waited for: 6 -> 4; matrix products, arithmetic and copies ran while one was open for 3% -> 0% of each run, Pallas kernels for 31% -> 31%
where the time goes in v5:
time: 225 us
  Pallas kernels  78 us (35%)
  blocking collectives  76 us (34%)
  starting transfers between devices  30.8 us (14%)
  waiting for transfers between devices  18.5 us (8%)
  between operations  14.2 us (6%)
  local copies, waits for them, and re-layouts  5.75 us (3%)
    all_to_all x4, blocking collectives, each_to_each(): return lax.all_to_all(parts, axes, 0, 0, tiled=True)  76 us
    pallas_call x1, Pallas kernels, on_device(): on_core(inverse_kernel, jax.ShapeDtypeStruct((width, width), F32), [SMEM,...  63.1 us
    ppermute x3, starting transfers between devices, across(): lax.ppermute(value, ('core', *LIGHT), light_pairs(lax.axis_size(LIGHT), r...  17.7 us
    all_to_all x1, starting transfers between devices, each_to_each(): return lax.all_to_all(parts, axes, 0, 0, tiled=True)  9.02 us
    pallas_call x4, Pallas kernels, tile_call(): on_core(lambda *refs: tile_kernel(*refs, order=order), (jax.ShapeDtypeStr...  8.57 us
    all_to_all x1, waiting for transfers between devices, each_to_each(): return lax.all_to_all(parts, axes, 0, 0, tiled=True)  8.25 us
    ppermute x3, waiting for transfers between devices, across(): lax.ppermute(value, ('core', *LIGHT), light_pairs(lax.axis_size(LIGHT), r...  5.57 us
    pallas_call x1, Pallas kernels, on_device(): on_core(basis_kernel, (jax.ShapeDtypeStruct((capacity, width), F32), jax....  5.25 us
  transfers between devices with their start and end apart: 7, of which 4 were waited for; matrix products, arithmetic and copies ran while one was open for 0% of the time, Pallas kernels for 31%

profile of v5, /device:TPU:1, one launch (start us, length us, event | category | flops | bytes accessed | tf_op | source)
XLA Modules:
  0.0 224.8 jit_solution(1896908135597489715)
XLA Ops:
  7.2 0.7 concatenate.3.refs_0_.where_ref
  7.9 1.4 copy-done
  9.3 1.2 copy-done.1
  10.5 1.1 copy-done.2
  11.7 2.1 tile_quarter.4
  13.8 11.9 %collective-permute-start.1 = (f32[256,256]{1,0:T(8,128)S(1)}, f32[256,256]{1,0:T(8,128)S(1)}, u32[]{:S(2)}, u32[]{:S(2)}) collective-permute-start(f32[256,256]{1,0:T(8,128)S(1)} %get-tuple-element.21), channel_id=1, source_target_pairs={{0,1},{1,0},{2,3},{3,2},{4,5},{5,4},{6,7},{7,6},{8,9},{9,8},{10,11... | collective-permute-start | bytes 786440 | tf_op jit(solution)/shard_map/ppermute | solution.py:200
  25.8 2.1 tile_quarter.5
  27.9 1.9 collective-permute-start
  29.8 2.1 tile_quarter.6
  32.0 3.8 %collective-permute-start.2 = (f32[256,256]{1,0:T(8,128)S(1)}, f32[256,256]{1,0:T(8,128)S(1)}, u32[]{:S(2)}, u32[]{:S(2)}) collective-permute-start(f32[256,256]{1,0:T(8,128)S(1)} %add.21), channel_id=1, source_target_pairs={{0,2},{1,3},{2,0},{3,1},{4,6},{5,7},{6,4},{7,5},{8,10},{9,11},{10,... | collective-permute-start | bytes 786440 | tf_op jit(solution)/shard_map/ppermute | solution.py:200
  35.9 2.1 tile_quarter.7
  38.0 5.6 %collective-permute-done.2 = f32[256,256]{1,0:T(8,128)S(1)} collective-permute-done((f32[256,256]{1,0:T(8,128)S(1)}, f32[256,256]{1,0:T(8,128)S(1)}, u32[]{:S(2)}, u32[]{:S(2)}) %collective-permute-start.2) | collective-permute-done | bytes 262176 | tf_op jit(solution)/shard_map/ppermute | solution.py:200
  43.6 0.1 add_add_fusion
  43.6 26.2 %all_to_all.25 = f32[4,64,256]{2,1,0:T(8,128)S(1)} all-to-all(f32[4,64,256]{2,1,0:T(8,128)S(1)} %bitcast.13), channel_id=1, replica_groups=mesh['x'=4,'y'=4,'core'=2,'z3'=2,'z2'=2,'z1'=2,'z0'=2] {'z3','z2'}, dimensions={0} | all-to-all | bytes 524288 | tf_op jit(solution)/shard_map/all_to_all | solution.py:208
  69.9 1.9 collective-permute-start.3
  71.8 1.1 gram_part.1
  72.9 2.0 collective-permute-done.3
  74.9 0.7 pad_maximum_fusion
  75.6 9.0 %all-to-all-start.1 = ((f32[32,8,256]{2,1,0:T(8,128)}), f32[32,8,256]{2,1,0:T(8,128)S(1)}, u32[]{:S(2)}, u32[]{:S(2)}) async-start(f32[32,8,256]{2,1,0:T(8,128)} %bitcast.7), calls=%async_computation.1 | async-start | bytes 524288 | tf_op jit(solution)/shard_map/all_to_all | solution.py:208
  84.6 0.0 all-gather.3.cloned.1.call-start
  84.6 0.7 all-gather.3.cloned.1.call-update
  85.3 8.3 %all-to-all-done.1 = f32[32,8,256]{2,1,0:T(8,128)S(1)} async-done(((f32[32,8,256]{2,1,0:T(8,128)}), f32[32,8,256]{2,1,0:T(8,128)S(1)}, u32[]{:S(2)}, u32[]{:S(2)}) %all-to-all-start.1) | async-done | bytes 262176 | tf_op jit(solution)/shard_map/all_to_all | solution.py:208
  93.6 18.4 %all_to_all.26 = f32[16,8,256]{2,1,0:T(8,128)S(1)} all-to-all(f32[16,8,256]{2,1,0:T(8,128)S(1)} %broadcast_in_dim.6), channel_id=1, replica_groups=mesh['x'=4,'y'=4,'core'=2,'z3'=2,'z2'=2,'z1'=2,'z0'=2] {'z3','z2','z1','..., dimensions={0} | all-to-all | bytes 262144 | tf_op jit(solution)/shard_map/all_to_all | solution.py:208
  112.1 14.9 %all_to_all.27 = f32[32,8,256]{2,1,0:T(8,128)S(1)} all-to-all(f32[32,8,256]{2,1,0:T(8,128)S(1)} %broadcast_in_dim.7), channel_id=1, replica_groups=mesh['x'=4,'y'=4,'core'=2,'z3'=2,'z2'=2,'z1'=2,'z0'=2] {'x','y','core'}, dimensions={0} | all-to-all | bytes 524288 | tf_op jit(solution)/shard_map/all_to_all | solution.py:208
  127.0 63.1 %inverse_factor.1.inverse_ref = f32[256,256]{1,0:T(8,128)S(1)} custom-call(s32[36]{0:T(128)S(1)} %concatenate.3.refs_0_.where_ref, f32[256,256]{1,0:T(8,128)S(1)} %bitcast.11), custom_call_target="tpu_custom_call" | custom-call | flops 10000000000 | bytes 1048576 | tf_op jit(solution)/shard_map/inverse_factor/pallas_call | solution.py:241
  190.2 1.2 copy-done.3
  191.4 5.2 %basis_and_coeffs.1 = (f32[1024,256]{1,0:T(8,128)}, f32[16,8,1536]{2,1,0:T(8,128)S(1)}, f32[16,8,1536]{2,1,0:T(8,128)S(1)}) custom-call(s32[36]{0:T(128)S(1)} %concatenate.3.refs_0_.where_ref, f32[256,256]{1,0:T(8,128)S(1)} %inverse_factor.1.inverse_ref, f32[8,2,64,256]{3,2,1,0:T(8,128)S(1)} %bitcast.10, bf16[1024,1536]{1,0:T(8,128)(2,1)S(1)} %get-tuple-element.24.tile_ref), custom_call_target="tpu_custom_call" | custom-call | flops 1000000000 | bytes 1048576 | tf_op jit(solution)/shard_map/basis_and_coeffs/pallas_call | solution.py:251
  196.6 2.1 collective-permute-start.4
  198.7 2.1 collective-permute-done.4
  200.8 0.1 add.23
  200.9 16.4 %all_to_all.28 = f32[16,8,1536]{2,1,0:T(8,128)S(1)} all-to-all(f32[16,8,1536]{2,1,0:T(8,128)S(1)} %add.23), channel_id=1, replica_groups=mesh['x'=4,'y'=4,'core'=2,'z3'=2,'z2'=2,'z1'=2,'z0'=2] {'x','y'}, dimensions={0} | all-to-all | bytes 1572864 | tf_op jit(solution)/shard_map/all_to_all | solution.py:208
  217.3 0.7 reduce_sum.39
  (13 shorter events, 0.2 us)
Async XLA Ops:
  7.9 1.4 copy-start
  9.3 1.2 copy-start.1
  10.5 1.1 copy-start.2
  13.8 18.2 %collective-permute-start.1 = (f32[256,256]{1,0:T(8,128)S(1)}, f32[256,256]{1,0:T(8,128)S(1)}, u32[]{:S(2)}, u32[]{:S(2)}) collective-permute-start(f32[256,256]{1,0:T(8,128)S(1)} %get-tuple-element.21), channel_id=1, source_target_pairs={{0,1},{1,0},{2,3},{3,2},{4,5},{5,4},{6,7},{7,6},{8,9},{9,8},{10,11... | collective-permute-start | bytes 786440 | tf_op jit(solution)/shard_map/ppermute | solution.py:200
  27.9 10.1 %collective-permute-start = (f32[256,256]{1,0:T(8,128)S(1)}, f32[256,256]{1,0:T(8,128)S(1)}, u32[]{:S(2)}, u32[]{:S(2)}) collective-permute-start(f32[256,256]{1,0:T(8,128)S(1)} %get-tuple-element.19), channel_id=1, source_target_pairs={{0,1},{1,0},{2,3},{3,2},{4,5},{5,4},{6,7},{7,6},{8,9},{9,8},{10,11... | collective-permute-start | bytes 786440 | tf_op jit(solution)/shard_map/ppermute | solution.py:200
  32.0 11.5 %collective-permute-start.2 = (f32[256,256]{1,0:T(8,128)S(1)}, f32[256,256]{1,0:T(8,128)S(1)}, u32[]{:S(2)}, u32[]{:S(2)}) collective-permute-start(f32[256,256]{1,0:T(8,128)S(1)} %add.21), channel_id=1, source_target_pairs={{0,2},{1,3},{2,0},{3,1},{4,6},{5,7},{6,4},{7,5},{8,10},{9,11},{10,... | collective-permute-start | bytes 786440 | tf_op jit(solution)/shard_map/ppermute | solution.py:200
  69.9 5.0 %collective-permute-start.3 = (f32[64,256]{1,0:T(8,128)S(1)}, f32[64,256]{1,0:T(8,128)S(1)}, u32[]{:S(2)}, u32[]{:S(2)}) collective-permute-start(f32[64,256]{1,0:T(8,128)S(1)} %reduce_sum.36.share_ref), channel_id=1, source_target_pairs={{0,1},{1,0},{2,3},{3,2},{4,5},{5,4},{6,7},{7,6},{8,9},{9,8},{10,11... | collective-permute-start | bytes 196616 | tf_op jit(solution)/shard_map/ppermute | solution.py:234
  75.6 18.0 %all-to-all-start.1 = ((f32[32,8,256]{2,1,0:T(8,128)}), f32[32,8,256]{2,1,0:T(8,128)S(1)}, u32[]{:S(2)}, u32[]{:S(2)}) async-start(f32[32,8,256]{2,1,0:T(8,128)} %bitcast.7), calls=%async_computation.1 | async-start | bytes 524288 | tf_op jit(solution)/shard_map/all_to_all | solution.py:208
  84.6 105.5 %all-gather.3.cloned.1.call-start = ((), (), s32[]{:S(2)}) async-start(), calls=%async_computation.5 | async-start | bytes 1179648 | tf_op jit(solution)/shard_map/all_gather | solution.py:237
  190.1 1.2 copy-start.3
  196.6 4.2 %collective-permute-start.4 = (f32[16,8,1536]{2,1,0:T(8,128)S(1)}, f32[16,8,1536]{2,1,0:T(8,128)S(1)}, u32[]{:S(2)}, u32[]{:S(2)}) collective-permute-start(f32[16,8,1536]{2,1,0:T(8,128)S(1)} %get-tuple-element.27), channel_id=1, source_target_pairs={{0,16},{16,0},{1,17},{17,1},{2,18},{18,2},{3,19},{19,3},{4,20},{20... | collective-permute-start | bytes 2359304 | tf_op jit(solution)/shard_map/ppermute | solution.py:204
Sparse Core Ops, SparseCore 0:
  87.5 48.2 all-gather.2

commit v6 on v5

--- a/solution.py
+++ b/solution.py
@@ -100,8 +100,9 @@
     )(where, tex, light, sketch, *tiles)
 
 
-def gram_kernel(share_ref, gram_ref):
-    gram_ref[...] = dot(share_ref[...], share_ref[...], (0, 0), HIGHEST)
+def gram_kernel(rows_ref, gram_ref):
+    rows = rows_ref[...].reshape(-1, rows_ref.shape[-1])
+    gram_ref[...] = dot(rows, rows, (0, 0), HIGHEST)
 
 
 def invert_factor(gram, y_ref, a_ref, w_ref):
@@ -160,27 +161,26 @@
     return total
 
 
-def inverse_kernel(where_ref, gram_ref, inverse_ref, a_ref, w_ref):
-    invert_factor(gram_ref[...] / total_of(where_ref), inverse_ref, a_ref, w_ref)
-
-
 def basis_kernel(
-    where_ref, inverse_ref, gathered_ref, tile_ref, basis_ref, keep_ref, send_ref, half_ref, coeff_ref
+    where_ref, gram_ref, own_ref, other_ref, tile_ref,
+    basis_ref, keep_ref, send_ref, inverse_ref, a_ref, w_ref, half_ref, coeff_ref,
 ):
-    pairs, two, share = gathered_ref.shape[:3]
+    total = total_of(where_ref)
+    invert_factor(gram_ref[...] / total, inverse_ref, a_ref, w_ref)
+    owners, share = own_ref.shape[:2]
     low, second, core = where_ref[1], where_ref[2], where_ref[3]
     rows = basis_ref.shape[0] // 4
-    basis = dot(gathered_ref[...].reshape(pairs * two * share, gathered_ref.shape[3]), inverse_ref[...], (1, 1), HIGHEST)
-    for k in range(pairs):
-        for j in range(two):
+    for j, ref in enumerate((own_ref, other_ref)):
+        basis = dot(ref[...].reshape(owners * share, ref.shape[2]), inverse_ref[...], (1, 1), HIGHEST)
+        for k in range(owners):
             quarter = 2 * ((low + j) % 2) + k % 2
             order = 2 - 2 * j + (second + j * core + k + 1) % 2
-            part = basis[(k * two + j) * share : (k * two + j + 1) * share, :]
+            part = basis[k * share : (k + 1) * share, :]
             at = k // 2 * share
             basis_ref[pl.ds(pl.multiple_of(quarter * rows + at, share), share), :] = part
             half_ref[pl.ds(pl.multiple_of(order * rows + at, share), share), :] = part.astype(BF16)
     coeffs = dot(half_ref[...], tile_ref[...], (0, 0))
-    scale = 1.0 / jnp.sqrt(jnp.full((1, 1), total_of(where_ref), F32))
+    scale = 1.0 / jnp.sqrt(jnp.full((1, 1), total, F32))
     coeff_ref[...] = (coeffs * scale).reshape(coeff_ref.shape)
     for i in range(keep_ref.shape[0]):
         keep_ref[i] = coeff_ref[2 * i + core]
@@ -223,29 +223,21 @@
     inputs = (where, tex_feat, light_feat, sketch)
     tiles, part = tile_call(0, *inputs)
     passing = across(part, 1)
+    tiles, turned = tile_call(2, *inputs, tiles)
     tiles, part = tile_call(1, *inputs, tiles)
     staying = across(part, 1)
-    tiles, part = tile_call(2, *inputs, tiles)
-    passed = across(part + passing, 2)
+    passed = across(turned + passing, 2)
     tiles, part = tile_call(3, *inputs, tiles)
     quarter = part + staying + passed
     share = jnp.sum(each_to_each(quarter.reshape(places // 4, share_rows, width), FAR), axis=0)
 
-    both = jnp.stack([share, lax.ppermute(share, "z0", [(0, 1), (1, 0)])])
-    gram = on_core(gram_kernel, jax.ShapeDtypeStruct((width, width), F32), [VMEM], "gram_part")(share)
-    gram, both = lax.optimization_barrier((gram, both))
-    gathered = lax.all_gather(both, FAR + ("z1",), axis=0)
+    own = lax.all_gather(share, FAR + ("z1",), axis=0)
+    gram = on_core(gram_kernel, jax.ShapeDtypeStruct((width, width), F32), [VMEM], "gram_part")(own)
+    other = across(own, 1)
     gram_rows = jnp.sum(each_to_each(gram.reshape(texels, width // texels, width), TEXEL), axis=0)
-    gram_rows = jnp.sum(to_each(gram_rows, LIGHT), axis=0)
+    gram_rows, other = lax.optimization_barrier((gram_rows, other))
+    gram_rows = gram_rows + lax.ppermute(gram_rows, "z0", [(0, 1), (1, 0)])
     gram = to_each(gram_rows, TEXEL).reshape(width, width)
-    inverse = on_core(
-        inverse_kernel,
-        jax.ShapeDtypeStruct((width, width), F32),
-        [SMEM, VMEM],
-        "inverse_factor",
-        [pltpu.VMEM((width, width), F32)] * 2,
-        10**10,
-    )(where, gram)
 
     lines, chips = width // texels, lax.axis_size(CHIP)
     basis, keep, send = on_core(
@@ -255,10 +247,11 @@
             jax.ShapeDtypeStruct((chips, lines, lights), F32),
             jax.ShapeDtypeStruct((chips, lines, lights), F32),
         ),
-        [SMEM] + [VMEM] * 3,
+        [SMEM] + [VMEM] * 4,
         "basis_and_coeffs",
-        [pltpu.VMEM((capacity, width), BF16), pltpu.VMEM((texels, lines, lights), F32)],
-    )(where, inverse, gathered, tiles)
+        [pltpu.VMEM((width, width), F32)] * 3
+        + [pltpu.VMEM((capacity, width), BF16), pltpu.VMEM((texels, lines, lights), F32)],
+    )(where, gram, own, other, tiles)
     mine = keep + across_cores(send)
     coeffs = jnp.sum(each_to_each(mine, CHIP), axis=0)
     return basis, coeffs

time: 225 us -> 222 us (0.987)
  blocking collectives: 76 us -> 106 us
  between operations: 14.2 us -> 0.75 us
  waiting for transfers between devices: 18.5 us -> 9.86 us
  starting transfers between devices: 30.8 us -> 24 us
  Pallas kernels: 78 us -> 75.6 us
    pallas_call x1 -> x0, Pallas kernels: 63.1 us -> none  [on_device(): on_core(inverse_kernel, jax.ShapeDtypeStruct((width, width), F32), [SMEM,...]
    pallas_call x1, Pallas kernels: 5.25 us -> 65.3 us  [on_device(): on_core(basis_kernel, (jax.ShapeDtypeStruct((capacity, width), F32), jax....]
    all_gather x0 -> x1, blocking collectives: none -> 25.5 us  [on_device(): own = lax.all_gather(share, FAR + ('z1',), axis=0)]
    all_to_all x1 -> x0, starting transfers between devices: 9.02 us -> none  [each_to_each(): return lax.all_to_all(parts, axes, 0, 0, tiled=True)]
    all_to_all x1 -> x0, waiting for transfers between devices: 8.25 us -> none  [each_to_each(): return lax.all_to_all(parts, axes, 0, 0, tiled=True)]
    all_to_all x4, blocking collectives: 76 us -> 80.6 us  [each_to_each(): return lax.all_to_all(parts, axes, 0, 0, tiled=True)]
    ppermute x3 -> x4, starting transfers between devices: 17.7 us -> 20 us  [across(): lax.ppermute(value, ('core', *LIGHT), light_pairs(lax.axis_size(LIGHT), r...]
    unnamed x8 -> x6, local copies, waits for them, and re-layouts: 4.98 us -> 3.77 us
  transfers between devices with their start and end apart: 7 -> 6, of which waited for: 4 -> 4; matrix products, arithmetic and copies ran while one was open for 0% -> 0% of each run, Pallas kernels for 31% -> 4%
where the time goes in v6:
time: 222 us
  blocking collectives  106 us (48%)
  Pallas kernels  75.6 us (34%)
  starting transfers between devices  24 us (11%)
  waiting for transfers between devices  9.86 us (4%)
  local copies, waits for them, and re-layouts  4.52 us (2%)
    all_to_all x4, blocking collectives, each_to_each(): return lax.all_to_all(parts, axes, 0, 0, tiled=True)  80.6 us
    pallas_call x1, Pallas kernels, on_device(): on_core(basis_kernel, (jax.ShapeDtypeStruct((capacity, width), F32), jax....  65.3 us
    all_gather x1, blocking collectives, on_device(): own = lax.all_gather(share, FAR + ('z1',), axis=0)  25.5 us
    ppermute x4, starting transfers between devices, across(): lax.ppermute(value, ('core', *LIGHT), light_pairs(lax.axis_size(LIGHT), r...  20 us
    pallas_call x4, Pallas kernels, tile_call(): on_core(lambda *refs: tile_kernel(*refs, order=order), (jax.ShapeDtypeStr...  8.54 us
    ppermute x4, waiting for transfers between devices, across(): lax.ppermute(value, ('core', *LIGHT), light_pairs(lax.axis_size(LIGHT), r...  5.32 us
  transfers between devices with their start and end apart: 6, of which 4 were waited for; matrix products, arithmetic and copies ran while one was open for 0% of the time, Pallas kernels for 4%

profile of v6, /device:TPU:1, one launch (start us, length us, event | category | flops | bytes accessed | tf_op | source)
XLA Modules:
  0.0 221.8 jit_solution(12171081748320059182)
XLA Ops:
  0.6 0.7 concatenate.3.refs_0_.where_ref
  1.4 0.0 copy-start
  1.4 1.4 copy-done
  2.8 0.0 copy-start.1
  2.8 1.2 copy-done.1
  4.0 1.1 copy-done.2
  5.1 2.1 tile_quarter.4
  7.3 11.9 %collective-permute-start.1 = (f32[256,256]{1,0:T(8,128)S(1)}, f32[256,256]{1,0:T(8,128)S(1)}, u32[]{:S(2)}, u32[]{:S(2)}) collective-permute-start(f32[256,256]{1,0:T(8,128)S(1)} %get-tuple-element.21), channel_id=1, source_target_pairs={{0,1},{1,0},{2,3},{3,2},{4,5},{5,4},{6,7},{7,6},{8,9},{9,8},{10,11... | collective-permute-start | bytes 786440 | tf_op jit(solution)/shard_map/ppermute | solution.py:200
  19.2 2.1 tile_quarter.5
  21.4 2.1 tile_quarter.6
  23.5 1.9 collective-permute-start
  25.4 0.0 collective-permute-done.1
  25.5 3.8 %collective-permute-start.2 = (f32[256,256]{1,0:T(8,128)S(1)}, f32[256,256]{1,0:T(8,128)S(1)}, u32[]{:S(2)}, u32[]{:S(2)}) collective-permute-start(f32[256,256]{1,0:T(8,128)S(1)} %add.24), channel_id=1, source_target_pairs={{0,2},{1,3},{2,0},{3,1},{4,6},{5,7},{6,4},{7,5},{8,10},{9,11},{10,... | collective-permute-start | bytes 786440 | tf_op jit(solution)/shard_map/ppermute | solution.py:200
  29.3 2.1 tile_quarter.7
  31.4 0.5 collective-permute-done
  32.0 4.8 %collective-permute-done.2 = f32[256,256]{1,0:T(8,128)S(1)} collective-permute-done((f32[256,256]{1,0:T(8,128)S(1)}, f32[256,256]{1,0:T(8,128)S(1)}, u32[]{:S(2)}, u32[]{:S(2)}) %collective-permute-start.2) | collective-permute-done | bytes 262176 | tf_op jit(solution)/shard_map/ppermute | solution.py:200
  36.7 0.1 add_add_fusion
  36.8 26.9 %all_to_all.20 = f32[4,64,256]{2,1,0:T(8,128)S(1)} all-to-all(f32[4,64,256]{2,1,0:T(8,128)S(1)} %bitcast.10), channel_id=1, replica_groups=mesh['x'=4,'y'=4,'core'=2,'z3'=2,'z2'=2,'z1'=2,'z0'=2] {'z3','z2'}, dimensions={0} | all-to-all | bytes 524288 | tf_op jit(solution)/shard_map/all_to_all | solution.py:208
  63.7 25.5 %all-gather = f32[512,256]{1,0:T(8,128)} all-gather(f32[64,256]{1,0:T(8,128)S(1)} %reduce_sum.27), channel_id=2, replica_groups=mesh['x'=4,'y'=4,'core'=2,'z3'=2,'z2'=2,'z1'=2,'z0'=2] {'z3','z2','z1'}, dimensions={0}, use_global_device_ids=true | all-gather | bytes 589824 | tf_op jit(solution)/shard_map/all_gather | solution.py:234
  89.2 2.3 %collective-permute-start.3 = (f32[8,64,256]{2,1,0:T(8,128)}, f32[8,64,256]{2,1,0:T(8,128)}, u32[]{:S(2)}, u32[]{:S(2)}) collective-permute-start(f32[8,64,256]{2,1,0:T(8,128)} %bitcast.5.rows_ref.own_ref), channel_id=1, source_target_pairs={{0,1},{1,0},{2,3},{3,2},{4,5},{5,4},{6,7},{7,6},{8,9},{9,8},{10,11... | collective-permute-start | bytes 1572872 | tf_op jit(solution)/shard_map/ppermute | solution.py:200
  91.6 1.8 gram_part.1
  93.4 24.0 %all_to_all.21 = f32[32,8,256]{2,1,0:T(8,128)S(1)} all-to-all(f32[32,8,256]{2,1,0:T(8,128)S(1)} %bitcast.9), channel_id=1, replica_groups=mesh['x'=4,'y'=4,'core'=2,'z3'=2,'z2'=2,'z1'=2,'z0'=2] {'x','y','core'}, dimensions={0} | all-to-all | bytes 524288 | tf_op jit(solution)/shard_map/all_to_all | solution.py:208
  117.4 0.0 collective-permute-done.3.other_ref
  117.4 1.9 collective-permute-start.4
  119.3 2.5 %collective-permute-done.4 = f32[8,256]{1,0:T(8,128)S(1)} collective-permute-done((f32[8,256]{1,0:T(8,128)S(1)}, f32[8,256]{1,0:T(8,128)S(1)}, u32[]{:S(2)}, u32[]{:S(2)}) %collective-permute-start.4) | collective-permute-done | bytes 8224 | tf_op jit(solution)/shard_map/ppermute | solution.py:239
  121.8 13.6 %all_to_all.22 = f32[32,8,256]{2,1,0:T(8,128)S(1)} all-to-all(f32[32,8,256]{2,1,0:T(8,128)S(1)} %broadcast_in_dim.3), channel_id=1, replica_groups=mesh['x'=4,'y'=4,'core'=2,'z3'=2,'z2'=2,'z1'=2,'z0'=2] {'x','y','core'}, dimensions={0} | all-to-all | bytes 524288 | tf_op jit(solution)/shard_map/all_to_all | solution.py:208
  135.4 65.3 %basis_and_coeffs.1 = (f32[1024,256]{1,0:T(8,128)}, f32[16,8,1536]{2,1,0:T(8,128)S(1)}, f32[16,8,1536]{2,1,0:T(8,128)S(1)}) custom-call(s32[36]{0:T(128)S(1)} %concatenate.3.refs_0_.where_ref, f32[256,256]{1,0:T(8,128)S(1)} %bitcast.8, f32[8,64,256]{2,1,0:T(8,128)} %bitcast.5.rows_ref.own_ref, f32[8,64,256]{2,1,0:T(8,128)} %collective-permute-done.3.other_ref, ...), custom_call_target="tpu_custom_call" | custom-call | flops 1000000000 | bytes 1048576 | tf_op jit(solution)/shard_map/basis_and_coeffs/pallas_call | solution.py:243
  200.7 2.1 collective-permute-start.5
  202.8 2.1 collective-permute-done.5
  204.9 0.1 add.27
  205.0 16.1 %all_to_all.23 = f32[16,8,1536]{2,1,0:T(8,128)S(1)} all-to-all(f32[16,8,1536]{2,1,0:T(8,128)S(1)} %add.27), channel_id=1, replica_groups=mesh['x'=4,'y'=4,'core'=2,'z3'=2,'z2'=2,'z1'=2,'z0'=2] {'x','y'}, dimensions={0} | all-to-all | bytes 1572864 | tf_op jit(solution)/shard_map/all_to_all | solution.py:208
  221.1 0.7 reduce_sum.29
  (6 shorter events, 0.1 us)
Async XLA Ops:
  1.4 1.4 copy-start
  2.8 1.2 copy-start.1
  4.0 1.1 copy-start.2
  7.3 18.2 %collective-permute-start.1 = (f32[256,256]{1,0:T(8,128)S(1)}, f32[256,256]{1,0:T(8,128)S(1)}, u32[]{:S(2)}, u32[]{:S(2)}) collective-permute-start(f32[256,256]{1,0:T(8,128)S(1)} %get-tuple-element.21), channel_id=1, source_target_pairs={{0,1},{1,0},{2,3},{3,2},{4,5},{5,4},{6,7},{7,6},{8,9},{9,8},{10,11... | collective-permute-start | bytes 786440 | tf_op jit(solution)/shard_map/ppermute | solution.py:200
  23.5 8.5 %collective-permute-start = (f32[256,256]{1,0:T(8,128)S(1)}, f32[256,256]{1,0:T(8,128)S(1)}, u32[]{:S(2)}, u32[]{:S(2)}) collective-permute-start(f32[256,256]{1,0:T(8,128)S(1)} %get-tuple-element.19), channel_id=1, source_target_pairs={{0,1},{1,0},{2,3},{3,2},{4,5},{5,4},{6,7},{7,6},{8,9},{9,8},{10,11... | collective-permute-start | bytes 786440 | tf_op jit(solution)/shard_map/ppermute | solution.py:200
  25.5 11.3 %collective-permute-start.2 = (f32[256,256]{1,0:T(8,128)S(1)}, f32[256,256]{1,0:T(8,128)S(1)}, u32[]{:S(2)}, u32[]{:S(2)}) collective-permute-start(f32[256,256]{1,0:T(8,128)S(1)} %add.24), channel_id=1, source_target_pairs={{0,2},{1,3},{2,0},{3,1},{4,6},{5,7},{6,4},{7,5},{8,10},{9,11},{10,... | collective-permute-start | bytes 786440 | tf_op jit(solution)/shard_map/ppermute | solution.py:200
  89.2 28.2 %collective-permute-start.3 = (f32[8,64,256]{2,1,0:T(8,128)}, f32[8,64,256]{2,1,0:T(8,128)}, u32[]{:S(2)}, u32[]{:S(2)}) collective-permute-start(f32[8,64,256]{2,1,0:T(8,128)} %bitcast.5.rows_ref.own_ref), channel_id=1, source_target_pairs={{0,1},{1,0},{2,3},{3,2},{4,5},{5,4},{6,7},{7,6},{8,9},{9,8},{10,11... | collective-permute-start | bytes 1572872 | tf_op jit(solution)/shard_map/ppermute | solution.py:200
  117.4 4.4 %collective-permute-start.4 = (f32[8,256]{1,0:T(8,128)S(1)}, f32[8,256]{1,0:T(8,128)S(1)}, u32[]{:S(2)}, u32[]{:S(2)}) collective-permute-start(f32[8,256]{1,0:T(8,128)S(1)} %reduce_sum.28), channel_id=1, source_target_pairs={{0,1},{1,0},{2,3},{3,2},{4,5},{5,4},{6,7},{7,6},{8,9},{9,8},{10,11... | collective-permute-start | bytes 24584 | tf_op jit(solution)/shard_map/ppermute | solution.py:239
  200.7 4.2 %collective-permute-start.5 = (f32[16,8,1536]{2,1,0:T(8,128)S(1)}, f32[16,8,1536]{2,1,0:T(8,128)S(1)}, u32[]{:S(2)}, u32[]{:S(2)}) collective-permute-start(f32[16,8,1536]{2,1,0:T(8,128)S(1)} %get-tuple-element.27), channel_id=1, source_target_pairs={{0,16},{16,0},{1,17},{17,1},{2,18},{18,2},{3,19},{19,3},{4,20},{20... | collective-permute-start | bytes 2359304 | tf_op jit(solution)/shard_map/ppermute | solution.py:204

commit v7 on v6

--- a/solution.py
+++ b/solution.py
@@ -1,3 +1,4 @@
+import functools
 import math
 
 import jax
@@ -16,7 +17,6 @@
 LIGHT = FAR + ("z1", "z0")
 HIGHEST = lax.Precision.HIGHEST
 VMEM_LIMIT = 24 * 2**20
-COUNTS = 4
 
 
 def sine_coefficients():
@@ -50,59 +50,54 @@
 
 
 VMEM = pl.BlockSpec(memory_space=pltpu.VMEM)
-SMEM = pl.BlockSpec(memory_space=pltpu.SMEM)
-
-
-def on_core(kernel, out_shape, in_specs, name, scratch=(), flops=10**9, aliases=None):
-    return pl.pallas_call(
+
+
+def on_core(kernel, out_shape, name, scratch=(), flops=10**9, aliases=None):
+    call = lambda *operands: pl.pallas_call(
         kernel,
         out_shape=out_shape,
-        in_specs=in_specs,
+        in_specs=[VMEM] * len(operands),
         out_specs=jax.tree.map(lambda _: VMEM, out_shape),
         scratch_shapes=scratch,
         input_output_aliases=aliases or {},
         compiler_params=pltpu.CompilerParams(vmem_limit_bytes=VMEM_LIMIT),
         cost_estimate=pl.CostEstimate(flops=flops, bytes_accessed=2**20, transcendentals=0),
         name=name,
-    )
-
-
-def quarter_of(order, where):
-    low, second, core = where[1], where[2], where[3]
+    )(*operands)
+    return call
+
+
+def quarter_of(order):
+    low, second, core = (lax.axis_index(axis) for axis in ("z0", "z1", "core"))
     if order < 2:
         return 2 * (1 - low) + (second + core + 1 - order) % 2
     return 2 * low + (second + 1 - (order - 2)) % 2
 
 
-def tile_kernel(where_ref, tex_ref, light_ref, sketch_ref, *refs, order, step=128):
+def tile_kernel(tex_ref, light_ref, sketch_ref, *refs, order, step=128):
     tile_ref, part_ref = refs[-2:]
     rows = part_ref.shape[0]
-    first = quarter_of(order, where_ref) * rows
-    count = where_ref[COUNTS + where_ref[0]]
+    first = quarter_of(order) * rows
     for at in range(0, rows, step):
         tex = tex_ref[pl.ds(pl.multiple_of(first + at, step), step), :]
         tile = sine(dot(tex, light_ref[...], (1, 1))).astype(BF16)
         tile_ref[order * rows + at : order * rows + at + step, :] = tile
-        part = dot(tile, sketch_ref[...], (1, 0))
-        row = first + at + lax.broadcasted_iota(jnp.int32, part.shape, 0)
-        part_ref[at : at + step, :] = jnp.where(row < count, part, 0.0)
-
-
-def tile_call(order, where, tex, light, sketch, *tiles):
+        part_ref[at : at + step, :] = dot(tile, sketch_ref[...], (1, 0))
+
+
+def tile_call(order, tex, light, sketch, *tiles):
     rows, lights, width = tex.shape[0] // 4, light.shape[0], sketch.shape[1]
     return on_core(
-        lambda *refs: tile_kernel(*refs, order=order),
+        functools.partial(tile_kernel, order=order),
         (jax.ShapeDtypeStruct((tex.shape[0], lights), BF16), jax.ShapeDtypeStruct((rows, width), F32)),
-        [SMEM] + [VMEM] * (3 + len(tiles)),
         "tile_quarter",
         flops=2 * rows * lights * (tex.shape[1] + width),
-        aliases={4: 0} if tiles else None,
-    )(where, tex, light, sketch, *tiles)
+        aliases={3: 0} if tiles else None,
+    )(tex, light, sketch, *tiles)
 
 
 def gram_kernel(rows_ref, gram_ref):
-    rows = rows_ref[...].reshape(-1, rows_ref.shape[-1])
-    gram_ref[...] = dot(rows, rows, (0, 0), HIGHEST)
+    gram_ref[...] = dot(rows_ref[...], rows_ref[...], (0, 0), HIGHEST)
 
 
 def invert_factor(gram, y_ref, a_ref, w_ref):
@@ -154,34 +149,22 @@
         lax.fori_loop(0, size, eliminate, 0)
 
 
-def total_of(where_ref):
-    total = F32(0)
-    for i in range(COUNTS, where_ref.shape[0]):
-        total = total + where_ref[i].astype(F32)
-    return total
-
-
 def basis_kernel(
-    where_ref, gram_ref, own_ref, other_ref, tile_ref,
+    total_ref, gram_ref, own_ref, other_ref, tile_ref,
     basis_ref, keep_ref, send_ref, inverse_ref, a_ref, w_ref, half_ref, coeff_ref,
 ):
-    total = total_of(where_ref)
+    total = total_ref[...]
     invert_factor(gram_ref[...] / total, inverse_ref, a_ref, w_ref)
-    owners, share = own_ref.shape[:2]
-    low, second, core = where_ref[1], where_ref[2], where_ref[3]
     rows = basis_ref.shape[0] // 4
-    for j, ref in enumerate((own_ref, other_ref)):
-        basis = dot(ref[...].reshape(owners * share, ref.shape[2]), inverse_ref[...], (1, 1), HIGHEST)
-        for k in range(owners):
-            quarter = 2 * ((low + j) % 2) + k % 2
-            order = 2 - 2 * j + (second + j * core + k + 1) % 2
-            part = basis[k * share : (k + 1) * share, :]
-            at = k // 2 * share
-            basis_ref[pl.ds(pl.multiple_of(quarter * rows + at, share), share), :] = part
-            half_ref[pl.ds(pl.multiple_of(order * rows + at, share), share), :] = part.astype(BF16)
+    for ref, orders in ((own_ref, (3, 2)), (other_ref, (1, 0))):
+        basis = dot(ref[...], inverse_ref[...], (1, 1), HIGHEST)
+        for i, order in enumerate(orders):
+            part = basis[i * rows : (i + 1) * rows, :]
+            basis_ref[pl.ds(pl.multiple_of(quarter_of(order) * rows, rows), rows), :] = part
+            half_ref[order * rows : (order + 1) * rows, :] = part.astype(BF16)
     coeffs = dot(half_ref[...], tile_ref[...], (0, 0))
-    scale = 1.0 / jnp.sqrt(jnp.full((1, 1), total, F32))
-    coeff_ref[...] = (coeffs * scale).reshape(coeff_ref.shape)
+    coeff_ref[...] = (coeffs * (1.0 / jnp.sqrt(total))).reshape(coeff_ref.shape)
+    core = lax.axis_index("core")
     for i in range(keep_ref.shape[0]):
         keep_ref[i] = coeff_ref[2 * i + core]
         send_ref[i] = coeff_ref[2 * i + 1 - core]
@@ -217,26 +200,30 @@
     lights = light_feat.shape[0]
     texels, places = lax.axis_size(TEXEL), lax.axis_size(LIGHT)
     share_rows = capacity // places
-    marks = [lax.axis_index(axes) for axes in (TEXEL, "z0", "z1", "core")]
-    where = jnp.concatenate([jnp.stack(marks).astype(jnp.int32), row_counts])
-
-    inputs = (where, tex_feat, light_feat, sketch)
+    total = jnp.sum(row_counts).astype(F32).reshape(1, 1)
+    used = row_counts[lax.axis_index(TEXEL)] - quarter_of(3) * (capacity // 4) - lax.axis_index(FAR) * share_rows
+
+    inputs = (tex_feat, light_feat, sketch)
     tiles, part = tile_call(0, *inputs)
     passing = across(part, 1)
-    tiles, turned = tile_call(2, *inputs, tiles)
+    tiles, part = tile_call(2, *inputs, tiles)
+    tiles, passing = lax.optimization_barrier((tiles, passing))
+    passed = across(part + passing, 2)
     tiles, part = tile_call(1, *inputs, tiles)
     staying = across(part, 1)
-    passed = across(turned + passing, 2)
     tiles, part = tile_call(3, *inputs, tiles)
     quarter = part + staying + passed
     share = jnp.sum(each_to_each(quarter.reshape(places // 4, share_rows, width), FAR), axis=0)
-
-    own = lax.all_gather(share, FAR + ("z1",), axis=0)
-    gram = on_core(gram_kernel, jax.ShapeDtypeStruct((width, width), F32), [VMEM], "gram_part")(own)
+    share = jnp.where(lax.broadcasted_iota(jnp.int32, share.shape, 0) < used, share, 0.0)
+
+    quarter = lax.all_gather(share, FAR, axis=0, tiled=True)
+    near = across(quarter, 2)
+    gram = on_core(gram_kernel, jax.ShapeDtypeStruct((width, width), F32), "gram_part")(quarter)
+    gram_rows = jnp.sum(each_to_each(gram.reshape(texels, width // texels, width), TEXEL), axis=0)
+    gram_rows, near = lax.optimization_barrier((gram_rows, near))
+    own = jnp.concatenate([quarter, near])
     other = across(own, 1)
-    gram_rows = jnp.sum(each_to_each(gram.reshape(texels, width // texels, width), TEXEL), axis=0)
-    gram_rows, other = lax.optimization_barrier((gram_rows, other))
-    gram_rows = gram_rows + lax.ppermute(gram_rows, "z0", [(0, 1), (1, 0)])
+    gram_rows = jnp.sum(to_each(gram_rows, ("z1", "z0")), axis=0)
     gram = to_each(gram_rows, TEXEL).reshape(width, width)
 
     lines, chips = width // texels, lax.axis_size(CHIP)
@@ -247,11 +234,10 @@
             jax.ShapeDtypeStruct((chips, lines, lights), F32),
             jax.ShapeDtypeStruct((chips, lines, lights), F32),
         ),
-        [SMEM] + [VMEM] * 4,
         "basis_and_coeffs",
         [pltpu.VMEM((width, width), F32)] * 3
         + [pltpu.VMEM((capacity, width), BF16), pltpu.VMEM((texels, lines, lights), F32)],
-    )(where, gram, own, other, tiles)
+    )(total, gram, own, other, tiles)
     mine = keep + across_cores(send)
     coeffs = jnp.sum(each_to_each(mine, CHIP), axis=0)
     return basis, coeffs

time: 222 us -> 224 us (level)
  blocking collectives: 106 us -> 39.2 us
  starting transfers between devices: 24 us -> 60 us
  waiting for transfers between devices: 9.86 us -> 37.2 us
  local copies, waits for them, and re-layouts: 4.52 us -> 9.22 us
  Pallas kernels: 75.6 us -> 71.7 us
  other arithmetic: 0.91 us -> 3.26 us
    all_to_all x4 -> x2, blocking collectives: 80.6 us -> 23.1 us  [each_to_each(): return lax.all_to_all(parts, axes, 0, 0, tiled=True)]
    all_to_all x0 -> x3, waiting for transfers between devices: none -> 28.6 us  [each_to_each(): return lax.all_to_all(parts, axes, 0, 0, tiled=True)]
    all_to_all x0 -> x3, starting transfers between devices: none -> 27.1 us  [each_to_each(): return lax.all_to_all(parts, axes, 0, 0, tiled=True)]
    ppermute x4 -> x5, starting transfers between devices: 20 us -> 30.8 us  [across(): lax.ppermute(value, ('core', *LIGHT), light_pairs(lax.axis_size(LIGHT), r...]
    all_gather x1, blocking collectives: 25.5 us -> 16.2 us  [on_device(): quarter = lax.all_gather(share, FAR, axis=0, tiled=True)]
    pallas_call x6, Pallas kernels: 75.6 us -> 71.7 us  [on_core(): pl.pallas_call(kernel, out_shape=out_shape, in_specs=[VMEM] * len(operand...]
    ppermute x1 -> x0, waiting for transfers between devices: 2.47 us -> none  [on_device(): gram_rows = gram_rows + lax.ppermute(gram_rows, 'z0', [(0, 1), (1, 0)])]
    unnamed x6 -> x13, local copies, waits for them, and re-layouts: 3.77 us -> 6.23 us
  transfers between devices with their start and end apart: 6 -> 9, of which waited for: 4 -> 7; matrix products, arithmetic and copies ran while one was open for 0% -> 2% of each run, Pallas kernels for 4% -> 2%
where the time goes in v7:
time: 224 us; the launch traced here: 223 us
  Pallas kernels  71.7 us (32%)
  starting transfers between devices  60 us (27%)
  blocking collectives  39.2 us (18%)
  waiting for transfers between devices  37.2 us (17%)
  local copies, waits for them, and re-layouts  9.22 us (4%)
  other arithmetic  3.26 us (1%)
    pallas_call x6, Pallas kernels, on_core(): pl.pallas_call(kernel, out_shape=out_shape, in_specs=[VMEM] * len(operand...  71.7 us
    ppermute x5, starting transfers between devices, across(): lax.ppermute(value, ('core', *LIGHT), light_pairs(lax.axis_size(LIGHT), r...  30.8 us
    all_to_all x3, waiting for transfers between devices, each_to_each(): return lax.all_to_all(parts, axes, 0, 0, tiled=True)  28.6 us
    all_to_all x3, starting transfers between devices, each_to_each(): return lax.all_to_all(parts, axes, 0, 0, tiled=True)  27.1 us
    all_to_all x2, blocking collectives, each_to_each(): return lax.all_to_all(parts, axes, 0, 0, tiled=True)  23.1 us
    all_gather x1, blocking collectives, on_device(): quarter = lax.all_gather(share, FAR, axis=0, tiled=True)  16.2 us
    ppermute x5, waiting for transfers between devices, across(): lax.ppermute(value, ('core', *LIGHT), light_pairs(lax.axis_size(LIGHT), r...  6.55 us
    unnamed x13, local copies, waits for them, and re-layouts  6.23 us
  transfers between devices with their start and end apart: 9, of which 7 were waited for; matrix products, arithmetic and copies ran while one was open for 2% of the time, Pallas kernels for 2%

profile of v7, /device:TPU:1, one launch (start us, length us, event | category | flops | bytes accessed | tf_op | source)
XLA Modules:
  0.0 222.7 jit_solution(11866704299659177557)
XLA Ops:
  0.6 1.4 copy-done
  2.0 1.2 copy-done.1
  3.3 1.1 copy-done.2
  4.4 1.6 tile_quarter.4
  6.0 11.9 %collective-permute-start = (f32[256,256]{1,0:T(8,128)S(1)}, f32[256,256]{1,0:T(8,128)S(1)}, u32[]{:S(2)}, u32[]{:S(2)}) collective-permute-start(f32[256,256]{1,0:T(8,128)S(1)} %get-tuple-element.19), channel_id=1, source_target_pairs={{0,1},{1,0},{2,3},{3,2},{4,5},{5,4},{6,7},{7,6},{8,9},{9,8},{10,11... | collective-permute-start | bytes 786440 | tf_op jit(solution)/shard_map/ppermute | solution.py:183
  17.9 1.6 tile_quarter.5
  19.5 2.2 collective-permute-done
  21.7 4.1 %collective-permute-start.2 = (f32[256,256]{1,0:T(8,128)S(1)}, f32[256,256]{1,0:T(8,128)S(1)}, u32[]{:S(2)}, u32[]{:S(2)}) collective-permute-start(f32[256,256]{1,0:T(8,128)S(1)} %add.42), channel_id=1, source_target_pairs={{0,2},{1,3},{2,0},{3,1},{4,6},{5,7},{6,4},{7,5},{8,10},{9,11},{10,... | collective-permute-start | bytes 786440 | tf_op jit(solution)/shard_map/ppermute | solution.py:183
  25.8 1.6 tile_quarter.6
  27.4 2.4 %collective-permute-start.1 = (f32[256,256]{1,0:T(8,128)S(1)}, f32[256,256]{1,0:T(8,128)S(1)}, u32[]{:S(2)}, u32[]{:S(2)}) collective-permute-start(f32[256,256]{1,0:T(8,128)S(1)} %get-tuple-element.23), channel_id=1, source_target_pairs={{0,1},{1,0},{2,3},{3,2},{4,5},{5,4},{6,7},{7,6},{8,9},{9,8},{10,11... | collective-permute-start | bytes 786440 | tf_op jit(solution)/shard_map/ppermute | solution.py:183
  29.8 1.6 tile_quarter.7
  31.3 1.3 collective-permute-done.2
  32.6 3.0 %collective-permute-done.1 = f32[256,256]{1,0:T(8,128)S(1)} collective-permute-done((f32[256,256]{1,0:T(8,128)S(1)}, f32[256,256]{1,0:T(8,128)S(1)}, u32[]{:S(2)}, u32[]{:S(2)}) %collective-permute-start.1) | collective-permute-done | bytes 262176 | tf_op jit(solution)/shard_map/ppermute | solution.py:183
  35.7 0.8 add_add_fusion
  36.4 7.8 %all-to-all-start = ((f32[4,64,256]{2,1,0:T(8,128)}), f32[4,64,256]{2,1,0:T(8,128)S(1)}, u32[]{:S(2)}, u32[]{:S(2)}) async-start(f32[4,64,256]{2,1,0:T(8,128)} %bitcast.7), calls=%async_computation | async-start | bytes 524288 | tf_op jit(solution)/shard_map/all_to_all | solution.py:191
  45.4 12.5 %all-to-all-done = f32[4,64,256]{2,1,0:T(8,128)S(1)} async-done(((f32[4,64,256]{2,1,0:T(8,128)}), f32[4,64,256]{2,1,0:T(8,128)S(1)}, u32[]{:S(2)}, u32[]{:S(2)}) %all-to-all-start) | async-done | bytes 262176 | tf_op jit(solution)/shard_map/all_to_all | solution.py:191
  58.0 16.2 %all_gather.3.rows_ref = f32[256,256]{1,0:T(8,128)S(1)} all-gather(f32[64,256]{1,0:T(8,128)S(1)} %broadcast_select_fusion), channel_id=1, replica_groups=mesh['x'=4,'y'=4,'core'=2,'z3'=2,'z2'=2,'z1'=2,'z0'=2] {'z3','z2'}, dimensions={0}, use_global_device_ids=true | all-gather | bytes 327680 | tf_op jit(solution)/shard_map/all_gather | solution.py:219
  74.2 10.5 %collective-permute-start.3 = (f32[256,256]{1,0:T(8,128)S(1)}, f32[256,256]{1,0:T(8,128)}, u32[]{:S(2)}, u32[]{:S(2)}) collective-permute-start(f32[256,256]{1,0:T(8,128)S(1)} %all_gather.3.rows_ref), channel_id=1, source_target_pairs={{0,2},{1,3},{2,0},{3,1},{4,6},{5,7},{6,4},{7,5},{8,10},{9,11},{10,... | collective-permute-start | bytes 786440 | tf_op jit(solution)/shard_map/ppermute | solution.py:183
  85.8 12.8 %all-to-all-start.1 = ((f32[32,8,256]{2,1,0:T(8,128)}), f32[32,8,256]{2,1,0:T(8,128)}, u32[]{:S(2)}, u32[]{:S(2)}) async-start(f32[32,8,256]{2,1,0:T(8,128)} %bitcast.6), calls=%async_computation.1 | async-start | bytes 524288 | tf_op jit(solution)/shard_map/all_to_all | solution.py:191
  99.3 8.3 %all-to-all-done.1 = f32[32,8,256]{2,1,0:T(8,128)} async-done(((f32[32,8,256]{2,1,0:T(8,128)}), f32[32,8,256]{2,1,0:T(8,128)}, u32[]{:S(2)}, u32[]{:S(2)}) %all-to-all-start.1) | async-done | bytes 262176 | tf_op jit(solution)/shard_map/all_to_all | solution.py:191
  107.6 1.0 reduce_sum.47
  108.6 1.7 constant_dynamic-update-slice_fusion.own_ref
  110.3 1.9 collective-permute-start.4
  112.2 7.0 %all_to_all.25 = f32[4,8,256]{2,1,0:T(8,128)S(1)} all-to-all(f32[4,8,256]{2,1,0:T(8,128)S(1)} %broadcast_in_dim.11), channel_id=1, replica_groups=mesh['x'=4,'y'=4,'core'=2,'z3'=2,'z2'=2,'z1'=2,'z0'=2] {'z1','z0'}, dimensions={0} | all-to-all | bytes 65536 | tf_op jit(solution)/shard_map/all_to_all | solution.py:191
  119.2 0.7 broadcast_in_dim.12
  119.9 6.6 %all-to-all-start.3 = ((f32[32,8,256]{2,1,0:T(8,128)}), f32[32,8,256]{2,1,0:T(8,128)S(1)}, u32[]{:S(2)}, u32[]{:S(2)}) async-start(f32[32,8,256]{2,1,0:T(8,128)} %broadcast_in_dim.12), calls=%async_computation.3 | async-start | bytes 524288 | tf_op jit(solution)/shard_map/all_to_all | solution.py:191
  127.8 7.8 %all-to-all-done.3 = f32[32,8,256]{2,1,0:T(8,128)S(1)} async-done(((f32[32,8,256]{2,1,0:T(8,128)}), f32[32,8,256]{2,1,0:T(8,128)S(1)}, u32[]{:S(2)}, u32[]{:S(2)}) %all-to-all-start.3) | async-done | bytes 262176 | tf_op jit(solution)/shard_map/all_to_all | solution.py:191
  135.6 1.0 copy-done.3
  136.7 65.1 %basis_and_coeffs.1 = (f32[1024,256]{1,0:T(8,128)}, f32[16,8,1536]{2,1,0:T(8,128)S(1)}, f32[16,8,1536]{2,1,0:T(8,128)S(1)}) custom-call(f32[1,1]{1,0:T(1,128)} %bitcast.total_ref, f32[256,256]{1,0:T(8,128)S(1)} %bitcast.5, f32[512,256]{1,0:T(8,128)S(1)} %copy-done.3, f32[512,256]{1,0:T(8,128)} %collective-permute-done.4.other_ref, ...), custom_call_target="tpu_custom_call" | custom-call | flops 1000000000 | bytes 1048576 | tf_op jit(solution)/shard_map/basis_and_coeffs/pallas_call | solution.py:56
  201.7 2.1 collective-permute-start.5
  203.8 2.1 collective-permute-done.5
  206.0 16.1 %all_to_all.26 = f32[16,8,1536]{2,1,0:T(8,128)S(1)} all-to-all(f32[16,8,1536]{2,1,0:T(8,128)S(1)} %add.44), channel_id=1, replica_groups=mesh['x'=4,'y'=4,'core'=2,'z3'=2,'z2'=2,'z1'=2,'z0'=2] {'x','y'}, dimensions={0} | all-to-all | bytes 1572864 | tf_op jit(solution)/shard_map/all_to_all | solution.py:191
  (22 shorter events, 4.0 us)
Async XLA Ops:
  0.6 1.4 copy-start
  2.0 1.2 copy-start.1
  3.3 1.1 copy-start.2
  6.0 15.7 %collective-permute-start = (f32[256,256]{1,0:T(8,128)S(1)}, f32[256,256]{1,0:T(8,128)S(1)}, u32[]{:S(2)}, u32[]{:S(2)}) collective-permute-start(f32[256,256]{1,0:T(8,128)S(1)} %get-tuple-element.19), channel_id=1, source_target_pairs={{0,1},{1,0},{2,3},{3,2},{4,5},{5,4},{6,7},{7,6},{8,9},{9,8},{10,11... | collective-permute-start | bytes 786440 | tf_op jit(solution)/shard_map/ppermute | solution.py:183
  21.7 10.9 %collective-permute-start.2 = (f32[256,256]{1,0:T(8,128)S(1)}, f32[256,256]{1,0:T(8,128)S(1)}, u32[]{:S(2)}, u32[]{:S(2)}) collective-permute-start(f32[256,256]{1,0:T(8,128)S(1)} %add.42), channel_id=1, source_target_pairs={{0,2},{1,3},{2,0},{3,1},{4,6},{5,7},{6,4},{7,5},{8,10},{9,11},{10,... | collective-permute-start | bytes 786440 | tf_op jit(solution)/shard_map/ppermute | solution.py:183
  27.4 8.3 %collective-permute-start.1 = (f32[256,256]{1,0:T(8,128)S(1)}, f32[256,256]{1,0:T(8,128)S(1)}, u32[]{:S(2)}, u32[]{:S(2)}) collective-permute-start(f32[256,256]{1,0:T(8,128)S(1)} %get-tuple-element.23), channel_id=1, source_target_pairs={{0,1},{1,0},{2,3},{3,2},{4,5},{5,4},{6,7},{7,6},{8,9},{9,8},{10,11... | collective-permute-start | bytes 786440 | tf_op jit(solution)/shard_map/ppermute | solution.py:183
  29.8 14.4 %copy-start.5 = (s32[32]{0:T(128)S(1)}, s32[32]{0:T(128)}, u32[]{:S(2)}) copy-start(s32[32]{0:T(128)} %param.7) | copy-start | bytes 388
  36.4 21.5 %all-to-all-start = ((f32[4,64,256]{2,1,0:T(8,128)}), f32[4,64,256]{2,1,0:T(8,128)S(1)}, u32[]{:S(2)}, u32[]{:S(2)}) async-start(f32[4,64,256]{2,1,0:T(8,128)} %bitcast.7), calls=%async_computation | async-start | bytes 524288 | tf_op jit(solution)/shard_map/all_to_all | solution.py:191
  74.2 34.4 %collective-permute-start.3 = (f32[256,256]{1,0:T(8,128)S(1)}, f32[256,256]{1,0:T(8,128)}, u32[]{:S(2)}, u32[]{:S(2)}) collective-permute-start(f32[256,256]{1,0:T(8,128)S(1)} %all_gather.3.rows_ref), channel_id=1, source_target_pairs={{0,2},{1,3},{2,0},{3,1},{4,6},{5,7},{6,4},{7,5},{8,10},{9,11},{10,... | collective-permute-start | bytes 786440 | tf_op jit(solution)/shard_map/ppermute | solution.py:183
  85.1 0.7 copy-start.4
  85.8 21.8 %all-to-all-start.1 = ((f32[32,8,256]{2,1,0:T(8,128)}), f32[32,8,256]{2,1,0:T(8,128)}, u32[]{:S(2)}, u32[]{:S(2)}) async-start(f32[32,8,256]{2,1,0:T(8,128)} %bitcast.6), calls=%async_computation.1 | async-start | bytes 524288 | tf_op jit(solution)/shard_map/all_to_all | solution.py:191
  110.3 25.4 %collective-permute-start.4 = (f32[512,256]{1,0:T(8,128)}, f32[512,256]{1,0:T(8,128)}, u32[]{:S(2)}, u32[]{:S(2)}) collective-permute-start(f32[512,256]{1,0:T(8,128)} %constant_dynamic-update-slice_fusion.own_ref), channel_id=1, source_target_pairs={{0,1},{1,0},{2,3},{3,2},{4,5},{5,4},{6,7},{7,6},{8,9},{9,8},{10,11... | collective-permute-start | bytes 1572872 | tf_op jit(solution)/shard_map/ppermute | solution.py:183
  119.9 15.7 %all-to-all-start.3 = ((f32[32,8,256]{2,1,0:T(8,128)}), f32[32,8,256]{2,1,0:T(8,128)S(1)}, u32[]{:S(2)}, u32[]{:S(2)}) async-start(f32[32,8,256]{2,1,0:T(8,128)} %broadcast_in_dim.12), calls=%async_computation.3 | async-start | bytes 524288 | tf_op jit(solution)/shard_map/all_to_all | solution.py:191
  135.6 1.0 copy-start.3
  201.7 4.2 %collective-permute-start.5 = (f32[16,8,1536]{2,1,0:T(8,128)S(1)}, f32[16,8,1536]{2,1,0:T(8,128)S(1)}, u32[]{:S(2)}, u32[]{:S(2)}) collective-permute-start(f32[16,8,1536]{2,1,0:T(8,128)S(1)} %get-tuple-element.31), channel_id=1, source_target_pairs={{0,16},{16,0},{1,17},{17,1},{2,18},{18,2},{3,19},{19,3},{4,20},{20... | collective-permute-start | bytes 2359304 | tf_op jit(solution)/shard_map/ppermute | solution.py:187

commit v8 on v7

--- a/solution.py
+++ b/solution.py
@@ -74,6 +74,16 @@
     return 2 * low + (second + 1 - (order - 2)) % 2
 
 
+def split(value):
+    high = value.astype(BF16)
+    return high, (value - high.astype(F32)).astype(BF16)
+
+
+def dot_split(a, b, contract):
+    (a_high, a_low), (b_high, b_low) = a, b
+    return dot(a_high, b_high, contract) + (dot(a_high, b_low, contract) + dot(a_low, b_high, contract))
+
+
 def tile_kernel(tex_ref, light_ref, sketch_ref, *refs, order, step=128):
     tile_ref, part_ref = refs[-2:]
     rows = part_ref.shape[0]
@@ -96,8 +106,15 @@
     )(tex, light, sketch, *tiles)
 
 
-def gram_kernel(rows_ref, gram_ref):
-    gram_ref[...] = dot(rows_ref[...], rows_ref[...], (0, 0), HIGHEST)
+def gram_kernel(counts_ref, quarter_ref, near_ref, rows_ref, gram_ref):
+    rows = quarter_ref.shape[0]
+    texel = lax.broadcasted_iota(jnp.int32, counts_ref.shape, 1)
+    count = jnp.sum(jnp.where(texel == lax.axis_index(TEXEL), counts_ref[...], 0), axis=1, keepdims=True)
+    row = lax.broadcasted_iota(jnp.int32, quarter_ref.shape, 0)
+    rows_ref[:rows, :] = jnp.where(row + quarter_of(3) * rows < count, quarter_ref[...], 0.0)
+    rows_ref[rows:, :] = jnp.where(row + quarter_of(2) * rows < count, near_ref[...], 0.0)
+    parts = split(rows_ref[...])
+    gram_ref[...] = dot_split(parts, parts, (0, 0))
 
 
 def invert_factor(gram, y_ref, a_ref, w_ref):
@@ -156,8 +173,9 @@
     total = total_ref[...]
     invert_factor(gram_ref[...] / total, inverse_ref, a_ref, w_ref)
     rows = basis_ref.shape[0] // 4
+    inverse = split(inverse_ref[...])
     for ref, orders in ((own_ref, (3, 2)), (other_ref, (1, 0))):
-        basis = dot(ref[...], inverse_ref[...], (1, 1), HIGHEST)
+        basis = dot_split(split(ref[...]), inverse, (1, 1))
         for i, order in enumerate(orders):
             part = basis[i * rows : (i + 1) * rows, :]
             basis_ref[pl.ds(pl.multiple_of(quarter_of(order) * rows, rows), rows), :] = part
@@ -201,30 +219,28 @@
     texels, places = lax.axis_size(TEXEL), lax.axis_size(LIGHT)
     share_rows = capacity // places
     total = jnp.sum(row_counts).astype(F32).reshape(1, 1)
-    used = row_counts[lax.axis_index(TEXEL)] - quarter_of(3) * (capacity // 4) - lax.axis_index(FAR) * share_rows
 
     inputs = (tex_feat, light_feat, sketch)
     tiles, part = tile_call(0, *inputs)
     passing = across(part, 1)
-    tiles, part = tile_call(2, *inputs, tiles)
-    tiles, passing = lax.optimization_barrier((tiles, passing))
-    passed = across(part + passing, 2)
+    tiles, turned = tile_call(2, *inputs, tiles)
     tiles, part = tile_call(1, *inputs, tiles)
     staying = across(part, 1)
+    passed = across(turned + passing, 2)
     tiles, part = tile_call(3, *inputs, tiles)
     quarter = part + staying + passed
     share = jnp.sum(each_to_each(quarter.reshape(places // 4, share_rows, width), FAR), axis=0)
-    share = jnp.where(lax.broadcasted_iota(jnp.int32, share.shape, 0) < used, share, 0.0)
 
     quarter = lax.all_gather(share, FAR, axis=0, tiled=True)
-    near = across(quarter, 2)
-    gram = on_core(gram_kernel, jax.ShapeDtypeStruct((width, width), F32), "gram_part")(quarter)
+    half_shape, square = (capacity // 2, width), (width, width)
+    own, gram = on_core(
+        gram_kernel, (jax.ShapeDtypeStruct(half_shape, F32), jax.ShapeDtypeStruct(square, F32)), "gram_part"
+    )(row_counts.reshape(1, texels), quarter, across(quarter, 2))
+    other = across(own, 1)
     gram_rows = jnp.sum(each_to_each(gram.reshape(texels, width // texels, width), TEXEL), axis=0)
-    gram_rows, near = lax.optimization_barrier((gram_rows, near))
-    own = jnp.concatenate([quarter, near])
-    other = across(own, 1)
-    gram_rows = jnp.sum(to_each(gram_rows, ("z1", "z0")), axis=0)
-    gram = to_each(gram_rows, TEXEL).reshape(width, width)
+    gram_rows, other = lax.optimization_barrier((gram_rows, other))
+    gram_rows = gram_rows + lax.ppermute(gram_rows, "z0", [(0, 1), (1, 0)])
+    gram = to_each(gram_rows, TEXEL).reshape(square)
 
     lines, chips = width // texels, lax.axis_size(CHIP)
     basis, keep, send = on_core(
@@ -235,7 +251,7 @@
             jax.ShapeDtypeStruct((chips, lines, lights), F32),
         ),
         "basis_and_coeffs",
-        [pltpu.VMEM((width, width), F32)] * 3
+        [pltpu.VMEM(square, F32)] * 3
         + [pltpu.VMEM((capacity, width), BF16), pltpu.VMEM((texels, lines, lights), F32)],
     )(total, gram, own, other, tiles)
     mine = keep + across_cores(send)

time: 224 us -> 218 us (0.973)
  blocking collectives: 39.2 us -> 79 us
  starting transfers between devices: 60 us -> 34.5 us
  waiting for transfers between devices: 37.2 us -> 24.5 us
  local copies, waits for them, and re-layouts: 9.22 us -> 4.49 us
    all_to_all x2 -> x3, blocking collectives: 23.1 us -> 62.8 us  [each_to_each(): return lax.all_to_all(parts, axes, 0, 0, tiled=True)]
    all_to_all x3 -> x1, starting transfers between devices: 27.1 us -> 4.86 us  [each_to_each(): return lax.all_to_all(parts, axes, 0, 0, tiled=True)]
    all_to_all x3 -> x1, waiting for transfers between devices: 28.6 us -> 7.82 us  [each_to_each(): return lax.all_to_all(parts, axes, 0, 0, tiled=True)]
    ppermute x5, waiting for transfers between devices: 6.55 us -> 13.3 us  [across(): lax.ppermute(value, ('core', *LIGHT), light_pairs(lax.axis_size(LIGHT), r...]
    ppermute x5, starting transfers between devices: 30.8 us -> 24.4 us  [across(): lax.ppermute(value, ('core', *LIGHT), light_pairs(lax.axis_size(LIGHT), r...]
    ppermute x0 -> x1, starting transfers between devices: none -> 3.06 us  [on_device(): gram_rows = gram_rows + lax.ppermute(gram_rows, 'z0', [(0, 1), (1, 0)])]
    unnamed x13 -> x8, local copies, waits for them, and re-layouts: 6.23 us -> 3.76 us
  transfers between devices with their start and end apart: 9 -> 8, of which waited for: 7 -> 6; matrix products, arithmetic and copies ran while one was open for 2% -> 0% of each run, Pallas kernels for 2% -> 2%
where the time goes in v8:
time: 218 us; the launch traced here: 217 us
  blocking collectives  79 us (36%)
  Pallas kernels  72 us (33%)
  starting transfers between devices  34.5 us (16%)
  waiting for transfers between devices  24.5 us (11%)
  local copies, waits for them, and re-layouts  4.49 us (2%)
    pallas_call x6, Pallas kernels, on_core(): pl.pallas_call(kernel, out_shape=out_shape, in_specs=[VMEM] * len(operand...  72 us
    all_to_all x3, blocking collectives, each_to_each(): return lax.all_to_all(parts, axes, 0, 0, tiled=True)  62.8 us
    ppermute x5, starting transfers between devices, across(): lax.ppermute(value, ('core', *LIGHT), light_pairs(lax.axis_size(LIGHT), r...  24.4 us
    all_gather x1, blocking collectives, on_device(): quarter = lax.all_gather(share, FAR, axis=0, tiled=True)  16.2 us
    ppermute x5, waiting for transfers between devices, across(): lax.ppermute(value, ('core', *LIGHT), light_pairs(lax.axis_size(LIGHT), r...  13.3 us
    all_to_all x1, waiting for transfers between devices, each_to_each(): return lax.all_to_all(parts, axes, 0, 0, tiled=True)  7.82 us
    all_to_all x1, starting transfers between devices, each_to_each(): return lax.all_to_all(parts, axes, 0, 0, tiled=True)  4.86 us
  transfers between devices with their start and end apart: 8, of which 6 were waited for; matrix products, arithmetic and copies ran while one was open for 0% of the time, Pallas kernels for 2%

profile of v8, /device:TPU:1, one launch (start us, length us, event | category | flops | bytes accessed | tf_op | source)
XLA Modules:
  0.0 217.3 jit_solution(6382749516666935680)
XLA Ops:
  0.6 1.4 copy-done
  2.0 1.2 copy-done.1
  3.3 1.1 copy-done.2
  4.4 1.6 tile_quarter.4
  6.0 11.9 %collective-permute-start.1 = (f32[256,256]{1,0:T(8,128)S(1)}, f32[256,256]{1,0:T(8,128)S(1)}, u32[]{:S(2)}, u32[]{:S(2)}) collective-permute-start(f32[256,256]{1,0:T(8,128)S(1)} %get-tuple-element.23), channel_id=1, source_target_pairs={{0,1},{1,0},{2,3},{3,2},{4,5},{5,4},{6,7},{7,6},{8,9},{9,8},{10,11... | collective-permute-start | bytes 786440 | tf_op jit(solution)/shard_map/ppermute | solution.py:201
  17.9 1.6 tile_quarter.5
  19.5 1.6 tile_quarter.6
  21.0 1.9 collective-permute-start
  23.0 3.8 %collective-permute-start.2 = (f32[256,256]{1,0:T(8,128)S(1)}, f32[256,256]{1,0:T(8,128)S(1)}, u32[]{:S(2)}, u32[]{:S(2)}) collective-permute-start(f32[256,256]{1,0:T(8,128)S(1)} %add.16), channel_id=1, source_target_pairs={{0,2},{1,3},{2,0},{3,1},{4,6},{5,7},{6,4},{7,5},{8,10},{9,11},{10,... | collective-permute-start | bytes 786440 | tf_op jit(solution)/shard_map/ppermute | solution.py:201
  26.8 1.6 tile_quarter.7
  28.4 1.1 collective-permute-done
  29.5 4.8 %collective-permute-done.2 = f32[256,256]{1,0:T(8,128)S(1)} collective-permute-done((f32[256,256]{1,0:T(8,128)S(1)}, f32[256,256]{1,0:T(8,128)S(1)}, u32[]{:S(2)}, u32[]{:S(2)}) %collective-permute-start.2) | collective-permute-done | bytes 262176 | tf_op jit(solution)/shard_map/ppermute | solution.py:201
  34.3 0.1 add_add_fusion
  34.3 26.9 %all_to_all.20 = f32[4,64,256]{2,1,0:T(8,128)S(1)} all-to-all(f32[4,64,256]{2,1,0:T(8,128)S(1)} %bitcast.8), channel_id=1, replica_groups=mesh['x'=4,'y'=4,'core'=2,'z3'=2,'z2'=2,'z1'=2,'z0'=2] {'z3','z2'}, dimensions={0} | all-to-all | bytes 524288 | tf_op jit(solution)/shard_map/all_to_all | solution.py:209
  61.2 16.2 %all_gather.3.quarter_ref = f32[256,256]{1,0:T(8,128)S(1)} all-gather(f32[64,256]{1,0:T(8,128)S(1)} %reduce_sum.37), channel_id=1, replica_groups=mesh['x'=4,'y'=4,'core'=2,'z3'=2,'z2'=2,'z1'=2,'z0'=2] {'z3','z2'}, dimensions={0}, use_global_device_ids=true | all-gather | bytes 327680 | tf_op jit(solution)/shard_map/all_gather | solution.py:234
  77.4 1.9 collective-permute-start.3
  79.3 7.4 %collective-permute-done.3.near_ref = f32[256,256]{1,0:T(8,128)S(1)} collective-permute-done((f32[256,256]{1,0:T(8,128)S(1)}, f32[256,256]{1,0:T(8,128)S(1)}, u32[]{:S(2)}, u32[]{:S(2)}) %collective-permute-start.3) | collective-permute-done | bytes 262176 | tf_op jit(solution)/shard_map/ppermute | solution.py:201
  86.7 1.0 gram_part.1
  87.7 4.9 %collective-permute-start.4 = (f32[512,256]{1,0:T(8,128)}, f32[512,256]{1,0:T(8,128)}, u32[]{:S(2)}, u32[]{:S(2)}) collective-permute-start(f32[512,256]{1,0:T(8,128)} %get-tuple-element.25.own_ref), channel_id=1, source_target_pairs={{0,1},{1,0},{2,3},{3,2},{4,5},{5,4},{6,7},{7,6},{8,9},{9,8},{10,11... | collective-permute-start | bytes 1572872 | tf_op jit(solution)/shard_map/ppermute | solution.py:201
  92.6 19.8 %all_to_all.21 = f32[32,8,256]{2,1,0:T(8,128)S(1)} all-to-all(f32[32,8,256]{2,1,0:T(8,128)S(1)} %bitcast.6), channel_id=1, replica_groups=mesh['x'=4,'y'=4,'core'=2,'z3'=2,'z2'=2,'z1'=2,'z0'=2] {'x','y','core'}, dimensions={0} | all-to-all | bytes 524288 | tf_op jit(solution)/shard_map/all_to_all | solution.py:209
  112.5 3.1 %collective-permute-start.5 = (f32[8,256]{1,0:T(8,128)S(1)}, f32[8,256]{1,0:T(8,128)S(1)}, u32[]{:S(2)}, u32[]{:S(2)}) collective-permute-start(f32[8,256]{1,0:T(8,128)S(1)} %reduce_sum.38), channel_id=1, source_target_pairs={{0,1},{1,0},{2,3},{3,2},{4,5},{5,4},{6,7},{7,6},{8,9},{9,8},{10,11... | collective-permute-start | bytes 24584 | tf_op jit(solution)/shard_map/ppermute | solution.py:242
  115.5 1.3 collective-permute-done.5
  116.9 0.7 broadcast_in_dim.3
  117.6 4.9 %all-to-all-start.2 = ((f32[32,8,256]{2,1,0:T(8,128)}), f32[32,8,256]{2,1,0:T(8,128)S(1)}, u32[]{:S(2)}, u32[]{:S(2)}) async-start(f32[32,8,256]{2,1,0:T(8,128)} %broadcast_in_dim.3), calls=%async_computation.2 | async-start | bytes 524288 | tf_op jit(solution)/shard_map/all_to_all | solution.py:209
  122.5 0.6 reduce_sum.36
  123.8 7.8 %all-to-all-done.2 = f32[32,8,256]{2,1,0:T(8,128)S(1)} async-done(((f32[32,8,256]{2,1,0:T(8,128)}), f32[32,8,256]{2,1,0:T(8,128)S(1)}, u32[]{:S(2)}, u32[]{:S(2)}) %all-to-all-start.2) | async-done | bytes 262176 | tf_op jit(solution)/shard_map/all_to_all | solution.py:209
  131.6 64.8 %basis_and_coeffs.1 = (f32[1024,256]{1,0:T(8,128)}, f32[16,8,1536]{2,1,0:T(8,128)S(1)}, f32[16,8,1536]{2,1,0:T(8,128)S(1)}) custom-call(f32[1,1]{1,0:T(1,128)} %bitcast.total_ref, f32[256,256]{1,0:T(8,128)S(1)} %bitcast.5, f32[512,256]{1,0:T(8,128)} %get-tuple-element.25.own_ref, f32[512,256]{1,0:T(8,128)} %collective-permute-done.4.other_ref, ...), custom_call_target="tpu_custom_call" | custom-call | flops 1000000000 | bytes 1048576 | tf_op jit(solution)/shard_map/basis_and_coeffs/pallas_call | solution.py:56
  196.4 2.1 collective-permute-start.6
  198.4 2.1 collective-permute-done.6
  200.5 0.1 add.19
  200.6 16.1 %all_to_all.22 = f32[16,8,1536]{2,1,0:T(8,128)S(1)} all-to-all(f32[16,8,1536]{2,1,0:T(8,128)S(1)} %add.19), channel_id=1, replica_groups=mesh['x'=4,'y'=4,'core'=2,'z3'=2,'z2'=2,'z1'=2,'z0'=2] {'x','y'}, dimensions={0} | all-to-all | bytes 1572864 | tf_op jit(solution)/shard_map/all_to_all | solution.py:209
  216.7 0.7 reduce_sum.39
  (11 shorter events, 0.1 us)
Async XLA Ops:
  0.6 1.4 copy-start
  2.0 1.2 copy-start.1
  3.3 1.1 copy-start.2
  6.0 17.0 %collective-permute-start.1 = (f32[256,256]{1,0:T(8,128)S(1)}, f32[256,256]{1,0:T(8,128)S(1)}, u32[]{:S(2)}, u32[]{:S(2)}) collective-permute-start(f32[256,256]{1,0:T(8,128)S(1)} %get-tuple-element.23), channel_id=1, source_target_pairs={{0,1},{1,0},{2,3},{3,2},{4,5},{5,4},{6,7},{7,6},{8,9},{9,8},{10,11... | collective-permute-start | bytes 786440 | tf_op jit(solution)/shard_map/ppermute | solution.py:201
  21.0 8.5 %collective-permute-start = (f32[256,256]{1,0:T(8,128)S(1)}, f32[256,256]{1,0:T(8,128)S(1)}, u32[]{:S(2)}, u32[]{:S(2)}) collective-permute-start(f32[256,256]{1,0:T(8,128)S(1)} %get-tuple-element.21), channel_id=1, source_target_pairs={{0,1},{1,0},{2,3},{3,2},{4,5},{5,4},{6,7},{7,6},{8,9},{9,8},{10,11... | collective-permute-start | bytes 786440 | tf_op jit(solution)/shard_map/ppermute | solution.py:201
  23.0 11.2 %collective-permute-start.2 = (f32[256,256]{1,0:T(8,128)S(1)}, f32[256,256]{1,0:T(8,128)S(1)}, u32[]{:S(2)}, u32[]{:S(2)}) collective-permute-start(f32[256,256]{1,0:T(8,128)S(1)} %add.16), channel_id=1, source_target_pairs={{0,2},{1,3},{2,0},{3,1},{4,6},{5,7},{6,4},{7,5},{8,10},{9,11},{10,... | collective-permute-start | bytes 786440 | tf_op jit(solution)/shard_map/ppermute | solution.py:201
  26.8 59.9 %copy-start.3 = (s32[32]{0:T(128)S(1)}, s32[32]{0:T(128)}, u32[]{:S(2)}) copy-start(s32[32]{0:T(128)} %param.7) | copy-start | bytes 388
  77.4 9.3 %collective-permute-start.3 = (f32[256,256]{1,0:T(8,128)S(1)}, f32[256,256]{1,0:T(8,128)S(1)}, u32[]{:S(2)}, u32[]{:S(2)}) collective-permute-start(f32[256,256]{1,0:T(8,128)S(1)} %all_gather.3.quarter_ref), channel_id=1, source_target_pairs={{0,2},{1,3},{2,0},{3,1},{4,6},{5,7},{6,4},{7,5},{8,10},{9,11},{10,... | collective-permute-start | bytes 786440 | tf_op jit(solution)/shard_map/ppermute | solution.py:201
  87.7 24.7 %collective-permute-start.4 = (f32[512,256]{1,0:T(8,128)}, f32[512,256]{1,0:T(8,128)}, u32[]{:S(2)}, u32[]{:S(2)}) collective-permute-start(f32[512,256]{1,0:T(8,128)} %get-tuple-element.25.own_ref), channel_id=1, source_target_pairs={{0,1},{1,0},{2,3},{3,2},{4,5},{5,4},{6,7},{7,6},{8,9},{9,8},{10,11... | collective-permute-start | bytes 1572872 | tf_op jit(solution)/shard_map/ppermute | solution.py:201
  112.5 4.4 %collective-permute-start.5 = (f32[8,256]{1,0:T(8,128)S(1)}, f32[8,256]{1,0:T(8,128)S(1)}, u32[]{:S(2)}, u32[]{:S(2)}) collective-permute-start(f32[8,256]{1,0:T(8,128)S(1)} %reduce_sum.38), channel_id=1, source_target_pairs={{0,1},{1,0},{2,3},{3,2},{4,5},{5,4},{6,7},{7,6},{8,9},{9,8},{10,11... | collective-permute-start | bytes 24584 | tf_op jit(solution)/shard_map/ppermute | solution.py:242
  117.6 14.0 %all-to-all-start.2 = ((f32[32,8,256]{2,1,0:T(8,128)}), f32[32,8,256]{2,1,0:T(8,128)S(1)}, u32[]{:S(2)}, u32[]{:S(2)}) async-start(f32[32,8,256]{2,1,0:T(8,128)} %broadcast_in_dim.3), calls=%async_computation.2 | async-start | bytes 524288 | tf_op jit(solution)/shard_map/all_to_all | solution.py:209
  196.4 4.2 %collective-permute-start.6 = (f32[16,8,1536]{2,1,0:T(8,128)S(1)}, f32[16,8,1536]{2,1,0:T(8,128)S(1)}, u32[]{:S(2)}, u32[]{:S(2)}) collective-permute-start(f32[16,8,1536]{2,1,0:T(8,128)S(1)} %get-tuple-element.31), channel_id=1, source_target_pairs={{0,16},{16,0},{1,17},{17,1},{2,18},{18,2},{3,19},{19,3},{4,20},{20... | collective-permute-start | bytes 2359304 | tf_op jit(solution)/shard_map/ppermute | solution.py:205

commit v9 on v8

--- a/solution.py
+++ b/solution.py
@@ -106,13 +106,15 @@
     )(tex, light, sketch, *tiles)
 
 
-def gram_kernel(counts_ref, quarter_ref, near_ref, rows_ref, gram_ref):
+def mask_kernel(counts_ref, quarter_ref, rows_ref):
     rows = quarter_ref.shape[0]
     texel = lax.broadcasted_iota(jnp.int32, counts_ref.shape, 1)
     count = jnp.sum(jnp.where(texel == lax.axis_index(TEXEL), counts_ref[...], 0), axis=1, keepdims=True)
     row = lax.broadcasted_iota(jnp.int32, quarter_ref.shape, 0)
-    rows_ref[:rows, :] = jnp.where(row + quarter_of(3) * rows < count, quarter_ref[...], 0.0)
-    rows_ref[rows:, :] = jnp.where(row + quarter_of(2) * rows < count, near_ref[...], 0.0)
+    rows_ref[...] = jnp.where(row + quarter_of(3) * rows < count, quarter_ref[...], 0.0)
+
+
+def gram_kernel(rows_ref, gram_ref):
     parts = split(rows_ref[...])
     gram_ref[...] = dot_split(parts, parts, (0, 0))
 
@@ -121,34 +123,42 @@
     size = gram.shape[0]
     row = lax.broadcasted_iota(jnp.int32, (size, size), 0)
     col = lax.broadcasted_iota(jnp.int32, (size, size), 1)
-    diagonal = jnp.sum(jnp.where(row == col, gram, 0.0), axis=0, keepdims=True)
+
+    def lower_half(rest):
+        return jnp.where(row > col, rest, jnp.where(row == col, 0.5 * rest, 0.0))
+
+    diagonal = jnp.where(row == col, gram, 0.0)
+    across_columns = lax.rsqrt(jnp.sum(diagonal, axis=0, keepdims=True))
+    down_rows = lax.rsqrt(jnp.sum(diagonal, axis=1, keepdims=True))
+    unit = jnp.where(row == col, F32(1), F32(0))
     a_ref[...] = gram
-    y_ref[...] = jnp.where(row == col, lax.rsqrt(diagonal), 0.0)
+    y_ref[...] = (unit - lower_half(gram * down_rows * across_columns - unit)) * across_columns
 
     def refine(exact):
-        precision = HIGHEST if exact else None
-        cast = (lambda v: v) if exact else (lambda v: v.astype(BF16))
-        y = cast(y_ref[...])
-        product = dot(dot(y, cast(a_ref[...]), (1, 0), precision).astype(y.dtype), y, (1, 1), precision)
-        off = product - jnp.where(row == col, F32(1), F32(0))
-        step = jnp.where(row > col, off, jnp.where(row == col, 0.5 * off, 0.0))
-        y_ref[...] = y_ref[...] - dot(cast(step), y, (1, 0), precision)
-        return jnp.sum(off * off)
-
-    def coarse(state):
-        count, _ = state
-        return count + 1, refine(False)
-
-    def fine(state):
-        count, _ = state
-        return count + 1, refine(True)
-
-    lax.while_loop(lambda s: (s[0] < 8) & (s[1] > 2e-2), coarse, (jnp.int32(0), F32(1)))
-    _, rest = lax.while_loop(lambda s: (s[0] < 8) & (s[1] > 4e-6), fine, (jnp.int32(0), F32(1)))
+        y = y_ref[...]
+        if exact:
+            parts = split(y)
+            rest = dot_split(split(dot_split(parts, split(a_ref[...]), (1, 0))), parts, (1, 1)) - unit
+            y_ref[...] = y - dot_split(split(lower_half(rest)), parts, (1, 0))
+        else:
+            rough = y.astype(BF16)
+            rest = dot(dot(rough, a_ref[...].astype(BF16), (1, 0)).astype(BF16), rough, (1, 1)) - unit
+            y_ref[...] = y - dot(lower_half(rest).astype(BF16), rough, (1, 0))
+        return jnp.sum(rest * rest)
+
+    def steps(exact, enough):
+        return lax.while_loop(
+            lambda state: (state[0] < 8) & (state[1] > enough),
+            lambda state: (state[0] + 1, refine(exact)),
+            (jnp.int32(0), F32(1)),
+        )[1]
+
+    steps(False, 1e-1)
+    rest = steps(True, 4e-6)
 
     @pl.when(jnp.logical_not(rest <= 4e-6))
     def _():
-        y_ref[...] = jnp.where(row == col, F32(1), F32(0))
+        y_ref[...] = unit
         line = lax.broadcasted_iota(jnp.int32, (size, 1), 0)
         w_ref[...] = gram
 
@@ -166,20 +176,17 @@
         lax.fori_loop(0, size, eliminate, 0)
 
 
-def basis_kernel(
-    total_ref, gram_ref, own_ref, other_ref, tile_ref,
-    basis_ref, keep_ref, send_ref, inverse_ref, a_ref, w_ref, half_ref, coeff_ref,
-):
+def basis_kernel(total_ref, gram_ref, *refs):
+    quarter_refs, tile_ref = refs[:4], refs[4]
+    basis_ref, keep_ref, send_ref, inverse_ref, a_ref, w_ref, half_ref, coeff_ref = refs[5:]
     total = total_ref[...]
     invert_factor(gram_ref[...] / total, inverse_ref, a_ref, w_ref)
     rows = basis_ref.shape[0] // 4
     inverse = split(inverse_ref[...])
-    for ref, orders in ((own_ref, (3, 2)), (other_ref, (1, 0))):
+    for order, ref in enumerate(quarter_refs):
         basis = dot_split(split(ref[...]), inverse, (1, 1))
-        for i, order in enumerate(orders):
-            part = basis[i * rows : (i + 1) * rows, :]
-            basis_ref[pl.ds(pl.multiple_of(quarter_of(order) * rows, rows), rows), :] = part
-            half_ref[order * rows : (order + 1) * rows, :] = part.astype(BF16)
+        basis_ref[pl.ds(pl.multiple_of(quarter_of(order) * rows, rows), rows), :] = basis
+        half_ref[order * rows : (order + 1) * rows, :] = basis.astype(BF16)
     coeffs = dot(half_ref[...], tile_ref[...], (0, 0))
     coeff_ref[...] = (coeffs * (1.0 / jnp.sqrt(total))).reshape(coeff_ref.shape)
     core = lax.axis_index("core")
@@ -231,15 +238,17 @@
     quarter = part + staying + passed
     share = jnp.sum(each_to_each(quarter.reshape(places // 4, share_rows, width), FAR), axis=0)
 
+    square = (width, width)
     quarter = lax.all_gather(share, FAR, axis=0, tiled=True)
-    half_shape, square = (capacity // 2, width), (width, width)
-    own, gram = on_core(
-        gram_kernel, (jax.ShapeDtypeStruct(half_shape, F32), jax.ShapeDtypeStruct(square, F32)), "gram_part"
-    )(row_counts.reshape(1, texels), quarter, across(quarter, 2))
-    other = across(own, 1)
+    quarter = on_core(mask_kernel, jax.ShapeDtypeStruct(quarter.shape, F32), "used_rows")(
+        row_counts.reshape(1, texels), quarter
+    )
+    near, beside = across(quarter, 2), across(quarter, 1)
+    gram = on_core(gram_kernel, jax.ShapeDtypeStruct(square, F32), "gram_part")(quarter)
     gram_rows = jnp.sum(each_to_each(gram.reshape(texels, width // texels, width), TEXEL), axis=0)
-    gram_rows, other = lax.optimization_barrier((gram_rows, other))
-    gram_rows = gram_rows + lax.ppermute(gram_rows, "z0", [(0, 1), (1, 0)])
+    gram_rows, near, beside = lax.optimization_barrier((gram_rows, near, beside))
+    beyond = across(near, 1)
+    gram_rows = jnp.sum(to_each(gram_rows, ("z1", "z0")), axis=0)
     gram = to_each(gram_rows, TEXEL).reshape(square)
 
     lines, chips = width // texels, lax.axis_size(CHIP)
@@ -253,7 +262,7 @@
         "basis_and_coeffs",
         [pltpu.VMEM(square, F32)] * 3
         + [pltpu.VMEM((capacity, width), BF16), pltpu.VMEM((texels, lines, lights), F32)],
-    )(total, gram, own, other, tiles)
+    )(total, gram, beyond, beside, near, quarter, tiles)
     mine = keep + across_cores(send)
     coeffs = jnp.sum(each_to_each(mine, CHIP), axis=0)
     return basis, coeffs

time: 218 us -> 216 us (level)
  waiting for transfers between devices: 24.5 us -> 18.3 us
    ppermute x5 -> x6, waiting for transfers between devices: 13.3 us -> 5.88 us  [across(): lax.ppermute(value, ('core', *LIGHT), light_pairs(lax.axis_size(LIGHT), r...]
    all_to_all x1 -> x2, starting transfers between devices: 4.86 us -> 9.21 us  [each_to_each(): return lax.all_to_all(parts, axes, 0, 0, tiled=True)]
    ppermute x1 -> x0, starting transfers between devices: 3.06 us -> none  [on_device(): gram_rows = gram_rows + lax.ppermute(gram_rows, 'z0', [(0, 1), (1, 0)])]
    all_to_all x1 -> x2, waiting for transfers between devices: 7.82 us -> 10.3 us  [each_to_each(): return lax.all_to_all(parts, axes, 0, 0, tiled=True)]
    pallas_call x6 -> x7, Pallas kernels: 72 us -> 70 us  [on_core(): pl.pallas_call(kernel, out_shape=out_shape, in_specs=[VMEM] * len(operand...]
    unnamed x8 -> x12, local copies, waits for them, and re-layouts: 3.76 us -> 4.72 us
    ppermute x5 -> x6, starting transfers between devices: 24.4 us -> 25.3 us  [across(): lax.ppermute(value, ('core', *LIGHT), light_pairs(lax.axis_size(LIGHT), r...]
  transfers between devices with their start and end apart: 8 -> 9, of which waited for: 6 -> 5; matrix products, arithmetic and copies ran while one was open for 0% -> 1% of each run, Pallas kernels for 2% -> 2%
where the time goes in v9:
time: 216 us; the launch traced here: 215 us
  blocking collectives  80.1 us (37%)
  Pallas kernels  70 us (32%)
  starting transfers between devices  36.6 us (17%)
  waiting for transfers between devices  18.3 us (8%)
  local copies, waits for them, and re-layouts  6.06 us (3%)
  other arithmetic  2.48 us (1%)
    pallas_call x7, Pallas kernels, on_core(): pl.pallas_call(kernel, out_shape=out_shape, in_specs=[VMEM] * len(operand...  70 us
    all_to_all x3, blocking collectives, each_to_each(): return lax.all_to_all(parts, axes, 0, 0, tiled=True)  63.9 us
    ppermute x6, starting transfers between devices, across(): lax.ppermute(value, ('core', *LIGHT), light_pairs(lax.axis_size(LIGHT), r...  25.3 us
    all_gather x1, blocking collectives, on_device(): quarter = lax.all_gather(share, FAR, axis=0, tiled=True)  16.2 us
    all_to_all x2, waiting for transfers between devices, each_to_each(): return lax.all_to_all(parts, axes, 0, 0, tiled=True)  10.3 us
    all_to_all x2, starting transfers between devices, each_to_each(): return lax.all_to_all(parts, axes, 0, 0, tiled=True)  9.21 us
    ppermute x6, waiting for transfers between devices, across(): lax.ppermute(value, ('core', *LIGHT), light_pairs(lax.axis_size(LIGHT), r...  5.88 us
    unnamed x12, local copies, waits for them, and re-layouts  4.72 us
  transfers between devices with their start and end apart: 9, of which 5 were waited for; matrix products, arithmetic and copies ran while one was open for 1% of the time, Pallas kernels for 2%

profile of v9, /device:TPU:1, one launch (start us, length us, event | category | flops | bytes accessed | tf_op | source)
XLA Modules:
  0.0 214.9 jit_solution(14875487503787400279)
XLA Ops:
  0.6 1.4 copy-done
  2.0 1.2 copy-done.1
  3.3 1.1 copy-done.2
  4.4 1.6 tile_quarter.4
  6.0 11.9 %collective-permute-start.1 = (f32[256,256]{1,0:T(8,128)S(1)}, f32[256,256]{1,0:T(8,128)S(1)}, u32[]{:S(2)}, u32[]{:S(2)}) collective-permute-start(f32[256,256]{1,0:T(8,128)S(1)} %get-tuple-element.22), channel_id=1, source_target_pairs={{0,1},{1,0},{2,3},{3,2},{4,5},{5,4},{6,7},{7,6},{8,9},{9,8},{10,11... | collective-permute-start | bytes 786440 | tf_op jit(solution)/shard_map/ppermute | solution.py:208
  17.9 1.6 tile_quarter.5
  19.5 1.6 tile_quarter.6
  21.0 1.9 collective-permute-start
  23.0 3.8 %collective-permute-start.2 = (f32[256,256]{1,0:T(8,128)S(1)}, f32[256,256]{1,0:T(8,128)S(1)}, u32[]{:S(2)}, u32[]{:S(2)}) collective-permute-start(f32[256,256]{1,0:T(8,128)S(1)} %add.13), channel_id=1, source_target_pairs={{0,2},{1,3},{2,0},{3,1},{4,6},{5,7},{6,4},{7,5},{8,10},{9,11},{10,... | collective-permute-start | bytes 786440 | tf_op jit(solution)/shard_map/ppermute | solution.py:208
  26.8 1.6 tile_quarter.7
  28.4 1.1 collective-permute-done
  29.5 4.8 %collective-permute-done.2 = f32[256,256]{1,0:T(8,128)S(1)} collective-permute-done((f32[256,256]{1,0:T(8,128)S(1)}, f32[256,256]{1,0:T(8,128)S(1)}, u32[]{:S(2)}, u32[]{:S(2)}) %collective-permute-start.2) | collective-permute-done | bytes 262176 | tf_op jit(solution)/shard_map/ppermute | solution.py:208
  34.3 26.9 %all_to_all.25 = f32[4,64,256]{2,1,0:T(8,128)S(1)} all-to-all(f32[4,64,256]{2,1,0:T(8,128)S(1)} %bitcast.8), channel_id=1, replica_groups=mesh['x'=4,'y'=4,'core'=2,'z3'=2,'z2'=2,'z1'=2,'z0'=2] {'z3','z2'}, dimensions={0} | all-to-all | bytes 524288 | tf_op jit(solution)/shard_map/all_to_all | solution.py:216
  61.2 16.2 %all_gather.3.quarter_ref = f32[256,256]{1,0:T(8,128)S(1)} all-gather(f32[64,256]{1,0:T(8,128)S(1)} %reduce_sum.46), channel_id=1, replica_groups=mesh['x'=4,'y'=4,'core'=2,'z3'=2,'z2'=2,'z1'=2,'z0'=2] {'z3','z2'}, dimensions={0}, use_global_device_ids=true | all-gather | bytes 327680 | tf_op jit(solution)/shard_map/all_gather | solution.py:242
  77.6 1.9 collective-permute-start.3
  79.5 3.8 %collective-permute-start.4 = (f32[256,256]{1,0:T(8,128)S(1)}, f32[256,256]{1,0:T(8,128)}, u32[]{:S(2)}, u32[]{:S(2)}) collective-permute-start(f32[256,256]{1,0:T(8,128)S(1)} %used_rows.1.rows_ref.refs_3_), channel_id=1, source_target_pairs={{0,1},{1,0},{2,3},{3,2},{4,5},{5,4},{6,7},{7,6},{8,9},{9,8},{10,11... | collective-permute-start | bytes 786440 | tf_op jit(solution)/shard_map/ppermute | solution.py:208
  83.6 20.9 %all_to_all.26 = f32[32,8,256]{2,1,0:T(8,128)} all-to-all(f32[32,8,256]{2,1,0:T(8,128)S(1)} %bitcast.6), channel_id=1, replica_groups=mesh['x'=4,'y'=4,'core'=2,'z3'=2,'z2'=2,'z1'=2,'z0'=2] {'x','y','core'}, dimensions={0} | all-to-all | bytes 524288 | tf_op jit(solution)/shard_map/all_to_all | solution.py:216
  104.5 1.0 reduce_sum.47
  105.5 0.6 broadcast_in_dim.6
  106.1 3.9 %all-to-all-start.2 = ((f32[4,8,256]{2,1,0:T(8,128)}), f32[4,8,256]{2,1,0:T(8,128)S(1)}, u32[]{:S(2)}, u32[]{:S(2)}) async-start(f32[4,8,256]{2,1,0:T(8,128)} %broadcast_in_dim.6), calls=%async_computation.2 | async-start | bytes 65536 | tf_op jit(solution)/shard_map/all_to_all | solution.py:216
  110.0 1.9 collective-permute-start.5
  112.0 2.6 %all-to-all-done.2 = f32[4,8,256]{2,1,0:T(8,128)S(1)} async-done(((f32[4,8,256]{2,1,0:T(8,128)}), f32[4,8,256]{2,1,0:T(8,128)S(1)}, u32[]{:S(2)}, u32[]{:S(2)}) %all-to-all-start.2) | async-done | bytes 32800 | tf_op jit(solution)/shard_map/all_to_all | solution.py:216
  114.5 0.7 broadcast_in_dim.7
  115.3 5.3 %all-to-all-start.3 = ((f32[32,8,256]{2,1,0:T(8,128)}), f32[32,8,256]{2,1,0:T(8,128)S(1)}, u32[]{:S(2)}, u32[]{:S(2)}) async-start(f32[32,8,256]{2,1,0:T(8,128)} %broadcast_in_dim.7), calls=%async_computation.3 | async-start | bytes 524288 | tf_op jit(solution)/shard_map/all_to_all | solution.py:216
  120.6 0.6 reduce_sum.45
  121.9 7.7 %all-to-all-done.3 = f32[32,8,256]{2,1,0:T(8,128)S(1)} async-done(((f32[32,8,256]{2,1,0:T(8,128)}), f32[32,8,256]{2,1,0:T(8,128)S(1)}, u32[]{:S(2)}, u32[]{:S(2)}) %all-to-all-start.3) | async-done | bytes 262176 | tf_op jit(solution)/shard_map/all_to_all | solution.py:216
  129.6 0.9 copy-done.4
  130.5 63.4 %basis_and_coeffs.1 = (f32[1024,256]{1,0:T(8,128)}, f32[16,8,1536]{2,1,0:T(8,128)S(1)}, f32[16,8,1536]{2,1,0:T(8,128)S(1)}) custom-call(f32[1,1]{1,0:T(1,128)} %bitcast.total_ref, f32[256,256]{1,0:T(8,128)S(1)} %bitcast.5, f32[256,256]{1,0:T(8,128)} %collective-permute-done.5.refs_0_, f32[256,256]{1,0:T(8,128)} %collective-permute-done.4.refs_1_, ...), custom_call_target="tpu_custom_call" | custom-call | flops 1000000000 | bytes 1048576 | tf_op jit(solution)/shard_map/basis_and_coeffs/pallas_call | solution.py:56
  193.9 2.1 collective-permute-start.6
  196.0 2.1 collective-permute-done.6
  198.2 16.0 %all_to_all.27 = f32[16,8,1536]{2,1,0:T(8,128)S(1)} all-to-all(f32[16,8,1536]{2,1,0:T(8,128)S(1)} %add.15), channel_id=1, replica_groups=mesh['x'=4,'y'=4,'core'=2,'z3'=2,'z2'=2,'z1'=2,'z0'=2] {'x','y'}, dimensions={0} | all-to-all | bytes 1572864 | tf_op jit(solution)/shard_map/all_to_all | solution.py:216
  214.2 0.7 reduce_sum.49
  (19 shorter events, 0.6 us)
Async XLA Ops:
  0.6 1.4 copy-start
  2.0 1.2 copy-start.1
  3.3 1.1 copy-start.2
  6.0 17.0 %collective-permute-start.1 = (f32[256,256]{1,0:T(8,128)S(1)}, f32[256,256]{1,0:T(8,128)S(1)}, u32[]{:S(2)}, u32[]{:S(2)}) collective-permute-start(f32[256,256]{1,0:T(8,128)S(1)} %get-tuple-element.22), channel_id=1, source_target_pairs={{0,1},{1,0},{2,3},{3,2},{4,5},{5,4},{6,7},{7,6},{8,9},{9,8},{10,11... | collective-permute-start | bytes 786440 | tf_op jit(solution)/shard_map/ppermute | solution.py:208
  21.0 8.5 %collective-permute-start = (f32[256,256]{1,0:T(8,128)S(1)}, f32[256,256]{1,0:T(8,128)S(1)}, u32[]{:S(2)}, u32[]{:S(2)}) collective-permute-start(f32[256,256]{1,0:T(8,128)S(1)} %get-tuple-element.20), channel_id=1, source_target_pairs={{0,1},{1,0},{2,3},{3,2},{4,5},{5,4},{6,7},{7,6},{8,9},{9,8},{10,11... | collective-permute-start | bytes 786440 | tf_op jit(solution)/shard_map/ppermute | solution.py:208
  23.0 11.2 %collective-permute-start.2 = (f32[256,256]{1,0:T(8,128)S(1)}, f32[256,256]{1,0:T(8,128)S(1)}, u32[]{:S(2)}, u32[]{:S(2)}) collective-permute-start(f32[256,256]{1,0:T(8,128)S(1)} %add.13), channel_id=1, source_target_pairs={{0,2},{1,3},{2,0},{3,1},{4,6},{5,7},{6,4},{7,5},{8,10},{9,11},{10,... | collective-permute-start | bytes 786440 | tf_op jit(solution)/shard_map/ppermute | solution.py:208
  26.8 50.6 %copy-start.5 = (s32[32]{0:T(128)S(1)}, s32[32]{0:T(128)}, u32[]{:S(2)}) copy-start(s32[32]{0:T(128)} %param.7) | copy-start | bytes 388
  77.6 37.7 %copy-start.3 = (f32[256,256]{1,0:T(8,128)}, f32[256,256]{1,0:T(8,128)S(1)}, u32[]{:S(2)}) copy-start(f32[256,256]{1,0:T(8,128)S(1)} %used_rows.1.rows_ref.refs_3_) | copy-start | bytes 786436
  77.6 27.9 %collective-permute-start.3 = (f32[256,256]{1,0:T(8,128)S(1)}, f32[256,256]{1,0:T(8,128)}, u32[]{:S(2)}, u32[]{:S(2)}) collective-permute-start(f32[256,256]{1,0:T(8,128)S(1)} %used_rows.1.rows_ref.refs_3_), channel_id=1, source_target_pairs={{0,2},{1,3},{2,0},{3,1},{4,6},{5,7},{6,4},{7,5},{8,10},{9,11},{10,... | collective-permute-start | bytes 786440 | tf_op jit(solution)/shard_map/ppermute | solution.py:208
  79.5 26.0 %collective-permute-start.4 = (f32[256,256]{1,0:T(8,128)S(1)}, f32[256,256]{1,0:T(8,128)}, u32[]{:S(2)}, u32[]{:S(2)}) collective-permute-start(f32[256,256]{1,0:T(8,128)S(1)} %used_rows.1.rows_ref.refs_3_), channel_id=1, source_target_pairs={{0,1},{1,0},{2,3},{3,2},{4,5},{5,4},{6,7},{7,6},{8,9},{9,8},{10,11... | collective-permute-start | bytes 786440 | tf_op jit(solution)/shard_map/ppermute | solution.py:208
  106.1 8.4 %all-to-all-start.2 = ((f32[4,8,256]{2,1,0:T(8,128)}), f32[4,8,256]{2,1,0:T(8,128)S(1)}, u32[]{:S(2)}, u32[]{:S(2)}) async-start(f32[4,8,256]{2,1,0:T(8,128)} %broadcast_in_dim.6), calls=%async_computation.2 | async-start | bytes 65536 | tf_op jit(solution)/shard_map/all_to_all | solution.py:216
  110.0 11.8 %collective-permute-start.5 = (f32[256,256]{1,0:T(8,128)}, f32[256,256]{1,0:T(8,128)}, u32[]{:S(2)}, u32[]{:S(2)}) collective-permute-start(f32[256,256]{1,0:T(8,128)} %collective-permute-done.3.refs_2_), channel_id=1, source_target_pairs={{0,1},{1,0},{2,3},{3,2},{4,5},{5,4},{6,7},{7,6},{8,9},{9,8},{10,11... | collective-permute-start | bytes 786440 | tf_op jit(solution)/shard_map/ppermute | solution.py:208
  115.3 14.3 %all-to-all-start.3 = ((f32[32,8,256]{2,1,0:T(8,128)}), f32[32,8,256]{2,1,0:T(8,128)S(1)}, u32[]{:S(2)}, u32[]{:S(2)}) async-start(f32[32,8,256]{2,1,0:T(8,128)} %broadcast_in_dim.7), calls=%async_computation.3 | async-start | bytes 524288 | tf_op jit(solution)/shard_map/all_to_all | solution.py:216
  129.6 1.0 copy-start.4
  193.9 4.2 %collective-permute-start.6 = (f32[16,8,1536]{2,1,0:T(8,128)S(1)}, f32[16,8,1536]{2,1,0:T(8,128)S(1)}, u32[]{:S(2)}, u32[]{:S(2)}) collective-permute-start(f32[16,8,1536]{2,1,0:T(8,128)S(1)} %get-tuple-element.29), channel_id=1, source_target_pairs={{0,16},{16,0},{1,17},{17,1},{2,18},{18,2},{3,19},{19,3},{4,20},{20... | collective-permute-start | bytes 2359304 | tf_op jit(solution)/shard_map/ppermute | solution.py:212

commit v10 on v9

--- a/solution.py
+++ b/solution.py
@@ -74,6 +74,11 @@
     return 2 * low + (second + 1 - (order - 2)) % 2
 
 
+def partner(place, reach):
+    places, shift = lax.axis_size(LIGHT), lax.axis_index("core") * reach
+    return (((place - shift + places) % places ^ reach) + shift) % places
+
+
 def split(value):
     high = value.astype(BF16)
     return high, (value - high.astype(F32)).astype(BF16)
@@ -86,13 +91,24 @@
 
 def tile_kernel(tex_ref, light_ref, sketch_ref, *refs, order, step=128):
     tile_ref, part_ref = refs[-2:]
-    rows = part_ref.shape[0]
+    rows, groups = part_ref.shape[0], lax.axis_size(FAR)
+    share = rows // groups
     first = quarter_of(order) * rows
+    holder = lax.axis_index(LIGHT)
+    if order < 2:
+        holder = partner(holder, 1)
+    if order % 2 == 0:
+        holder = partner(holder, 2)
+    holder = holder // (lax.axis_size(LIGHT) // groups)
+    onward = 1 - 2 * lax.axis_index("core")
     for at in range(0, rows, step):
         tex = tex_ref[pl.ds(pl.multiple_of(first + at, step), step), :]
         tile = sine(dot(tex, light_ref[...], (1, 1))).astype(BF16)
         tile_ref[order * rows + at : order * rows + at + step, :] = tile
-        part_ref[at : at + step, :] = dot(tile, sketch_ref[...], (1, 0))
+        part = dot(tile, sketch_ref[...], (1, 0))
+        for i in range(step // share):
+            turn = (onward * (at // share + i - holder) + groups) % groups
+            part_ref[pl.ds(pl.multiple_of(turn * share, share), share), :] = part[i * share : (i + 1) * share, :]
 
 
 def tile_call(order, tex, light, sketch, *tiles):
@@ -208,6 +224,12 @@
     return lax.ppermute(value, ("core", *LIGHT), light_pairs(lax.axis_size(LIGHT), reach))
 
 
+def onward(value, turn):
+    count = lax.axis_size(LIGHT)
+    pairs = [(c * count + z, c * count + (z + 4 * turn * (1 - 2 * c)) % count) for c in range(2) for z in range(count)]
+    return lax.ppermute(value, ("core", *LIGHT), pairs)
+
+
 def across_cores(value):
     return lax.ppermute(value, "core", [(0, 1), (1, 0)])
 
@@ -236,7 +258,9 @@
     passed = across(turned + passing, 2)
     tiles, part = tile_call(3, *inputs, tiles)
     quarter = part + staying + passed
-    share = jnp.sum(each_to_each(quarter.reshape(places // 4, share_rows, width), FAR), axis=0)
+    own, following, opposite, previous = quarter.reshape(4, share_rows, width)
+    arrived, third = onward(opposite, 1), onward(previous, -1)
+    share = own + third + onward(following + arrived, 1)
 
     square = (width, width)
     quarter = lax.all_gather(share, FAR, axis=0, tiled=True)

time: 216 us -> 213 us (0.986)
  blocking collectives: 80.1 us -> 56.4 us
  starting transfers between devices: 36.6 us -> 53.3 us
  waiting for transfers between devices: 18.3 us -> 22.5 us
    all_to_all x3 -> x2, blocking collectives: 63.9 us -> 39.1 us  [each_to_each(): return lax.all_to_all(parts, axes, 0, 0, tiled=True)]
    ppermute x0 -> x3, starting transfers between devices: none -> 15.4 us  [onward(): return lax.ppermute(value, ('core', *LIGHT), pairs)]
    ppermute x0 -> x3, waiting for transfers between devices: none -> 4.52 us  [onward(): return lax.ppermute(value, ('core', *LIGHT), pairs)]
  transfers between devices with their start and end apart: 9 -> 12, of which waited for: 5 -> 6; matrix products, arithmetic and copies ran while one was open for 1% -> 1% of each run, Pallas kernels for 2% -> 2%
where the time goes in v10:
time: 213 us; the launch traced here: 212 us
  Pallas kernels  70 us (33%)
  blocking collectives  56.4 us (26%)
  starting transfers between devices  53.3 us (25%)
  waiting for transfers between devices  22.5 us (11%)
  local copies, waits for them, and re-layouts  6.07 us (3%)
  other arithmetic  2.49 us (1%)
    pallas_call x7, Pallas kernels, on_core(): pl.pallas_call(kernel, out_shape=out_shape, in_specs=[VMEM] * len(operand...  70 us
    all_to_all x2, blocking collectives, each_to_each(): return lax.all_to_all(parts, axes, 0, 0, tiled=True)  39.1 us
    ppermute x6, starting transfers between devices, across(): lax.ppermute(value, ('core', *LIGHT), light_pairs(lax.axis_size(LIGHT), r...  26.6 us
    all_gather x1, blocking collectives, on_device(): quarter = lax.all_gather(share, FAR, axis=0, tiled=True)  17.3 us
    ppermute x3, starting transfers between devices, onward(): return lax.ppermute(value, ('core', *LIGHT), pairs)  15.4 us
    all_to_all x2, waiting for transfers between devices, each_to_each(): return lax.all_to_all(parts, axes, 0, 0, tiled=True)  10.1 us
    all_to_all x2, starting transfers between devices, each_to_each(): return lax.all_to_all(parts, axes, 0, 0, tiled=True)  9.21 us
    ppermute x6, waiting for transfers between devices, across(): lax.ppermute(value, ('core', *LIGHT), light_pairs(lax.axis_size(LIGHT), r...  5.88 us
  transfers between devices with their start and end apart: 12, of which 6 were waited for; matrix products, arithmetic and copies ran while one was open for 1% of the time, Pallas kernels for 2%

profile of v10, /device:TPU:1, one launch (start us, length us, event | category | flops | bytes accessed | tf_op | source)
XLA Modules:
  0.0 212.3 jit_solution(10198929702052842706)
XLA Ops:
  0.6 1.4 copy-done
  2.0 1.2 copy-done.1
  3.3 1.1 copy-done.2
  4.4 1.6 tile_quarter.4
  6.0 11.9 %collective-permute-start.1 = (f32[256,256]{1,0:T(8,128)S(1)}, f32[256,256]{1,0:T(8,128)S(1)}, u32[]{:S(2)}, u32[]{:S(2)}) collective-permute-start(f32[256,256]{1,0:T(8,128)S(1)} %get-tuple-element.22), channel_id=1, source_target_pairs={{0,1},{1,0},{2,3},{3,2},{4,5},{5,4},{6,7},{7,6},{8,9},{9,8},{10,11... | collective-permute-start | bytes 786440 | tf_op jit(solution)/shard_map/ppermute | solution.py:224
  17.9 1.6 tile_quarter.5
  19.5 1.6 tile_quarter.6
  21.0 1.9 collective-permute-start
  23.0 3.8 %collective-permute-start.2 = (f32[256,256]{1,0:T(8,128)S(1)}, f32[256,256]{1,0:T(8,128)S(1)}, u32[]{:S(2)}, u32[]{:S(2)}) collective-permute-start(f32[256,256]{1,0:T(8,128)S(1)} %add.22), channel_id=1, source_target_pairs={{0,2},{1,3},{2,0},{3,1},{4,6},{5,7},{6,4},{7,5},{8,10},{9,11},{10,... | collective-permute-start | bytes 786440 | tf_op jit(solution)/shard_map/ppermute | solution.py:224
  26.8 1.6 tile_quarter.7
  28.4 1.1 collective-permute-done
  29.5 4.8 %collective-permute-done.2 = f32[256,256]{1,0:T(8,128)S(1)} collective-permute-done((f32[256,256]{1,0:T(8,128)S(1)}, f32[256,256]{1,0:T(8,128)S(1)}, u32[]{:S(2)}, u32[]{:S(2)}) %collective-permute-start.2) | collective-permute-done | bytes 262176 | tf_op jit(solution)/shard_map/ppermute | solution.py:224
  34.3 6.1 %collective-permute-start.4 = (f32[64,256]{1,0:T(8,128)S(1)}, f32[64,256]{1,0:T(8,128)S(1)}, u32[]{:S(2)}, u32[]{:S(2)}) collective-permute-start(f32[64,256]{1,0:T(8,128)S(1)} %get-tuple-element.31), channel_id=1, source_target_pairs={{0,4},{1,5},{2,6},{3,7},{4,8},{5,9},{6,10},{7,11},{8,12},{9,13},{1... | collective-permute-start | bytes 196616 | tf_op jit(solution)/shard_map/ppermute | solution.py:230
  40.5 3.0 %collective-permute-start.3 = (f32[64,256]{1,0:T(8,128)S(1)}, f32[64,256]{1,0:T(8,128)S(1)}, u32[]{:S(2)}, u32[]{:S(2)}) collective-permute-start(f32[64,256]{1,0:T(8,128)S(1)} %get-tuple-element.30), channel_id=1, source_target_pairs={{0,12},{1,13},{2,14},{3,15},{4,0},{5,1},{6,2},{7,3},{8,4},{9,5},{1... | collective-permute-start | bytes 196616 | tf_op jit(solution)/shard_map/ppermute | solution.py:230
  43.6 6.2 %collective-permute-start.5 = (f32[64,256]{1,0:T(8,128)S(1)}, f32[64,256]{1,0:T(8,128)S(1)}, u32[]{:S(2)}, u32[]{:S(2)}) collective-permute-start(f32[64,256]{1,0:T(8,128)S(1)} %slice_add_fusion), channel_id=1, source_target_pairs={{0,4},{1,5},{2,6},{3,7},{4,8},{5,9},{6,10},{7,11},{8,12},{9,13},{1... | collective-permute-start | bytes 196616 | tf_op jit(solution)/shard_map/ppermute | solution.py:230
  49.8 4.5 %collective-permute-done.5 = f32[64,256]{1,0:T(8,128)S(1)} collective-permute-done((f32[64,256]{1,0:T(8,128)S(1)}, f32[64,256]{1,0:T(8,128)S(1)}, u32[]{:S(2)}, u32[]{:S(2)}) %collective-permute-start.5) | collective-permute-done | bytes 65568 | tf_op jit(solution)/shard_map/ppermute | solution.py:230
  54.3 17.3 %all_gather.3.quarter_ref = f32[256,256]{1,0:T(8,128)S(1)} all-gather(f32[64,256]{1,0:T(8,128)S(1)} %fusion), channel_id=1, replica_groups=mesh['x'=4,'y'=4,'core'=2,'z3'=2,'z2'=2,'z1'=2,'z0'=2] {'z3','z2'}, dimensions={0}, use_global_device_ids=true | all-gather | bytes 327680 | tf_op jit(solution)/shard_map/all_gather | solution.py:266
  71.8 1.9 collective-permute-start.6
  73.7 4.9 %collective-permute-start.7 = (f32[256,256]{1,0:T(8,128)S(1)}, f32[256,256]{1,0:T(8,128)}, u32[]{:S(2)}, u32[]{:S(2)}) collective-permute-start(f32[256,256]{1,0:T(8,128)S(1)} %used_rows.1.rows_ref.refs_3_), channel_id=1, source_target_pairs={{0,1},{1,0},{2,3},{3,2},{4,5},{5,4},{6,7},{7,6},{8,9},{9,8},{10,11... | collective-permute-start | bytes 786440 | tf_op jit(solution)/shard_map/ppermute | solution.py:224
  78.9 23.0 %all_to_all.20 = f32[32,8,256]{2,1,0:T(8,128)} all-to-all(f32[32,8,256]{2,1,0:T(8,128)S(1)} %bitcast.5), channel_id=1, replica_groups=mesh['x'=4,'y'=4,'core'=2,'z3'=2,'z2'=2,'z1'=2,'z0'=2] {'x','y','core'}, dimensions={0} | all-to-all | bytes 524288 | tf_op jit(solution)/shard_map/all_to_all | solution.py:238
  101.9 1.0 reduce_sum.37
  103.6 3.9 %all-to-all-start.1 = ((f32[4,8,256]{2,1,0:T(8,128)}), f32[4,8,256]{2,1,0:T(8,128)S(1)}, u32[]{:S(2)}, u32[]{:S(2)}) async-start(f32[4,8,256]{2,1,0:T(8,128)} %broadcast_in_dim.6), calls=%async_computation.1 | async-start | bytes 65536 | tf_op jit(solution)/shard_map/all_to_all | solution.py:238
  107.5 2.1 %collective-permute-start.8 = (f32[256,256]{1,0:T(8,128)}, f32[256,256]{1,0:T(8,128)}, u32[]{:S(2)}, u32[]{:S(2)}) collective-permute-start(f32[256,256]{1,0:T(8,128)} %collective-permute-done.6.refs_2_), channel_id=1, source_target_pairs={{0,1},{1,0},{2,3},{3,2},{4,5},{5,4},{6,7},{7,6},{8,9},{9,8},{10,11... | collective-permute-start | bytes 786440 | tf_op jit(solution)/shard_map/ppermute | solution.py:224
  109.6 2.4 %all-to-all-done.1 = f32[4,8,256]{2,1,0:T(8,128)S(1)} async-done(((f32[4,8,256]{2,1,0:T(8,128)}), f32[4,8,256]{2,1,0:T(8,128)S(1)}, u32[]{:S(2)}, u32[]{:S(2)}) %all-to-all-start.1) | async-done | bytes 32800 | tf_op jit(solution)/shard_map/all_to_all | solution.py:238
  112.0 0.7 broadcast_in_dim.7
  112.7 5.3 %all-to-all-start.2 = ((f32[32,8,256]{2,1,0:T(8,128)}), f32[32,8,256]{2,1,0:T(8,128)S(1)}, u32[]{:S(2)}, u32[]{:S(2)}) async-start(f32[32,8,256]{2,1,0:T(8,128)} %broadcast_in_dim.7), calls=%async_computation.2 | async-start | bytes 524288 | tf_op jit(solution)/shard_map/all_to_all | solution.py:238
  119.3 7.7 %all-to-all-done.2 = f32[32,8,256]{2,1,0:T(8,128)S(1)} async-done(((f32[32,8,256]{2,1,0:T(8,128)}), f32[32,8,256]{2,1,0:T(8,128)S(1)}, u32[]{:S(2)}, u32[]{:S(2)}) %all-to-all-start.2) | async-done | bytes 262176 | tf_op jit(solution)/shard_map/all_to_all | solution.py:238
  127.0 0.9 copy-done.4
  128.0 63.4 %basis_and_coeffs.1 = (f32[1024,256]{1,0:T(8,128)}, f32[16,8,1536]{2,1,0:T(8,128)S(1)}, f32[16,8,1536]{2,1,0:T(8,128)S(1)}) custom-call(f32[1,1]{1,0:T(1,128)} %bitcast.total_ref, f32[256,256]{1,0:T(8,128)S(1)} %bitcast.4, f32[256,256]{1,0:T(8,128)} %collective-permute-done.8.refs_0_, f32[256,256]{1,0:T(8,128)} %collective-permute-done.7.refs_1_, ...), custom_call_target="tpu_custom_call" | custom-call | flops 1000000000 | bytes 1048576 | tf_op jit(solution)/shard_map/basis_and_coeffs/pallas_call | solution.py:56
  191.4 2.1 collective-permute-start.9
  193.4 2.1 collective-permute-done.9
  195.6 16.0 %all_to_all.21 = f32[16,8,1536]{2,1,0:T(8,128)S(1)} all-to-all(f32[16,8,1536]{2,1,0:T(8,128)S(1)} %add.27), channel_id=1, replica_groups=mesh['x'=4,'y'=4,'core'=2,'z3'=2,'z2'=2,'z1'=2,'z0'=2] {'x','y'}, dimensions={0} | all-to-all | bytes 1572864 | tf_op jit(solution)/shard_map/all_to_all | solution.py:238
  (26 shorter events, 2.6 us)
Async XLA Ops:
  0.6 1.4 copy-start
  2.0 1.2 copy-start.1
  3.3 1.1 copy-start.2
  6.0 17.0 %collective-permute-start.1 = (f32[256,256]{1,0:T(8,128)S(1)}, f32[256,256]{1,0:T(8,128)S(1)}, u32[]{:S(2)}, u32[]{:S(2)}) collective-permute-start(f32[256,256]{1,0:T(8,128)S(1)} %get-tuple-element.22), channel_id=1, source_target_pairs={{0,1},{1,0},{2,3},{3,2},{4,5},{5,4},{6,7},{7,6},{8,9},{9,8},{10,11... | collective-permute-start | bytes 786440 | tf_op jit(solution)/shard_map/ppermute | solution.py:224
  21.0 8.5 %collective-permute-start = (f32[256,256]{1,0:T(8,128)S(1)}, f32[256,256]{1,0:T(8,128)S(1)}, u32[]{:S(2)}, u32[]{:S(2)}) collective-permute-start(f32[256,256]{1,0:T(8,128)S(1)} %get-tuple-element.20), channel_id=1, source_target_pairs={{0,1},{1,0},{2,3},{3,2},{4,5},{5,4},{6,7},{7,6},{8,9},{9,8},{10,11... | collective-permute-start | bytes 786440 | tf_op jit(solution)/shard_map/ppermute | solution.py:224
  23.0 11.2 %collective-permute-start.2 = (f32[256,256]{1,0:T(8,128)S(1)}, f32[256,256]{1,0:T(8,128)S(1)}, u32[]{:S(2)}, u32[]{:S(2)}) collective-permute-start(f32[256,256]{1,0:T(8,128)S(1)} %add.22), channel_id=1, source_target_pairs={{0,2},{1,3},{2,0},{3,1},{4,6},{5,7},{6,4},{7,5},{8,10},{9,11},{10,... | collective-permute-start | bytes 786440 | tf_op jit(solution)/shard_map/ppermute | solution.py:224
  26.8 44.8 %copy-start.5 = (s32[32]{0:T(128)S(1)}, s32[32]{0:T(128)}, u32[]{:S(2)}) copy-start(s32[32]{0:T(128)} %param.7) | copy-start | bytes 388
  34.3 9.2 %collective-permute-start.4 = (f32[64,256]{1,0:T(8,128)S(1)}, f32[64,256]{1,0:T(8,128)S(1)}, u32[]{:S(2)}, u32[]{:S(2)}) collective-permute-start(f32[64,256]{1,0:T(8,128)S(1)} %get-tuple-element.31), channel_id=1, source_target_pairs={{0,4},{1,5},{2,6},{3,7},{4,8},{5,9},{6,10},{7,11},{8,12},{9,13},{1... | collective-permute-start | bytes 196616 | tf_op jit(solution)/shard_map/ppermute | solution.py:230
  40.5 9.3 %collective-permute-start.3 = (f32[64,256]{1,0:T(8,128)S(1)}, f32[64,256]{1,0:T(8,128)S(1)}, u32[]{:S(2)}, u32[]{:S(2)}) collective-permute-start(f32[64,256]{1,0:T(8,128)S(1)} %get-tuple-element.30), channel_id=1, source_target_pairs={{0,12},{1,13},{2,14},{3,15},{4,0},{5,1},{6,2},{7,3},{8,4},{9,5},{1... | collective-permute-start | bytes 196616 | tf_op jit(solution)/shard_map/ppermute | solution.py:230
  43.6 10.7 %collective-permute-start.5 = (f32[64,256]{1,0:T(8,128)S(1)}, f32[64,256]{1,0:T(8,128)S(1)}, u32[]{:S(2)}, u32[]{:S(2)}) collective-permute-start(f32[64,256]{1,0:T(8,128)S(1)} %slice_add_fusion), channel_id=1, source_target_pairs={{0,4},{1,5},{2,6},{3,7},{4,8},{5,9},{6,10},{7,11},{8,12},{9,13},{1... | collective-permute-start | bytes 196616 | tf_op jit(solution)/shard_map/ppermute | solution.py:230
  71.8 40.9 %copy-start.3 = (f32[256,256]{1,0:T(8,128)}, f32[256,256]{1,0:T(8,128)S(1)}, u32[]{:S(2)}) copy-start(f32[256,256]{1,0:T(8,128)S(1)} %used_rows.1.rows_ref.refs_3_) | copy-start | bytes 786436
  71.8 31.1 %collective-permute-start.6 = (f32[256,256]{1,0:T(8,128)S(1)}, f32[256,256]{1,0:T(8,128)}, u32[]{:S(2)}, u32[]{:S(2)}) collective-permute-start(f32[256,256]{1,0:T(8,128)S(1)} %used_rows.1.rows_ref.refs_3_), channel_id=1, source_target_pairs={{0,2},{1,3},{2,0},{3,1},{4,6},{5,7},{6,4},{7,5},{8,10},{9,11},{10,... | collective-permute-start | bytes 786440 | tf_op jit(solution)/shard_map/ppermute | solution.py:224
  73.7 29.2 %collective-permute-start.7 = (f32[256,256]{1,0:T(8,128)S(1)}, f32[256,256]{1,0:T(8,128)}, u32[]{:S(2)}, u32[]{:S(2)}) collective-permute-start(f32[256,256]{1,0:T(8,128)S(1)} %used_rows.1.rows_ref.refs_3_), channel_id=1, source_target_pairs={{0,1},{1,0},{2,3},{3,2},{4,5},{5,4},{6,7},{7,6},{8,9},{9,8},{10,11... | collective-permute-start | bytes 786440 | tf_op jit(solution)/shard_map/ppermute | solution.py:224
  103.6 8.4 %all-to-all-start.1 = ((f32[4,8,256]{2,1,0:T(8,128)}), f32[4,8,256]{2,1,0:T(8,128)S(1)}, u32[]{:S(2)}, u32[]{:S(2)}) async-start(f32[4,8,256]{2,1,0:T(8,128)} %broadcast_in_dim.6), calls=%async_computation.1 | async-start | bytes 65536 | tf_op jit(solution)/shard_map/all_to_all | solution.py:238
  107.5 11.8 %collective-permute-start.8 = (f32[256,256]{1,0:T(8,128)}, f32[256,256]{1,0:T(8,128)}, u32[]{:S(2)}, u32[]{:S(2)}) collective-permute-start(f32[256,256]{1,0:T(8,128)} %collective-permute-done.6.refs_2_), channel_id=1, source_target_pairs={{0,1},{1,0},{2,3},{3,2},{4,5},{5,4},{6,7},{7,6},{8,9},{9,8},{10,11... | collective-permute-start | bytes 786440 | tf_op jit(solution)/shard_map/ppermute | solution.py:224
  112.7 14.3 %all-to-all-start.2 = ((f32[32,8,256]{2,1,0:T(8,128)}), f32[32,8,256]{2,1,0:T(8,128)S(1)}, u32[]{:S(2)}, u32[]{:S(2)}) async-start(f32[32,8,256]{2,1,0:T(8,128)} %broadcast_in_dim.7), calls=%async_computation.2 | async-start | bytes 524288 | tf_op jit(solution)/shard_map/all_to_all | solution.py:238
  127.0 1.0 copy-start.4
  191.4 4.2 %collective-permute-start.9 = (f32[16,8,1536]{2,1,0:T(8,128)S(1)}, f32[16,8,1536]{2,1,0:T(8,128)S(1)}, u32[]{:S(2)}, u32[]{:S(2)}) collective-permute-start(f32[16,8,1536]{2,1,0:T(8,128)S(1)} %get-tuple-element.29), channel_id=1, source_target_pairs={{0,16},{16,0},{1,17},{17,1},{2,18},{18,2},{3,19},{19,3},{4,20},{20... | collective-permute-start | bytes 2359304 | tf_op jit(solution)/shard_map/ppermute | solution.py:234

commit v11 on v10

--- a/solution.py
+++ b/solution.py
@@ -267,11 +267,11 @@
     quarter = on_core(mask_kernel, jax.ShapeDtypeStruct(quarter.shape, F32), "used_rows")(
         row_counts.reshape(1, texels), quarter
     )
-    near, beside = across(quarter, 2), across(quarter, 1)
+    near = across(quarter, 2)
     gram = on_core(gram_kernel, jax.ShapeDtypeStruct(square, F32), "gram_part")(quarter)
     gram_rows = jnp.sum(each_to_each(gram.reshape(texels, width // texels, width), TEXEL), axis=0)
-    gram_rows, near, beside = lax.optimization_barrier((gram_rows, near, beside))
-    beyond = across(near, 1)
+    gram_rows, near, quarter = lax.optimization_barrier((gram_rows, near, quarter))
+    beyond, beside = across(near, 1), across(quarter, 1)
     gram_rows = jnp.sum(to_each(gram_rows, ("z1", "z0")), axis=0)
     gram = to_each(gram_rows, TEXEL).reshape(square)
 

time: 213 us -> 211 us (level)
  waiting for transfers between devices: 22.5 us -> 20 us
  blocking collectives: 56.4 us -> 58.7 us
    all_to_all x2, waiting for transfers between devices: 10.1 us -> 7.49 us  [each_to_each(): return lax.all_to_all(parts, axes, 0, 0, tiled=True)]
    all_to_all x2, blocking collectives: 39.1 us -> 41.3 us  [each_to_each(): return lax.all_to_all(parts, axes, 0, 0, tiled=True)]
    unnamed x12 -> x8, local copies, waits for them, and re-layouts: 4.72 us -> 3.76 us
  transfers between devices with their start and end apart: 12 -> 12, of which waited for: 6 -> 5; matrix products, arithmetic and copies ran while one was open for 1% -> 1% of each run, Pallas kernels for 2% -> 3%
where the time goes in v11:
time: 211 us; the launch traced here: 210 us
  Pallas kernels  71.8 us (34%)
  blocking collectives  58.7 us (28%)
  starting transfers between devices  51.2 us (24%)
  waiting for transfers between devices  20 us (9%)
  local copies, waits for them, and re-layouts  5.11 us (2%)
    pallas_call x7, Pallas kernels, on_core(): pl.pallas_call(kernel, out_shape=out_shape, in_specs=[VMEM] * len(operand...  71.8 us
    all_to_all x2, blocking collectives, each_to_each(): return lax.all_to_all(parts, axes, 0, 0, tiled=True)  41.3 us
    ppermute x6, starting transfers between devices, across(): lax.ppermute(value, ('core', *LIGHT), light_pairs(lax.axis_size(LIGHT), r...  26.1 us
    all_gather x1, blocking collectives, on_device(): quarter = lax.all_gather(share, FAR, axis=0, tiled=True)  17.3 us
    ppermute x3, starting transfers between devices, onward(): return lax.ppermute(value, ('core', *LIGHT), pairs)  15.4 us
    all_to_all x2, starting transfers between devices, each_to_each(): return lax.all_to_all(parts, axes, 0, 0, tiled=True)  7.64 us
    all_to_all x2, waiting for transfers between devices, each_to_each(): return lax.all_to_all(parts, axes, 0, 0, tiled=True)  7.49 us
    ppermute x6, waiting for transfers between devices, across(): lax.ppermute(value, ('core', *LIGHT), light_pairs(lax.axis_size(LIGHT), r...  5.88 us
  transfers between devices with their start and end apart: 12, of which 5 were waited for; matrix products, arithmetic and copies ran while one was open for 1% of the time, Pallas kernels for 3%

profile of v11, /device:TPU:1, one launch (start us, length us, event | category | flops | bytes accessed | tf_op | source)
XLA Modules:
  0.0 209.7 jit_solution(15803605990455730586)
XLA Ops:
  0.6 1.4 copy-done
  2.0 1.2 copy-done.1
  3.3 1.1 copy-done.2
  4.4 1.6 tile_quarter.4
  6.0 11.9 %collective-permute-start.1 = (f32[256,256]{1,0:T(8,128)S(1)}, f32[256,256]{1,0:T(8,128)S(1)}, u32[]{:S(2)}, u32[]{:S(2)}) collective-permute-start(f32[256,256]{1,0:T(8,128)S(1)} %get-tuple-element.22), channel_id=1, source_target_pairs={{0,1},{1,0},{2,3},{3,2},{4,5},{5,4},{6,7},{7,6},{8,9},{9,8},{10,11... | collective-permute-start | bytes 786440 | tf_op jit(solution)/shard_map/ppermute | solution.py:224
  17.9 1.6 tile_quarter.5
  19.5 1.6 tile_quarter.6
  21.0 1.9 collective-permute-start
  23.0 3.8 %collective-permute-start.2 = (f32[256,256]{1,0:T(8,128)S(1)}, f32[256,256]{1,0:T(8,128)S(1)}, u32[]{:S(2)}, u32[]{:S(2)}) collective-permute-start(f32[256,256]{1,0:T(8,128)S(1)} %add.22), channel_id=1, source_target_pairs={{0,2},{1,3},{2,0},{3,1},{4,6},{5,7},{6,4},{7,5},{8,10},{9,11},{10,... | collective-permute-start | bytes 786440 | tf_op jit(solution)/shard_map/ppermute | solution.py:224
  26.8 1.6 tile_quarter.7
  28.4 1.1 collective-permute-done
  29.5 4.8 %collective-permute-done.2 = f32[256,256]{1,0:T(8,128)S(1)} collective-permute-done((f32[256,256]{1,0:T(8,128)S(1)}, f32[256,256]{1,0:T(8,128)S(1)}, u32[]{:S(2)}, u32[]{:S(2)}) %collective-permute-start.2) | collective-permute-done | bytes 262176 | tf_op jit(solution)/shard_map/ppermute | solution.py:224
  34.3 6.1 %collective-permute-start.4 = (f32[64,256]{1,0:T(8,128)S(1)}, f32[64,256]{1,0:T(8,128)S(1)}, u32[]{:S(2)}, u32[]{:S(2)}) collective-permute-start(f32[64,256]{1,0:T(8,128)S(1)} %get-tuple-element.31), channel_id=1, source_target_pairs={{0,4},{1,5},{2,6},{3,7},{4,8},{5,9},{6,10},{7,11},{8,12},{9,13},{1... | collective-permute-start | bytes 196616 | tf_op jit(solution)/shard_map/ppermute | solution.py:230
  40.5 3.0 %collective-permute-start.3 = (f32[64,256]{1,0:T(8,128)S(1)}, f32[64,256]{1,0:T(8,128)S(1)}, u32[]{:S(2)}, u32[]{:S(2)}) collective-permute-start(f32[64,256]{1,0:T(8,128)S(1)} %get-tuple-element.30), channel_id=1, source_target_pairs={{0,12},{1,13},{2,14},{3,15},{4,0},{5,1},{6,2},{7,3},{8,4},{9,5},{1... | collective-permute-start | bytes 196616 | tf_op jit(solution)/shard_map/ppermute | solution.py:230
  43.6 6.2 %collective-permute-start.5 = (f32[64,256]{1,0:T(8,128)S(1)}, f32[64,256]{1,0:T(8,128)S(1)}, u32[]{:S(2)}, u32[]{:S(2)}) collective-permute-start(f32[64,256]{1,0:T(8,128)S(1)} %slice_add_fusion), channel_id=1, source_target_pairs={{0,4},{1,5},{2,6},{3,7},{4,8},{5,9},{6,10},{7,11},{8,12},{9,13},{1... | collective-permute-start | bytes 196616 | tf_op jit(solution)/shard_map/ppermute | solution.py:230
  49.8 4.5 %collective-permute-done.5 = f32[64,256]{1,0:T(8,128)S(1)} collective-permute-done((f32[64,256]{1,0:T(8,128)S(1)}, f32[64,256]{1,0:T(8,128)S(1)}, u32[]{:S(2)}, u32[]{:S(2)}) %collective-permute-start.5) | collective-permute-done | bytes 65568 | tf_op jit(solution)/shard_map/ppermute | solution.py:230
  54.3 17.3 %all_gather.3.quarter_ref = f32[256,256]{1,0:T(8,128)S(1)} all-gather(f32[64,256]{1,0:T(8,128)S(1)} %fusion), channel_id=1, replica_groups=mesh['x'=4,'y'=4,'core'=2,'z3'=2,'z2'=2,'z1'=2,'z0'=2] {'z3','z2'}, dimensions={0}, use_global_device_ids=true | all-gather | bytes 327680 | tf_op jit(solution)/shard_map/all_gather | solution.py:266
  71.7 0.8 used_rows.1.rows_ref.refs_3_
  72.5 1.9 collective-permute-start.6
  74.4 1.3 gram_part.1
  75.7 25.2 %all_to_all.20 = f32[32,8,256]{2,1,0:T(8,128)S(1)} all-to-all(f32[32,8,256]{2,1,0:T(8,128)S(1)} %bitcast.5), channel_id=1, replica_groups=mesh['x'=4,'y'=4,'core'=2,'z3'=2,'z2'=2,'z1'=2,'z0'=2] {'x','y','core'}, dimensions={0} | all-to-all | bytes 524288 | tf_op jit(solution)/shard_map/all_to_all | solution.py:238
  101.6 4.0 %all-to-all-start.1 = ((f32[4,8,256]{2,1,0:T(8,128)}), f32[4,8,256]{2,1,0:T(8,128)S(1)}, u32[]{:S(2)}, u32[]{:S(2)}) async-start(f32[4,8,256]{2,1,0:T(8,128)} %broadcast_in_dim.6), calls=%async_computation.1 | async-start | bytes 65536 | tf_op jit(solution)/shard_map/all_to_all | solution.py:238
  105.6 2.7 %collective-permute-start.7 = (f32[256,256]{1,0:T(8,128)}, f32[256,256]{1,0:T(8,128)}, u32[]{:S(2)}, u32[]{:S(2)}) collective-permute-start(f32[256,256]{1,0:T(8,128)} %collective-permute-done.6.refs_2_), channel_id=1, source_target_pairs={{0,1},{1,0},{2,3},{3,2},{4,5},{5,4},{6,7},{7,6},{8,9},{9,8},{10,11... | collective-permute-start | bytes 786440 | tf_op jit(solution)/shard_map/ppermute | solution.py:224
  108.3 3.8 %collective-permute-start.8 = (f32[256,256]{1,0:T(8,128)}, f32[256,256]{1,0:T(8,128)}, u32[]{:S(2)}, u32[]{:S(2)}) collective-permute-start(f32[256,256]{1,0:T(8,128)} %used_rows.1.rows_ref.refs_3_), channel_id=1, source_target_pairs={{0,1},{1,0},{2,3},{3,2},{4,5},{5,4},{6,7},{7,6},{8,9},{9,8},{10,11... | collective-permute-start | bytes 786440 | tf_op jit(solution)/shard_map/ppermute | solution.py:224
  112.1 0.7 broadcast_in_dim.7
  112.8 3.7 %all-to-all-start.2 = ((f32[32,8,256]{2,1,0:T(8,128)}), f32[32,8,256]{2,1,0:T(8,128)S(1)}, u32[]{:S(2)}, u32[]{:S(2)}) async-start(f32[32,8,256]{2,1,0:T(8,128)} %broadcast_in_dim.7), calls=%async_computation.2 | async-start | bytes 524288 | tf_op jit(solution)/shard_map/all_to_all | solution.py:238
  117.8 7.5 %all-to-all-done.2 = f32[32,8,256]{2,1,0:T(8,128)S(1)} async-done(((f32[32,8,256]{2,1,0:T(8,128)}), f32[32,8,256]{2,1,0:T(8,128)S(1)}, u32[]{:S(2)}, u32[]{:S(2)}) %all-to-all-start.2) | async-done | bytes 262176 | tf_op jit(solution)/shard_map/all_to_all | solution.py:238
  125.3 63.5 %basis_and_coeffs.1 = (f32[1024,256]{1,0:T(8,128)}, f32[16,8,1536]{2,1,0:T(8,128)S(1)}, f32[16,8,1536]{2,1,0:T(8,128)S(1)}) custom-call(f32[1,1]{1,0:T(1,128)} %bitcast.total_ref, f32[256,256]{1,0:T(8,128)S(1)} %bitcast.4, f32[256,256]{1,0:T(8,128)} %collective-permute-done.7.refs_0_, f32[256,256]{1,0:T(8,128)} %collective-permute-done.8.refs_1_, ...), custom_call_target="tpu_custom_call" | custom-call | flops 1000000000 | bytes 1048576 | tf_op jit(solution)/shard_map/basis_and_coeffs/pallas_call | solution.py:56
  188.7 2.1 collective-permute-start.9
  190.8 2.1 collective-permute-done.9
  193.0 16.1 %all_to_all.21 = f32[16,8,1536]{2,1,0:T(8,128)S(1)} all-to-all(f32[16,8,1536]{2,1,0:T(8,128)S(1)} %add.27), channel_id=1, replica_groups=mesh['x'=4,'y'=4,'core'=2,'z3'=2,'z2'=2,'z1'=2,'z0'=2] {'x','y'}, dimensions={0} | all-to-all | bytes 1572864 | tf_op jit(solution)/shard_map/all_to_all | solution.py:238
  209.1 0.7 reduce_sum.39
  (22 shorter events, 1.5 us)
Async XLA Ops:
  0.6 1.4 copy-start
  2.0 1.2 copy-start.1
  3.3 1.1 copy-start.2
  6.0 17.0 %collective-permute-start.1 = (f32[256,256]{1,0:T(8,128)S(1)}, f32[256,256]{1,0:T(8,128)S(1)}, u32[]{:S(2)}, u32[]{:S(2)}) collective-permute-start(f32[256,256]{1,0:T(8,128)S(1)} %get-tuple-element.22), channel_id=1, source_target_pairs={{0,1},{1,0},{2,3},{3,2},{4,5},{5,4},{6,7},{7,6},{8,9},{9,8},{10,11... | collective-permute-start | bytes 786440 | tf_op jit(solution)/shard_map/ppermute | solution.py:224
  21.0 8.5 %collective-permute-start = (f32[256,256]{1,0:T(8,128)S(1)}, f32[256,256]{1,0:T(8,128)S(1)}, u32[]{:S(2)}, u32[]{:S(2)}) collective-permute-start(f32[256,256]{1,0:T(8,128)S(1)} %get-tuple-element.20), channel_id=1, source_target_pairs={{0,1},{1,0},{2,3},{3,2},{4,5},{5,4},{6,7},{7,6},{8,9},{9,8},{10,11... | collective-permute-start | bytes 786440 | tf_op jit(solution)/shard_map/ppermute | solution.py:224
  23.0 11.2 %collective-permute-start.2 = (f32[256,256]{1,0:T(8,128)S(1)}, f32[256,256]{1,0:T(8,128)S(1)}, u32[]{:S(2)}, u32[]{:S(2)}) collective-permute-start(f32[256,256]{1,0:T(8,128)S(1)} %add.22), channel_id=1, source_target_pairs={{0,2},{1,3},{2,0},{3,1},{4,6},{5,7},{6,4},{7,5},{8,10},{9,11},{10,... | collective-permute-start | bytes 786440 | tf_op jit(solution)/shard_map/ppermute | solution.py:224
  26.8 44.8 %copy-start.3 = (s32[32]{0:T(128)S(1)}, s32[32]{0:T(128)}, u32[]{:S(2)}) copy-start(s32[32]{0:T(128)} %param.7) | copy-start | bytes 388
  34.3 9.2 %collective-permute-start.4 = (f32[64,256]{1,0:T(8,128)S(1)}, f32[64,256]{1,0:T(8,128)S(1)}, u32[]{:S(2)}, u32[]{:S(2)}) collective-permute-start(f32[64,256]{1,0:T(8,128)S(1)} %get-tuple-element.31), channel_id=1, source_target_pairs={{0,4},{1,5},{2,6},{3,7},{4,8},{5,9},{6,10},{7,11},{8,12},{9,13},{1... | collective-permute-start | bytes 196616 | tf_op jit(solution)/shard_map/ppermute | solution.py:230
  40.5 9.3 %collective-permute-start.3 = (f32[64,256]{1,0:T(8,128)S(1)}, f32[64,256]{1,0:T(8,128)S(1)}, u32[]{:S(2)}, u32[]{:S(2)}) collective-permute-start(f32[64,256]{1,0:T(8,128)S(1)} %get-tuple-element.30), channel_id=1, source_target_pairs={{0,12},{1,13},{2,14},{3,15},{4,0},{5,1},{6,2},{7,3},{8,4},{9,5},{1... | collective-permute-start | bytes 196616 | tf_op jit(solution)/shard_map/ppermute | solution.py:230
  43.6 10.7 %collective-permute-start.5 = (f32[64,256]{1,0:T(8,128)S(1)}, f32[64,256]{1,0:T(8,128)S(1)}, u32[]{:S(2)}, u32[]{:S(2)}) collective-permute-start(f32[64,256]{1,0:T(8,128)S(1)} %slice_add_fusion), channel_id=1, source_target_pairs={{0,4},{1,5},{2,6},{3,7},{4,8},{5,9},{6,10},{7,11},{8,12},{9,13},{1... | collective-permute-start | bytes 196616 | tf_op jit(solution)/shard_map/ppermute | solution.py:230
  72.5 28.5 %collective-permute-start.6 = (f32[256,256]{1,0:T(8,128)}, f32[256,256]{1,0:T(8,128)}, u32[]{:S(2)}, u32[]{:S(2)}) collective-permute-start(f32[256,256]{1,0:T(8,128)} %used_rows.1.rows_ref.refs_3_), channel_id=1, source_target_pairs={{0,2},{1,3},{2,0},{3,1},{4,6},{5,7},{6,4},{7,5},{8,10},{9,11},{10,... | collective-permute-start | bytes 786440 | tf_op jit(solution)/shard_map/ppermute | solution.py:224
  101.6 10.5 %all-to-all-start.1 = ((f32[4,8,256]{2,1,0:T(8,128)}), f32[4,8,256]{2,1,0:T(8,128)S(1)}, u32[]{:S(2)}, u32[]{:S(2)}) async-start(f32[4,8,256]{2,1,0:T(8,128)} %broadcast_in_dim.6), calls=%async_computation.1 | async-start | bytes 65536 | tf_op jit(solution)/shard_map/all_to_all | solution.py:238
  105.6 12.2 %collective-permute-start.7 = (f32[256,256]{1,0:T(8,128)}, f32[256,256]{1,0:T(8,128)}, u32[]{:S(2)}, u32[]{:S(2)}) collective-permute-start(f32[256,256]{1,0:T(8,128)} %collective-permute-done.6.refs_2_), channel_id=1, source_target_pairs={{0,1},{1,0},{2,3},{3,2},{4,5},{5,4},{6,7},{7,6},{8,9},{9,8},{10,11... | collective-permute-start | bytes 786440 | tf_op jit(solution)/shard_map/ppermute | solution.py:224
  108.3 9.5 %collective-permute-start.8 = (f32[256,256]{1,0:T(8,128)}, f32[256,256]{1,0:T(8,128)}, u32[]{:S(2)}, u32[]{:S(2)}) collective-permute-start(f32[256,256]{1,0:T(8,128)} %used_rows.1.rows_ref.refs_3_), channel_id=1, source_target_pairs={{0,1},{1,0},{2,3},{3,2},{4,5},{5,4},{6,7},{7,6},{8,9},{9,8},{10,11... | collective-permute-start | bytes 786440 | tf_op jit(solution)/shard_map/ppermute | solution.py:224
  112.8 12.5 %all-to-all-start.2 = ((f32[32,8,256]{2,1,0:T(8,128)}), f32[32,8,256]{2,1,0:T(8,128)S(1)}, u32[]{:S(2)}, u32[]{:S(2)}) async-start(f32[32,8,256]{2,1,0:T(8,128)} %broadcast_in_dim.7), calls=%async_computation.2 | async-start | bytes 524288 | tf_op jit(solution)/shard_map/all_to_all | solution.py:238
  188.7 4.2 %collective-permute-start.9 = (f32[16,8,1536]{2,1,0:T(8,128)S(1)}, f32[16,8,1536]{2,1,0:T(8,128)S(1)}, u32[]{:S(2)}, u32[]{:S(2)}) collective-permute-start(f32[16,8,1536]{2,1,0:T(8,128)S(1)} %get-tuple-element.29), channel_id=1, source_target_pairs={{0,16},{16,0},{1,17},{17,1},{2,18},{18,2},{3,19},{19,3},{4,20},{20... | collective-permute-start | bytes 2359304 | tf_op jit(solution)/shard_map/ppermute | solution.py:234

commit v12 on v11

--- a/solution.py
+++ b/solution.py
@@ -122,16 +122,14 @@
     )(tex, light, sketch, *tiles)
 
 
-def mask_kernel(counts_ref, quarter_ref, rows_ref):
-    rows = quarter_ref.shape[0]
+def used(counts_ref, order, shape):
     texel = lax.broadcasted_iota(jnp.int32, counts_ref.shape, 1)
     count = jnp.sum(jnp.where(texel == lax.axis_index(TEXEL), counts_ref[...], 0), axis=1, keepdims=True)
-    row = lax.broadcasted_iota(jnp.int32, quarter_ref.shape, 0)
-    rows_ref[...] = jnp.where(row + quarter_of(3) * rows < count, quarter_ref[...], 0.0)
-
-
-def gram_kernel(rows_ref, gram_ref):
-    parts = split(rows_ref[...])
+    return lax.broadcasted_iota(jnp.int32, shape, 0) + quarter_of(order) * shape[0] < count
+
+
+def gram_kernel(counts_ref, quarter_ref, gram_ref):
+    parts = split(jnp.where(used(counts_ref, 3, quarter_ref.shape), quarter_ref[...], 0.0))
     gram_ref[...] = dot_split(parts, parts, (0, 0))
 
 
@@ -192,15 +190,15 @@
         lax.fori_loop(0, size, eliminate, 0)
 
 
-def basis_kernel(total_ref, gram_ref, *refs):
+def basis_kernel(counts_ref, gram_ref, *refs):
     quarter_refs, tile_ref = refs[:4], refs[4]
     basis_ref, keep_ref, send_ref, inverse_ref, a_ref, w_ref, half_ref, coeff_ref = refs[5:]
-    total = total_ref[...]
+    total = jnp.sum(counts_ref[...].astype(F32), axis=1, keepdims=True)
     invert_factor(gram_ref[...] / total, inverse_ref, a_ref, w_ref)
     rows = basis_ref.shape[0] // 4
     inverse = split(inverse_ref[...])
     for order, ref in enumerate(quarter_refs):
-        basis = dot_split(split(ref[...]), inverse, (1, 1))
+        basis = jnp.where(used(counts_ref, order, ref.shape), dot_split(split(ref[...]), inverse, (1, 1)), 0.0)
         basis_ref[pl.ds(pl.multiple_of(quarter_of(order) * rows, rows), rows), :] = basis
         half_ref[order * rows : (order + 1) * rows, :] = basis.astype(BF16)
     coeffs = dot(half_ref[...], tile_ref[...], (0, 0))
@@ -247,7 +245,7 @@
     lights = light_feat.shape[0]
     texels, places = lax.axis_size(TEXEL), lax.axis_size(LIGHT)
     share_rows = capacity // places
-    total = jnp.sum(row_counts).astype(F32).reshape(1, 1)
+    counts = row_counts.reshape(1, texels)
 
     inputs = (tex_feat, light_feat, sketch)
     tiles, part = tile_call(0, *inputs)
@@ -264,11 +262,8 @@
 
     square = (width, width)
     quarter = lax.all_gather(share, FAR, axis=0, tiled=True)
-    quarter = on_core(mask_kernel, jax.ShapeDtypeStruct(quarter.shape, F32), "used_rows")(
-        row_counts.reshape(1, texels), quarter
-    )
     near = across(quarter, 2)
-    gram = on_core(gram_kernel, jax.ShapeDtypeStruct(square, F32), "gram_part")(quarter)
+    gram = on_core(gram_kernel, jax.ShapeDtypeStruct(square, F32), "gram_part")(counts, quarter)
     gram_rows = jnp.sum(each_to_each(gram.reshape(texels, width // texels, width), TEXEL), axis=0)
     gram_rows, near, quarter = lax.optimization_barrier((gram_rows, near, quarter))
     beyond, beside = across(near, 1), across(quarter, 1)
@@ -286,7 +281,7 @@
         "basis_and_coeffs",
         [pltpu.VMEM(square, F32)] * 3
         + [pltpu.VMEM((capacity, width), BF16), pltpu.VMEM((texels, lines, lights), F32)],
-    )(total, gram, beyond, beside, near, quarter, tiles)
+    )(counts, gram, beyond, beside, near, quarter, tiles)
     mine = keep + across_cores(send)
     coeffs = jnp.sum(each_to_each(mine, CHIP), axis=0)
     return basis, coeffs

time: 211 us -> 211 us (level)
  starting transfers between devices: 51.2 us -> 53.4 us
    all_to_all x2, starting transfers between devices: 7.64 us -> 9.93 us  [each_to_each(): return lax.all_to_all(parts, axes, 0, 0, tiled=True)]
    pallas_call x7 -> x6, Pallas kernels: 71.8 us -> 70.5 us  [on_core(): pl.pallas_call(kernel, out_shape=out_shape, in_specs=[VMEM] * len(operand...]
  transfers between devices with their start and end apart: 12 -> 12, of which waited for: 5 -> 5; matrix products, arithmetic and copies ran while one was open for 1% -> 1% of each run, Pallas kernels for 3% -> 2%
where the time goes in v12:
time: 211 us; the launch traced here: 210 us
  Pallas kernels  70.5 us (33%)
  blocking collectives  57.3 us (27%)
  starting transfers between devices  53.4 us (25%)
  waiting for transfers between devices  21.2 us (10%)
  local copies, waits for them, and re-layouts  5.11 us (2%)
    pallas_call x6, Pallas kernels, on_core(): pl.pallas_call(kernel, out_shape=out_shape, in_specs=[VMEM] * len(operand...  70.5 us
    all_to_all x2, blocking collectives, each_to_each(): return lax.all_to_all(parts, axes, 0, 0, tiled=True)  40.1 us
    ppermute x6, starting transfers between devices, across(): lax.ppermute(value, ('core', *LIGHT), light_pairs(lax.axis_size(LIGHT), r...  26.1 us
    all_gather x1, blocking collectives, on_device(): quarter = lax.all_gather(share, FAR, axis=0, tiled=True)  17.1 us
    ppermute x3, starting transfers between devices, onward(): return lax.ppermute(value, ('core', *LIGHT), pairs)  15.4 us
    all_to_all x2, starting transfers between devices, each_to_each(): return lax.all_to_all(parts, axes, 0, 0, tiled=True)  9.93 us
    all_to_all x2, waiting for transfers between devices, each_to_each(): return lax.all_to_all(parts, axes, 0, 0, tiled=True)  8.75 us
    ppermute x6, waiting for transfers between devices, across(): lax.ppermute(value, ('core', *LIGHT), light_pairs(lax.axis_size(LIGHT), r...  5.81 us
  transfers between devices with their start and end apart: 12, of which 5 were waited for; matrix products, arithmetic and copies ran while one was open for 1% of the time, Pallas kernels for 2%

profile of v12, /device:TPU:1, one launch (start us, length us, event | category | flops | bytes accessed | tf_op | source)
XLA Modules:
  0.0 210.3 jit_solution(3292878970490939600)
XLA Ops:
  0.6 1.4 copy-done
  2.0 1.2 copy-done.1
  3.3 1.1 copy-done.2
  4.4 1.6 tile_quarter.4
  6.0 11.9 %collective-permute-start.1 = (f32[256,256]{1,0:T(8,128)S(1)}, f32[256,256]{1,0:T(8,128)S(1)}, u32[]{:S(2)}, u32[]{:S(2)}) collective-permute-start(f32[256,256]{1,0:T(8,128)S(1)} %get-tuple-element.22), channel_id=1, source_target_pairs={{0,1},{1,0},{2,3},{3,2},{4,5},{5,4},{6,7},{7,6},{8,9},{9,8},{10,11... | collective-permute-start | bytes 786440 | tf_op jit(solution)/shard_map/ppermute | solution.py:222
  17.9 1.6 tile_quarter.5
  19.5 1.6 tile_quarter.6
  21.1 1.9 collective-permute-start
  23.1 3.8 %collective-permute-start.2 = (f32[256,256]{1,0:T(8,128)S(1)}, f32[256,256]{1,0:T(8,128)S(1)}, u32[]{:S(2)}, u32[]{:S(2)}) collective-permute-start(f32[256,256]{1,0:T(8,128)S(1)} %add.22), channel_id=1, source_target_pairs={{0,2},{1,3},{2,0},{3,1},{4,6},{5,7},{6,4},{7,5},{8,10},{9,11},{10,... | collective-permute-start | bytes 786440 | tf_op jit(solution)/shard_map/ppermute | solution.py:222
  26.9 1.6 tile_quarter.7
  28.5 1.1 collective-permute-done
  29.6 4.7 %collective-permute-done.2 = f32[256,256]{1,0:T(8,128)S(1)} collective-permute-done((f32[256,256]{1,0:T(8,128)S(1)}, f32[256,256]{1,0:T(8,128)S(1)}, u32[]{:S(2)}, u32[]{:S(2)}) %collective-permute-start.2) | collective-permute-done | bytes 262176 | tf_op jit(solution)/shard_map/ppermute | solution.py:222
  34.4 6.2 %collective-permute-start.4 = (f32[64,256]{1,0:T(8,128)S(1)}, f32[64,256]{1,0:T(8,128)S(1)}, u32[]{:S(2)}, u32[]{:S(2)}) collective-permute-start(f32[64,256]{1,0:T(8,128)S(1)} %get-tuple-element.31), channel_id=1, source_target_pairs={{0,4},{1,5},{2,6},{3,7},{4,8},{5,9},{6,10},{7,11},{8,12},{9,13},{1... | collective-permute-start | bytes 196616 | tf_op jit(solution)/shard_map/ppermute | solution.py:228
  40.6 3.0 %collective-permute-start.3 = (f32[64,256]{1,0:T(8,128)S(1)}, f32[64,256]{1,0:T(8,128)S(1)}, u32[]{:S(2)}, u32[]{:S(2)}) collective-permute-start(f32[64,256]{1,0:T(8,128)S(1)} %get-tuple-element.30), channel_id=1, source_target_pairs={{0,12},{1,13},{2,14},{3,15},{4,0},{5,1},{6,2},{7,3},{8,4},{9,5},{1... | collective-permute-start | bytes 196616 | tf_op jit(solution)/shard_map/ppermute | solution.py:228
  43.6 6.2 %collective-permute-start.5 = (f32[64,256]{1,0:T(8,128)S(1)}, f32[64,256]{1,0:T(8,128)S(1)}, u32[]{:S(2)}, u32[]{:S(2)}) collective-permute-start(f32[64,256]{1,0:T(8,128)S(1)} %slice_add_fusion), channel_id=1, source_target_pairs={{0,4},{1,5},{2,6},{3,7},{4,8},{5,9},{6,10},{7,11},{8,12},{9,13},{1... | collective-permute-start | bytes 196616 | tf_op jit(solution)/shard_map/ppermute | solution.py:228
  49.8 4.6 %collective-permute-done.5 = f32[64,256]{1,0:T(8,128)S(1)} collective-permute-done((f32[64,256]{1,0:T(8,128)S(1)}, f32[64,256]{1,0:T(8,128)S(1)}, u32[]{:S(2)}, u32[]{:S(2)}) %collective-permute-start.5) | collective-permute-done | bytes 65568 | tf_op jit(solution)/shard_map/ppermute | solution.py:228
  54.4 17.1 %all_gather.3.quarter_ref.refs_3_ = f32[256,256]{1,0:T(8,128)S(1)} all-gather(f32[64,256]{1,0:T(8,128)S(1)} %fusion), channel_id=1, replica_groups=mesh['x'=4,'y'=4,'core'=2,'z3'=2,'z2'=2,'z1'=2,'z0'=2] {'z3','z2'}, dimensions={0}, use_global_device_ids=true | all-gather | bytes 327680 | tf_op jit(solution)/shard_map/all_gather | solution.py:264
  71.6 1.9 collective-permute-start.6
  73.9 24.1 %all_to_all.20 = f32[32,8,256]{2,1,0:T(8,128)} all-to-all(f32[32,8,256]{2,1,0:T(8,128)S(1)} %bitcast.3), channel_id=1, replica_groups=mesh['x'=4,'y'=4,'core'=2,'z3'=2,'z2'=2,'z1'=2,'z0'=2] {'x','y','core'}, dimensions={0} | all-to-all | bytes 524288 | tf_op jit(solution)/shard_map/all_to_all | solution.py:236
  98.0 1.0 reduce_sum.27
  99.0 0.6 broadcast_in_dim.6
  99.6 5.5 %all-to-all-start.1 = ((f32[4,8,256]{2,1,0:T(8,128)}), f32[4,8,256]{2,1,0:T(8,128)S(1)}, u32[]{:S(2)}, u32[]{:S(2)}) async-start(f32[4,8,256]{2,1,0:T(8,128)} %broadcast_in_dim.6), calls=%async_computation.1 | async-start | bytes 65536 | tf_op jit(solution)/shard_map/all_to_all | solution.py:236
  105.2 2.7 %collective-permute-start.7 = (f32[256,256]{1,0:T(8,128)}, f32[256,256]{1,0:T(8,128)}, u32[]{:S(2)}, u32[]{:S(2)}) collective-permute-start(f32[256,256]{1,0:T(8,128)} %collective-permute-done.6.refs_2_), channel_id=1, source_target_pairs={{0,1},{1,0},{2,3},{3,2},{4,5},{5,4},{6,7},{7,6},{8,9},{9,8},{10,11... | collective-permute-start | bytes 786440 | tf_op jit(solution)/shard_map/ppermute | solution.py:222
  107.9 3.8 %collective-permute-start.8 = (f32[256,256]{1,0:T(8,128)S(1)}, f32[256,256]{1,0:T(8,128)}, u32[]{:S(2)}, u32[]{:S(2)}) collective-permute-start(f32[256,256]{1,0:T(8,128)S(1)} %all_gather.3.quarter_ref.refs_3_), channel_id=1, source_target_pairs={{0,1},{1,0},{2,3},{3,2},{4,5},{5,4},{6,7},{7,6},{8,9},{9,8},{10,11... | collective-permute-start | bytes 786440 | tf_op jit(solution)/shard_map/ppermute | solution.py:222
  111.7 0.7 broadcast_in_dim.7
  112.4 4.4 %all-to-all-start.2 = ((f32[32,8,256]{2,1,0:T(8,128)}), f32[32,8,256]{2,1,0:T(8,128)}, u32[]{:S(2)}, u32[]{:S(2)}) async-start(f32[32,8,256]{2,1,0:T(8,128)} %broadcast_in_dim.7), calls=%async_computation.2 | async-start | bytes 524288 | tf_op jit(solution)/shard_map/all_to_all | solution.py:236
  116.8 8.7 %all-to-all-done.2 = f32[32,8,256]{2,1,0:T(8,128)} async-done(((f32[32,8,256]{2,1,0:T(8,128)}), f32[32,8,256]{2,1,0:T(8,128)}, u32[]{:S(2)}, u32[]{:S(2)}) %all-to-all-start.2) | async-done | bytes 262176 | tf_op jit(solution)/shard_map/all_to_all | solution.py:236
  125.6 63.7 %basis_and_coeffs.1 = (f32[1024,256]{1,0:T(8,128)}, f32[16,8,1536]{2,1,0:T(8,128)S(1)}, f32[16,8,1536]{2,1,0:T(8,128)S(1)}) custom-call(s32[1,32]{1,0:T(1,128)S(1)} %bitcast.5, f32[256,256]{1,0:T(8,128)} %bitcast.2.gram_ref, f32[256,256]{1,0:T(8,128)} %collective-permute-done.7.refs_0_, f32[256,256]{1,0:T(8,128)} %collective-permute-done.8.refs_1_, ...), custom_call_target="tpu_custom_call" | custom-call | flops 1000000000 | bytes 1048576 | tf_op jit(solution)/shard_map/basis_and_coeffs/pallas_call | solution.py:56
  189.3 2.1 collective-permute-start.9
  191.4 2.1 collective-permute-done.9
  193.6 16.1 %all_to_all.21 = f32[16,8,1536]{2,1,0:T(8,128)S(1)} all-to-all(f32[16,8,1536]{2,1,0:T(8,128)S(1)} %add.27), channel_id=1, replica_groups=mesh['x'=4,'y'=4,'core'=2,'z3'=2,'z2'=2,'z1'=2,'z0'=2] {'x','y'}, dimensions={0} | all-to-all | bytes 1572864 | tf_op jit(solution)/shard_map/all_to_all | solution.py:236
  209.6 0.7 reduce_sum.29
  (20 shorter events, 0.7 us)
Async XLA Ops:
  0.6 1.4 copy-start
  2.0 1.2 copy-start.1
  3.3 1.1 copy-start.2
  6.0 17.1 %collective-permute-start.1 = (f32[256,256]{1,0:T(8,128)S(1)}, f32[256,256]{1,0:T(8,128)S(1)}, u32[]{:S(2)}, u32[]{:S(2)}) collective-permute-start(f32[256,256]{1,0:T(8,128)S(1)} %get-tuple-element.22), channel_id=1, source_target_pairs={{0,1},{1,0},{2,3},{3,2},{4,5},{5,4},{6,7},{7,6},{8,9},{9,8},{10,11... | collective-permute-start | bytes 786440 | tf_op jit(solution)/shard_map/ppermute | solution.py:222
  21.1 8.5 %collective-permute-start = (f32[256,256]{1,0:T(8,128)S(1)}, f32[256,256]{1,0:T(8,128)S(1)}, u32[]{:S(2)}, u32[]{:S(2)}) collective-permute-start(f32[256,256]{1,0:T(8,128)S(1)} %get-tuple-element.20), channel_id=1, source_target_pairs={{0,1},{1,0},{2,3},{3,2},{4,5},{5,4},{6,7},{7,6},{8,9},{9,8},{10,11... | collective-permute-start | bytes 786440 | tf_op jit(solution)/shard_map/ppermute | solution.py:222
  23.1 11.2 %collective-permute-start.2 = (f32[256,256]{1,0:T(8,128)S(1)}, f32[256,256]{1,0:T(8,128)S(1)}, u32[]{:S(2)}, u32[]{:S(2)}) collective-permute-start(f32[256,256]{1,0:T(8,128)S(1)} %add.22), channel_id=1, source_target_pairs={{0,2},{1,3},{2,0},{3,1},{4,6},{5,7},{6,4},{7,5},{8,10},{9,11},{10,... | collective-permute-start | bytes 786440 | tf_op jit(solution)/shard_map/ppermute | solution.py:222
  26.9 46.6 %copy-start.3 = (s32[32]{0:T(128)S(1)}, s32[32]{0:T(128)}, u32[]{:S(2)}) copy-start(s32[32]{0:T(128)} %param.7) | copy-start | bytes 388
  34.4 9.2 %collective-permute-start.4 = (f32[64,256]{1,0:T(8,128)S(1)}, f32[64,256]{1,0:T(8,128)S(1)}, u32[]{:S(2)}, u32[]{:S(2)}) collective-permute-start(f32[64,256]{1,0:T(8,128)S(1)} %get-tuple-element.31), channel_id=1, source_target_pairs={{0,4},{1,5},{2,6},{3,7},{4,8},{5,9},{6,10},{7,11},{8,12},{9,13},{1... | collective-permute-start | bytes 196616 | tf_op jit(solution)/shard_map/ppermute | solution.py:228
  40.6 9.2 %collective-permute-start.3 = (f32[64,256]{1,0:T(8,128)S(1)}, f32[64,256]{1,0:T(8,128)S(1)}, u32[]{:S(2)}, u32[]{:S(2)}) collective-permute-start(f32[64,256]{1,0:T(8,128)S(1)} %get-tuple-element.30), channel_id=1, source_target_pairs={{0,12},{1,13},{2,14},{3,15},{4,0},{5,1},{6,2},{7,3},{8,4},{9,5},{1... | collective-permute-start | bytes 196616 | tf_op jit(solution)/shard_map/ppermute | solution.py:228
  43.6 10.8 %collective-permute-start.5 = (f32[64,256]{1,0:T(8,128)S(1)}, f32[64,256]{1,0:T(8,128)S(1)}, u32[]{:S(2)}, u32[]{:S(2)}) collective-permute-start(f32[64,256]{1,0:T(8,128)S(1)} %slice_add_fusion), channel_id=1, source_target_pairs={{0,4},{1,5},{2,6},{3,7},{4,8},{5,9},{6,10},{7,11},{8,12},{9,13},{1... | collective-permute-start | bytes 196616 | tf_op jit(solution)/shard_map/ppermute | solution.py:228
  71.6 27.4 %collective-permute-start.6 = (f32[256,256]{1,0:T(8,128)S(1)}, f32[256,256]{1,0:T(8,128)}, u32[]{:S(2)}, u32[]{:S(2)}) collective-permute-start(f32[256,256]{1,0:T(8,128)S(1)} %all_gather.3.quarter_ref.refs_3_), channel_id=1, source_target_pairs={{0,2},{1,3},{2,0},{3,1},{4,6},{5,7},{6,4},{7,5},{8,10},{9,11},{10,... | collective-permute-start | bytes 786440 | tf_op jit(solution)/shard_map/ppermute | solution.py:222
  99.6 12.1 %all-to-all-start.1 = ((f32[4,8,256]{2,1,0:T(8,128)}), f32[4,8,256]{2,1,0:T(8,128)S(1)}, u32[]{:S(2)}, u32[]{:S(2)}) async-start(f32[4,8,256]{2,1,0:T(8,128)} %broadcast_in_dim.6), calls=%async_computation.1 | async-start | bytes 65536 | tf_op jit(solution)/shard_map/all_to_all | solution.py:236
  105.2 11.6 %collective-permute-start.7 = (f32[256,256]{1,0:T(8,128)}, f32[256,256]{1,0:T(8,128)}, u32[]{:S(2)}, u32[]{:S(2)}) collective-permute-start(f32[256,256]{1,0:T(8,128)} %collective-permute-done.6.refs_2_), channel_id=1, source_target_pairs={{0,1},{1,0},{2,3},{3,2},{4,5},{5,4},{6,7},{7,6},{8,9},{9,8},{10,11... | collective-permute-start | bytes 786440 | tf_op jit(solution)/shard_map/ppermute | solution.py:222
  107.9 8.9 %collective-permute-start.8 = (f32[256,256]{1,0:T(8,128)S(1)}, f32[256,256]{1,0:T(8,128)}, u32[]{:S(2)}, u32[]{:S(2)}) collective-permute-start(f32[256,256]{1,0:T(8,128)S(1)} %all_gather.3.quarter_ref.refs_3_), channel_id=1, source_target_pairs={{0,1},{1,0},{2,3},{3,2},{4,5},{5,4},{6,7},{7,6},{8,9},{9,8},{10,11... | collective-permute-start | bytes 786440 | tf_op jit(solution)/shard_map/ppermute | solution.py:222
  112.4 13.2 %all-to-all-start.2 = ((f32[32,8,256]{2,1,0:T(8,128)}), f32[32,8,256]{2,1,0:T(8,128)}, u32[]{:S(2)}, u32[]{:S(2)}) async-start(f32[32,8,256]{2,1,0:T(8,128)} %broadcast_in_dim.7), calls=%async_computation.2 | async-start | bytes 524288 | tf_op jit(solution)/shard_map/all_to_all | solution.py:236
  189.3 4.2 %collective-permute-start.9 = (f32[16,8,1536]{2,1,0:T(8,128)S(1)}, f32[16,8,1536]{2,1,0:T(8,128)S(1)}, u32[]{:S(2)}, u32[]{:S(2)}) collective-permute-start(f32[16,8,1536]{2,1,0:T(8,128)S(1)} %get-tuple-element.29), channel_id=1, source_target_pairs={{0,16},{16,0},{1,17},{17,1},{2,18},{18,2},{3,19},{19,3},{4,20},{20... | collective-permute-start | bytes 2359304 | tf_op jit(solution)/shard_map/ppermute | solution.py:232

commit v13 on v12

--- a/solution.py
+++ b/solution.py
@@ -236,8 +236,13 @@
     return lax.all_to_all(parts, axes, 0, 0, tiled=True)
 
 
-def to_each(value, axes):
-    return each_to_each(jnp.broadcast_to(value, (lax.axis_size(axes), *value.shape)), axes)
+def sum_kernel(parts_ref, copies_ref):
+    copies_ref[...] = jnp.broadcast_to(jnp.sum(parts_ref[...], axis=0, keepdims=True), copies_ref.shape)
+
+
+def sum_to_each(parts, axes):
+    copies = jax.ShapeDtypeStruct((lax.axis_size(axes), *parts.shape[1:]), parts.dtype)
+    return each_to_each(on_core(sum_kernel, copies, "sum_and_repeat")(parts), axes)
 
 
 def on_device(tex_feat, light_feat, sketch, row_counts):
@@ -264,11 +269,12 @@
     quarter = lax.all_gather(share, FAR, axis=0, tiled=True)
     near = across(quarter, 2)
     gram = on_core(gram_kernel, jax.ShapeDtypeStruct(square, F32), "gram_part")(counts, quarter)
-    gram_rows = jnp.sum(each_to_each(gram.reshape(texels, width // texels, width), TEXEL), axis=0)
+    gram_rows = each_to_each(gram.reshape(texels, width // texels, width), TEXEL)
     gram_rows, near, quarter = lax.optimization_barrier((gram_rows, near, quarter))
     beyond, beside = across(near, 1), across(quarter, 1)
-    gram_rows = jnp.sum(to_each(gram_rows, ("z1", "z0")), axis=0)
-    gram = to_each(gram_rows, TEXEL).reshape(square)
+    gram_rows = sum_to_each(gram_rows, ("z1", "z0"))
+    gram_rows = jnp.sum(gram_rows, axis=0)
+    gram = each_to_each(jnp.broadcast_to(gram_rows, (texels, *gram_rows.shape)), TEXEL).reshape(square)
 
     lines, chips = width // texels, lax.axis_size(CHIP)
     basis, keep, send = on_core(

time: 211 us -> 211 us (level)
    pallas_call x6 -> x7, Pallas kernels: 70.5 us -> 71.7 us  [on_core(): pl.pallas_call(kernel, out_shape=out_shape, in_specs=[VMEM] * len(operand...]
  transfers between devices with their start and end apart: 12 -> 12, of which waited for: 5 -> 5; matrix products, arithmetic and copies ran while one was open for 1% -> 0% of each run, Pallas kernels for 2% -> 2%
where the time goes in v13:
time: 211 us; the launch traced here: 210 us
  Pallas kernels  71.7 us (34%)
  blocking collectives  57.1 us (27%)
  starting transfers between devices  53.4 us (25%)
  waiting for transfers between devices  21.2 us (10%)
  local copies, waits for them, and re-layouts  4.5 us (2%)
    pallas_call x7, Pallas kernels, on_core(): pl.pallas_call(kernel, out_shape=out_shape, in_specs=[VMEM] * len(operand...  71.7 us
    all_to_all x2, blocking collectives, each_to_each(): return lax.all_to_all(parts, axes, 0, 0, tiled=True)  40 us
    ppermute x6, starting transfers between devices, across(): lax.ppermute(value, ('core', *LIGHT), light_pairs(lax.axis_size(LIGHT), r...  26.1 us
    all_gather x1, blocking collectives, on_device(): quarter = lax.all_gather(share, FAR, axis=0, tiled=True)  17.1 us
    ppermute x3, starting transfers between devices, onward(): return lax.ppermute(value, ('core', *LIGHT), pairs)  15.4 us
    all_to_all x2, starting transfers between devices, each_to_each(): return lax.all_to_all(parts, axes, 0, 0, tiled=True)  9.93 us
    all_to_all x2, waiting for transfers between devices, each_to_each(): return lax.all_to_all(parts, axes, 0, 0, tiled=True)  8.74 us
    ppermute x6, waiting for transfers between devices, across(): lax.ppermute(value, ('core', *LIGHT), light_pairs(lax.axis_size(LIGHT), r...  5.81 us
  transfers between devices with their start and end apart: 12, of which 5 were waited for; matrix products, arithmetic and copies ran while one was open for 0% of the time, Pallas kernels for 2%

profile of v13, /device:TPU:1, one launch (start us, length us, event | category | flops | bytes accessed | tf_op | source)
XLA Modules:
  0.0 209.7 jit_solution(9683655151071167938)
XLA Ops:
  0.6 1.4 copy-done
  2.0 1.2 copy-done.1
  3.3 1.1 copy-done.2
  4.4 1.6 tile_quarter.4
  6.0 11.9 %collective-permute-start.1 = (f32[256,256]{1,0:T(8,128)S(1)}, f32[256,256]{1,0:T(8,128)S(1)}, u32[]{:S(2)}, u32[]{:S(2)}) collective-permute-start(f32[256,256]{1,0:T(8,128)S(1)} %get-tuple-element.22), channel_id=1, source_target_pairs={{0,1},{1,0},{2,3},{3,2},{4,5},{5,4},{6,7},{7,6},{8,9},{9,8},{10,11... | collective-permute-start | bytes 786440 | tf_op jit(solution)/shard_map/ppermute | solution.py:222
  17.9 1.6 tile_quarter.5
  19.5 1.6 tile_quarter.6
  21.1 1.9 collective-permute-start
  23.1 3.8 %collective-permute-start.2 = (f32[256,256]{1,0:T(8,128)S(1)}, f32[256,256]{1,0:T(8,128)S(1)}, u32[]{:S(2)}, u32[]{:S(2)}) collective-permute-start(f32[256,256]{1,0:T(8,128)S(1)} %add.22), channel_id=1, source_target_pairs={{0,2},{1,3},{2,0},{3,1},{4,6},{5,7},{6,4},{7,5},{8,10},{9,11},{10,... | collective-permute-start | bytes 786440 | tf_op jit(solution)/shard_map/ppermute | solution.py:222
  26.9 1.6 tile_quarter.7
  28.5 1.1 collective-permute-done
  29.6 4.7 %collective-permute-done.2 = f32[256,256]{1,0:T(8,128)S(1)} collective-permute-done((f32[256,256]{1,0:T(8,128)S(1)}, f32[256,256]{1,0:T(8,128)S(1)}, u32[]{:S(2)}, u32[]{:S(2)}) %collective-permute-start.2) | collective-permute-done | bytes 262176 | tf_op jit(solution)/shard_map/ppermute | solution.py:222
  34.4 6.2 %collective-permute-start.4 = (f32[64,256]{1,0:T(8,128)S(1)}, f32[64,256]{1,0:T(8,128)S(1)}, u32[]{:S(2)}, u32[]{:S(2)}) collective-permute-start(f32[64,256]{1,0:T(8,128)S(1)} %get-tuple-element.31), channel_id=1, source_target_pairs={{0,4},{1,5},{2,6},{3,7},{4,8},{5,9},{6,10},{7,11},{8,12},{9,13},{1... | collective-permute-start | bytes 196616 | tf_op jit(solution)/shard_map/ppermute | solution.py:228
  40.6 3.0 %collective-permute-start.3 = (f32[64,256]{1,0:T(8,128)S(1)}, f32[64,256]{1,0:T(8,128)S(1)}, u32[]{:S(2)}, u32[]{:S(2)}) collective-permute-start(f32[64,256]{1,0:T(8,128)S(1)} %get-tuple-element.30), channel_id=1, source_target_pairs={{0,12},{1,13},{2,14},{3,15},{4,0},{5,1},{6,2},{7,3},{8,4},{9,5},{1... | collective-permute-start | bytes 196616 | tf_op jit(solution)/shard_map/ppermute | solution.py:228
  43.6 6.2 %collective-permute-start.5 = (f32[64,256]{1,0:T(8,128)S(1)}, f32[64,256]{1,0:T(8,128)S(1)}, u32[]{:S(2)}, u32[]{:S(2)}) collective-permute-start(f32[64,256]{1,0:T(8,128)S(1)} %slice_add_fusion), channel_id=1, source_target_pairs={{0,4},{1,5},{2,6},{3,7},{4,8},{5,9},{6,10},{7,11},{8,12},{9,13},{1... | collective-permute-start | bytes 196616 | tf_op jit(solution)/shard_map/ppermute | solution.py:228
  49.8 4.6 %collective-permute-done.5 = f32[64,256]{1,0:T(8,128)S(1)} collective-permute-done((f32[64,256]{1,0:T(8,128)S(1)}, f32[64,256]{1,0:T(8,128)S(1)}, u32[]{:S(2)}, u32[]{:S(2)}) %collective-permute-start.5) | collective-permute-done | bytes 65568 | tf_op jit(solution)/shard_map/ppermute | solution.py:228
  54.4 17.1 %all_gather.3.quarter_ref.refs_3_ = f32[256,256]{1,0:T(8,128)S(1)} all-gather(f32[64,256]{1,0:T(8,128)S(1)} %fusion), channel_id=1, replica_groups=mesh['x'=4,'y'=4,'core'=2,'z3'=2,'z2'=2,'z1'=2,'z0'=2] {'z3','z2'}, dimensions={0}, use_global_device_ids=true | all-gather | bytes 327680 | tf_op jit(solution)/shard_map/all_gather | solution.py:269
  71.6 1.9 collective-permute-start.6
  73.5 0.4 gram_part.1
  73.9 24.0 %all_to_all.20.parts_ref = f32[32,8,256]{2,1,0:T(8,128)S(1)} all-to-all(f32[32,8,256]{2,1,0:T(8,128)S(1)} %bitcast.3), channel_id=1, replica_groups=mesh['x'=4,'y'=4,'core'=2,'z3'=2,'z2'=2,'z1'=2,'z0'=2] {'x','y','core'}, dimensions={0} | all-to-all | bytes 524288 | tf_op jit(solution)/shard_map/all_to_all | solution.py:236
  97.9 0.7 sum_and_repeat.1
  98.6 5.5 %all-to-all-start.1 = ((f32[4,8,256]{2,1,0:T(8,128)}), f32[4,8,256]{2,1,0:T(8,128)S(1)}, u32[]{:S(2)}, u32[]{:S(2)}) async-start(f32[4,8,256]{2,1,0:T(8,128)} %sum_and_repeat.1), calls=%async_computation.1 | async-start | bytes 65536 | tf_op jit(solution)/shard_map/all_to_all | solution.py:236
  104.1 2.7 %collective-permute-start.7 = (f32[256,256]{1,0:T(8,128)}, f32[256,256]{1,0:T(8,128)}, u32[]{:S(2)}, u32[]{:S(2)}) collective-permute-start(f32[256,256]{1,0:T(8,128)} %collective-permute-done.6.refs_2_), channel_id=1, source_target_pairs={{0,1},{1,0},{2,3},{3,2},{4,5},{5,4},{6,7},{7,6},{8,9},{9,8},{10,11... | collective-permute-start | bytes 786440 | tf_op jit(solution)/shard_map/ppermute | solution.py:222
  106.8 3.8 %collective-permute-start.8 = (f32[256,256]{1,0:T(8,128)S(1)}, f32[256,256]{1,0:T(8,128)}, u32[]{:S(2)}, u32[]{:S(2)}) collective-permute-start(f32[256,256]{1,0:T(8,128)S(1)} %all_gather.3.quarter_ref.refs_3_), channel_id=1, source_target_pairs={{0,1},{1,0},{2,3},{3,2},{4,5},{5,4},{6,7},{7,6},{8,9},{9,8},{10,11... | collective-permute-start | bytes 786440 | tf_op jit(solution)/shard_map/ppermute | solution.py:222
  110.6 0.7 broadcast_in_dim.3
  111.4 4.4 %all-to-all-start.2 = ((f32[32,8,256]{2,1,0:T(8,128)}), f32[32,8,256]{2,1,0:T(8,128)}, u32[]{:S(2)}, u32[]{:S(2)}) async-start(f32[32,8,256]{2,1,0:T(8,128)} %broadcast_in_dim.3), calls=%async_computation.2 | async-start | bytes 524288 | tf_op jit(solution)/shard_map/all_to_all | solution.py:236
  115.8 8.7 %all-to-all-done.2 = f32[32,8,256]{2,1,0:T(8,128)} async-done(((f32[32,8,256]{2,1,0:T(8,128)}), f32[32,8,256]{2,1,0:T(8,128)}, u32[]{:S(2)}, u32[]{:S(2)}) %all-to-all-start.2) | async-done | bytes 262176 | tf_op jit(solution)/shard_map/all_to_all | solution.py:236
  124.5 64.2 %basis_and_coeffs.1 = (f32[1024,256]{1,0:T(8,128)}, f32[16,8,1536]{2,1,0:T(8,128)S(1)}, f32[16,8,1536]{2,1,0:T(8,128)S(1)}) custom-call(s32[1,32]{1,0:T(1,128)S(1)} %bitcast.5, f32[256,256]{1,0:T(8,128)} %bitcast.2.gram_ref, f32[256,256]{1,0:T(8,128)} %collective-permute-done.7.refs_0_, f32[256,256]{1,0:T(8,128)} %collective-permute-done.8.refs_1_, ...), custom_call_target="tpu_custom_call" | custom-call | flops 1000000000 | bytes 1048576 | tf_op jit(solution)/shard_map/basis_and_coeffs/pallas_call | solution.py:56
  188.7 2.1 collective-permute-start.9
  190.8 2.1 collective-permute-done.9
  193.0 16.1 %all_to_all.21 = f32[16,8,1536]{2,1,0:T(8,128)S(1)} all-to-all(f32[16,8,1536]{2,1,0:T(8,128)S(1)} %add.27), channel_id=1, replica_groups=mesh['x'=4,'y'=4,'core'=2,'z3'=2,'z2'=2,'z1'=2,'z0'=2] {'x','y'}, dimensions={0} | all-to-all | bytes 1572864 | tf_op jit(solution)/shard_map/all_to_all | solution.py:236
  209.1 0.7 reduce_sum.19
  (19 shorter events, 0.3 us)
Async XLA Ops:
  0.6 1.4 copy-start
  2.0 1.2 copy-start.1
  3.3 1.1 copy-start.2
  6.0 17.1 %collective-permute-start.1 = (f32[256,256]{1,0:T(8,128)S(1)}, f32[256,256]{1,0:T(8,128)S(1)}, u32[]{:S(2)}, u32[]{:S(2)}) collective-permute-start(f32[256,256]{1,0:T(8,128)S(1)} %get-tuple-element.22), channel_id=1, source_target_pairs={{0,1},{1,0},{2,3},{3,2},{4,5},{5,4},{6,7},{7,6},{8,9},{9,8},{10,11... | collective-permute-start | bytes 786440 | tf_op jit(solution)/shard_map/ppermute | solution.py:222
  21.1 8.5 %collective-permute-start = (f32[256,256]{1,0:T(8,128)S(1)}, f32[256,256]{1,0:T(8,128)S(1)}, u32[]{:S(2)}, u32[]{:S(2)}) collective-permute-start(f32[256,256]{1,0:T(8,128)S(1)} %get-tuple-element.20), channel_id=1, source_target_pairs={{0,1},{1,0},{2,3},{3,2},{4,5},{5,4},{6,7},{7,6},{8,9},{9,8},{10,11... | collective-permute-start | bytes 786440 | tf_op jit(solution)/shard_map/ppermute | solution.py:222
  23.1 11.2 %collective-permute-start.2 = (f32[256,256]{1,0:T(8,128)S(1)}, f32[256,256]{1,0:T(8,128)S(1)}, u32[]{:S(2)}, u32[]{:S(2)}) collective-permute-start(f32[256,256]{1,0:T(8,128)S(1)} %add.22), channel_id=1, source_target_pairs={{0,2},{1,3},{2,0},{3,1},{4,6},{5,7},{6,4},{7,5},{8,10},{9,11},{10,... | collective-permute-start | bytes 786440 | tf_op jit(solution)/shard_map/ppermute | solution.py:222
  26.9 46.6 %copy-start.3 = (s32[32]{0:T(128)S(1)}, s32[32]{0:T(128)}, u32[]{:S(2)}) copy-start(s32[32]{0:T(128)} %param.7) | copy-start | bytes 388
  34.4 9.2 %collective-permute-start.4 = (f32[64,256]{1,0:T(8,128)S(1)}, f32[64,256]{1,0:T(8,128)S(1)}, u32[]{:S(2)}, u32[]{:S(2)}) collective-permute-start(f32[64,256]{1,0:T(8,128)S(1)} %get-tuple-element.31), channel_id=1, source_target_pairs={{0,4},{1,5},{2,6},{3,7},{4,8},{5,9},{6,10},{7,11},{8,12},{9,13},{1... | collective-permute-start | bytes 196616 | tf_op jit(solution)/shard_map/ppermute | solution.py:228
  40.6 9.2 %collective-permute-start.3 = (f32[64,256]{1,0:T(8,128)S(1)}, f32[64,256]{1,0:T(8,128)S(1)}, u32[]{:S(2)}, u32[]{:S(2)}) collective-permute-start(f32[64,256]{1,0:T(8,128)S(1)} %get-tuple-element.30), channel_id=1, source_target_pairs={{0,12},{1,13},{2,14},{3,15},{4,0},{5,1},{6,2},{7,3},{8,4},{9,5},{1... | collective-permute-start | bytes 196616 | tf_op jit(solution)/shard_map/ppermute | solution.py:228
  43.6 10.8 %collective-permute-start.5 = (f32[64,256]{1,0:T(8,128)S(1)}, f32[64,256]{1,0:T(8,128)S(1)}, u32[]{:S(2)}, u32[]{:S(2)}) collective-permute-start(f32[64,256]{1,0:T(8,128)S(1)} %slice_add_fusion), channel_id=1, source_target_pairs={{0,4},{1,5},{2,6},{3,7},{4,8},{5,9},{6,10},{7,11},{8,12},{9,13},{1... | collective-permute-start | bytes 196616 | tf_op jit(solution)/shard_map/ppermute | solution.py:228
  71.6 26.3 %collective-permute-start.6 = (f32[256,256]{1,0:T(8,128)S(1)}, f32[256,256]{1,0:T(8,128)}, u32[]{:S(2)}, u32[]{:S(2)}) collective-permute-start(f32[256,256]{1,0:T(8,128)S(1)} %all_gather.3.quarter_ref.refs_3_), channel_id=1, source_target_pairs={{0,2},{1,3},{2,0},{3,1},{4,6},{5,7},{6,4},{7,5},{8,10},{9,11},{10,... | collective-permute-start | bytes 786440 | tf_op jit(solution)/shard_map/ppermute | solution.py:222
  98.6 12.1 %all-to-all-start.1 = ((f32[4,8,256]{2,1,0:T(8,128)}), f32[4,8,256]{2,1,0:T(8,128)S(1)}, u32[]{:S(2)}, u32[]{:S(2)}) async-start(f32[4,8,256]{2,1,0:T(8,128)} %sum_and_repeat.1), calls=%async_computation.1 | async-start | bytes 65536 | tf_op jit(solution)/shard_map/all_to_all | solution.py:236
  104.1 11.6 %collective-permute-start.7 = (f32[256,256]{1,0:T(8,128)}, f32[256,256]{1,0:T(8,128)}, u32[]{:S(2)}, u32[]{:S(2)}) collective-permute-start(f32[256,256]{1,0:T(8,128)} %collective-permute-done.6.refs_2_), channel_id=1, source_target_pairs={{0,1},{1,0},{2,3},{3,2},{4,5},{5,4},{6,7},{7,6},{8,9},{9,8},{10,11... | collective-permute-start | bytes 786440 | tf_op jit(solution)/shard_map/ppermute | solution.py:222
  106.8 8.9 %collective-permute-start.8 = (f32[256,256]{1,0:T(8,128)S(1)}, f32[256,256]{1,0:T(8,128)}, u32[]{:S(2)}, u32[]{:S(2)}) collective-permute-start(f32[256,256]{1,0:T(8,128)S(1)} %all_gather.3.quarter_ref.refs_3_), channel_id=1, source_target_pairs={{0,1},{1,0},{2,3},{3,2},{4,5},{5,4},{6,7},{7,6},{8,9},{9,8},{10,11... | collective-permute-start | bytes 786440 | tf_op jit(solution)/shard_map/ppermute | solution.py:222
  111.4 13.2 %all-to-all-start.2 = ((f32[32,8,256]{2,1,0:T(8,128)}), f32[32,8,256]{2,1,0:T(8,128)}, u32[]{:S(2)}, u32[]{:S(2)}) async-start(f32[32,8,256]{2,1,0:T(8,128)} %broadcast_in_dim.3), calls=%async_computation.2 | async-start | bytes 524288 | tf_op jit(solution)/shard_map/all_to_all | solution.py:236
  188.7 4.2 %collective-permute-start.9 = (f32[16,8,1536]{2,1,0:T(8,128)S(1)}, f32[16,8,1536]{2,1,0:T(8,128)S(1)}, u32[]{:S(2)}, u32[]{:S(2)}) collective-permute-start(f32[16,8,1536]{2,1,0:T(8,128)S(1)} %get-tuple-element.29), channel_id=1, source_target_pairs={{0,16},{16,0},{1,17},{17,1},{2,18},{18,2},{3,19},{19,3},{4,20},{20... | collective-permute-start | bytes 2359304 | tf_op jit(solution)/shard_map/ppermute | solution.py:232

commit v14 on v13

--- a/solution.py
+++ b/solution.py
@@ -271,9 +271,10 @@
     gram = on_core(gram_kernel, jax.ShapeDtypeStruct(square, F32), "gram_part")(counts, quarter)
     gram_rows = each_to_each(gram.reshape(texels, width // texels, width), TEXEL)
     gram_rows, near, quarter = lax.optimization_barrier((gram_rows, near, quarter))
-    beyond, beside = across(near, 1), across(quarter, 1)
+    beyond = across(near, 1)
     gram_rows = sum_to_each(gram_rows, ("z1", "z0"))
-    gram_rows = jnp.sum(gram_rows, axis=0)
+    gram_rows, quarter = lax.optimization_barrier((jnp.sum(gram_rows, axis=0), quarter))
+    beside = across(quarter, 1)
     gram = each_to_each(jnp.broadcast_to(gram_rows, (texels, *gram_rows.shape)), TEXEL).reshape(square)
 
     lines, chips = width // texels, lax.axis_size(CHIP)

time: 211 us -> 212 us (level)
  waiting for transfers between devices: 21.2 us -> 23.4 us
    all_to_all x2, waiting for transfers between devices: 8.74 us -> 10.9 us  [each_to_each(): return lax.all_to_all(parts, axes, 0, 0, tiled=True)]
  transfers between devices with their start and end apart: 12 -> 12, of which waited for: 5 -> 6; matrix products, arithmetic and copies ran while one was open for 0% -> 0% of each run, Pallas kernels for 2% -> 2%
where the time goes in v14:
time: 212 us
  Pallas kernels  71.2 us (34%)
  blocking collectives  57.1 us (27%)
  starting transfers between devices  53.7 us (25%)
  waiting for transfers between devices  23.4 us (11%)
  local copies, waits for them, and re-layouts  4.5 us (2%)
    pallas_call x7, Pallas kernels, on_core(): pl.pallas_call(kernel, out_shape=out_shape, in_specs=[VMEM] * len(operand...  71.2 us
    all_to_all x2, blocking collectives, each_to_each(): return lax.all_to_all(parts, axes, 0, 0, tiled=True)  40 us
    ppermute x6, starting transfers between devices, across(): lax.ppermute(value, ('core', *LIGHT), light_pairs(lax.axis_size(LIGHT), r...  24.3 us
    all_gather x1, blocking collectives, on_device(): quarter = lax.all_gather(share, FAR, axis=0, tiled=True)  17.1 us
    ppermute x3, starting transfers between devices, onward(): return lax.ppermute(value, ('core', *LIGHT), pairs)  15.4 us
    all_to_all x2, starting transfers between devices, each_to_each(): return lax.all_to_all(parts, axes, 0, 0, tiled=True)  12 us
    all_to_all x2, waiting for transfers between devices, each_to_each(): return lax.all_to_all(parts, axes, 0, 0, tiled=True)  10.9 us
    ppermute x6, waiting for transfers between devices, across(): lax.ppermute(value, ('core', *LIGHT), light_pairs(lax.axis_size(LIGHT), r...  5.81 us
  transfers between devices with their start and end apart: 12, of which 6 were waited for; matrix products, arithmetic and copies ran while one was open for 0% of the time, Pallas kernels for 2%

profile of v14, /device:TPU:1, one launch (start us, length us, event | category | flops | bytes accessed | tf_op | source)
XLA Modules:
  0.0 211.7 jit_solution(12450896608277823121)
XLA Ops:
  0.6 1.4 copy-done
  2.0 1.2 copy-done.1
  3.3 1.1 copy-done.2
  4.4 1.6 tile_quarter.4
  6.0 11.9 %collective-permute-start.1 = (f32[256,256]{1,0:T(8,128)S(1)}, f32[256,256]{1,0:T(8,128)S(1)}, u32[]{:S(2)}, u32[]{:S(2)}) collective-permute-start(f32[256,256]{1,0:T(8,128)S(1)} %get-tuple-element.24), channel_id=1, source_target_pairs={{0,1},{1,0},{2,3},{3,2},{4,5},{5,4},{6,7},{7,6},{8,9},{9,8},{10,11... | collective-permute-start | bytes 786440 | tf_op jit(solution)/shard_map/ppermute | solution.py:222
  17.9 1.6 tile_quarter.5
  19.5 1.6 tile_quarter.6
  21.1 1.9 collective-permute-start
  23.1 3.8 %collective-permute-start.2 = (f32[256,256]{1,0:T(8,128)S(1)}, f32[256,256]{1,0:T(8,128)S(1)}, u32[]{:S(2)}, u32[]{:S(2)}) collective-permute-start(f32[256,256]{1,0:T(8,128)S(1)} %add.22), channel_id=1, source_target_pairs={{0,2},{1,3},{2,0},{3,1},{4,6},{5,7},{6,4},{7,5},{8,10},{9,11},{10,... | collective-permute-start | bytes 786440 | tf_op jit(solution)/shard_map/ppermute | solution.py:222
  26.9 1.6 tile_quarter.7
  28.5 1.1 collective-permute-done
  29.6 4.7 %collective-permute-done.2 = f32[256,256]{1,0:T(8,128)S(1)} collective-permute-done((f32[256,256]{1,0:T(8,128)S(1)}, f32[256,256]{1,0:T(8,128)S(1)}, u32[]{:S(2)}, u32[]{:S(2)}) %collective-permute-start.2) | collective-permute-done | bytes 262176 | tf_op jit(solution)/shard_map/ppermute | solution.py:222
  34.4 6.2 %collective-permute-start.4 = (f32[64,256]{1,0:T(8,128)S(1)}, f32[64,256]{1,0:T(8,128)S(1)}, u32[]{:S(2)}, u32[]{:S(2)}) collective-permute-start(f32[64,256]{1,0:T(8,128)S(1)} %get-tuple-element.35), channel_id=1, source_target_pairs={{0,4},{1,5},{2,6},{3,7},{4,8},{5,9},{6,10},{7,11},{8,12},{9,13},{1... | collective-permute-start | bytes 196616 | tf_op jit(solution)/shard_map/ppermute | solution.py:228
  40.6 3.0 %collective-permute-start.3 = (f32[64,256]{1,0:T(8,128)S(1)}, f32[64,256]{1,0:T(8,128)S(1)}, u32[]{:S(2)}, u32[]{:S(2)}) collective-permute-start(f32[64,256]{1,0:T(8,128)S(1)} %get-tuple-element.34), channel_id=1, source_target_pairs={{0,12},{1,13},{2,14},{3,15},{4,0},{5,1},{6,2},{7,3},{8,4},{9,5},{1... | collective-permute-start | bytes 196616 | tf_op jit(solution)/shard_map/ppermute | solution.py:228
  43.6 6.2 %collective-permute-start.5 = (f32[64,256]{1,0:T(8,128)S(1)}, f32[64,256]{1,0:T(8,128)S(1)}, u32[]{:S(2)}, u32[]{:S(2)}) collective-permute-start(f32[64,256]{1,0:T(8,128)S(1)} %slice_add_fusion), channel_id=1, source_target_pairs={{0,4},{1,5},{2,6},{3,7},{4,8},{5,9},{6,10},{7,11},{8,12},{9,13},{1... | collective-permute-start | bytes 196616 | tf_op jit(solution)/shard_map/ppermute | solution.py:228
  49.8 4.6 %collective-permute-done.5 = f32[64,256]{1,0:T(8,128)S(1)} collective-permute-done((f32[64,256]{1,0:T(8,128)S(1)}, f32[64,256]{1,0:T(8,128)S(1)}, u32[]{:S(2)}, u32[]{:S(2)}) %collective-permute-start.5) | collective-permute-done | bytes 65568 | tf_op jit(solution)/shard_map/ppermute | solution.py:228
  54.4 17.1 %all_gather.3.quarter_ref.refs_3_ = f32[256,256]{1,0:T(8,128)S(1)} all-gather(f32[64,256]{1,0:T(8,128)S(1)} %fusion), channel_id=1, replica_groups=mesh['x'=4,'y'=4,'core'=2,'z3'=2,'z2'=2,'z1'=2,'z0'=2] {'z3','z2'}, dimensions={0}, use_global_device_ids=true | all-gather | bytes 327680 | tf_op jit(solution)/shard_map/all_gather | solution.py:269
  71.6 1.9 collective-permute-start.6
  73.9 24.0 %all_to_all.20.parts_ref = f32[32,8,256]{2,1,0:T(8,128)S(1)} all-to-all(f32[32,8,256]{2,1,0:T(8,128)S(1)} %bitcast.3), channel_id=1, replica_groups=mesh['x'=4,'y'=4,'core'=2,'z3'=2,'z2'=2,'z1'=2,'z0'=2] {'x','y','core'}, dimensions={0} | all-to-all | bytes 524288 | tf_op jit(solution)/shard_map/all_to_all | solution.py:236
  97.9 0.7 sum_and_repeat.1
  98.6 5.5 %all-to-all-start.1 = ((f32[4,8,256]{2,1,0:T(8,128)}), f32[4,8,256]{2,1,0:T(8,128)S(1)}, u32[]{:S(2)}, u32[]{:S(2)}) async-start(f32[4,8,256]{2,1,0:T(8,128)} %sum_and_repeat.1), calls=%async_computation.1 | async-start | bytes 65536 | tf_op jit(solution)/shard_map/all_to_all | solution.py:236
  104.1 2.7 %collective-permute-start.7 = (f32[256,256]{1,0:T(8,128)}, f32[256,256]{1,0:T(8,128)}, u32[]{:S(2)}, u32[]{:S(2)}) collective-permute-start(f32[256,256]{1,0:T(8,128)} %collective-permute-done.6.refs_2_), channel_id=1, source_target_pairs={{0,1},{1,0},{2,3},{3,2},{4,5},{5,4},{6,7},{7,6},{8,9},{9,8},{10,11... | collective-permute-start | bytes 786440 | tf_op jit(solution)/shard_map/ppermute | solution.py:222
  106.8 1.8 all-to-all-done.1
  108.6 2.0 collective-permute-start.8
  110.6 0.7 broadcast_in_dim.3
  111.4 6.4 %all-to-all-start.2 = ((f32[32,8,256]{2,1,0:T(8,128)}), f32[32,8,256]{2,1,0:T(8,128)}, u32[]{:S(2)}, u32[]{:S(2)}) async-start(f32[32,8,256]{2,1,0:T(8,128)} %broadcast_in_dim.3), calls=%async_computation.2 | async-start | bytes 524288 | tf_op jit(solution)/shard_map/all_to_all | solution.py:236
  117.8 9.1 %all-to-all-done.2 = f32[32,8,256]{2,1,0:T(8,128)} async-done(((f32[32,8,256]{2,1,0:T(8,128)}), f32[32,8,256]{2,1,0:T(8,128)}, u32[]{:S(2)}, u32[]{:S(2)}) %all-to-all-start.2) | async-done | bytes 262176 | tf_op jit(solution)/shard_map/all_to_all | solution.py:236
  126.9 63.7 %basis_and_coeffs.1 = (f32[1024,256]{1,0:T(8,128)}, f32[16,8,1536]{2,1,0:T(8,128)S(1)}, f32[16,8,1536]{2,1,0:T(8,128)S(1)}) custom-call(s32[1,32]{1,0:T(1,128)S(1)} %bitcast.5, f32[256,256]{1,0:T(8,128)} %bitcast.2.gram_ref, f32[256,256]{1,0:T(8,128)} %collective-permute-done.7.refs_0_, f32[256,256]{1,0:T(8,128)} %collective-permute-done.8.refs_1_, ...), custom_call_target="tpu_custom_call" | custom-call | flops 1000000000 | bytes 1048576 | tf_op jit(solution)/shard_map/basis_and_coeffs/pallas_call | solution.py:56
  190.7 2.1 collective-permute-start.9
  192.8 2.1 collective-permute-done.9
  195.0 16.1 %all_to_all.21 = f32[16,8,1536]{2,1,0:T(8,128)S(1)} all-to-all(f32[16,8,1536]{2,1,0:T(8,128)S(1)} %add.27), channel_id=1, replica_groups=mesh['x'=4,'y'=4,'core'=2,'z3'=2,'z2'=2,'z1'=2,'z0'=2] {'x','y'}, dimensions={0} | all-to-all | bytes 1572864 | tf_op jit(solution)/shard_map/all_to_all | solution.py:236
  211.0 0.7 reduce_sum.19
  (19 shorter events, 0.7 us)
Async XLA Ops:
  0.6 1.4 copy-start
  2.0 1.2 copy-start.1
  3.3 1.1 copy-start.2
  6.0 17.1 %collective-permute-start.1 = (f32[256,256]{1,0:T(8,128)S(1)}, f32[256,256]{1,0:T(8,128)S(1)}, u32[]{:S(2)}, u32[]{:S(2)}) collective-permute-start(f32[256,256]{1,0:T(8,128)S(1)} %get-tuple-element.24), channel_id=1, source_target_pairs={{0,1},{1,0},{2,3},{3,2},{4,5},{5,4},{6,7},{7,6},{8,9},{9,8},{10,11... | collective-permute-start | bytes 786440 | tf_op jit(solution)/shard_map/ppermute | solution.py:222
  21.1 8.5 %collective-permute-start = (f32[256,256]{1,0:T(8,128)S(1)}, f32[256,256]{1,0:T(8,128)S(1)}, u32[]{:S(2)}, u32[]{:S(2)}) collective-permute-start(f32[256,256]{1,0:T(8,128)S(1)} %get-tuple-element.22), channel_id=1, source_target_pairs={{0,1},{1,0},{2,3},{3,2},{4,5},{5,4},{6,7},{7,6},{8,9},{9,8},{10,11... | collective-permute-start | bytes 786440 | tf_op jit(solution)/shard_map/ppermute | solution.py:222
  23.1 11.2 %collective-permute-start.2 = (f32[256,256]{1,0:T(8,128)S(1)}, f32[256,256]{1,0:T(8,128)S(1)}, u32[]{:S(2)}, u32[]{:S(2)}) collective-permute-start(f32[256,256]{1,0:T(8,128)S(1)} %add.22), channel_id=1, source_target_pairs={{0,2},{1,3},{2,0},{3,1},{4,6},{5,7},{6,4},{7,5},{8,10},{9,11},{10,... | collective-permute-start | bytes 786440 | tf_op jit(solution)/shard_map/ppermute | solution.py:222
  26.9 46.6 %copy-start.3 = (s32[32]{0:T(128)S(1)}, s32[32]{0:T(128)}, u32[]{:S(2)}) copy-start(s32[32]{0:T(128)} %param.7) | copy-start | bytes 388
  34.4 9.2 %collective-permute-start.4 = (f32[64,256]{1,0:T(8,128)S(1)}, f32[64,256]{1,0:T(8,128)S(1)}, u32[]{:S(2)}, u32[]{:S(2)}) collective-permute-start(f32[64,256]{1,0:T(8,128)S(1)} %get-tuple-element.35), channel_id=1, source_target_pairs={{0,4},{1,5},{2,6},{3,7},{4,8},{5,9},{6,10},{7,11},{8,12},{9,13},{1... | collective-permute-start | bytes 196616 | tf_op jit(solution)/shard_map/ppermute | solution.py:228
  40.6 9.2 %collective-permute-start.3 = (f32[64,256]{1,0:T(8,128)S(1)}, f32[64,256]{1,0:T(8,128)S(1)}, u32[]{:S(2)}, u32[]{:S(2)}) collective-permute-start(f32[64,256]{1,0:T(8,128)S(1)} %get-tuple-element.34), channel_id=1, source_target_pairs={{0,12},{1,13},{2,14},{3,15},{4,0},{5,1},{6,2},{7,3},{8,4},{9,5},{1... | collective-permute-start | bytes 196616 | tf_op jit(solution)/shard_map/ppermute | solution.py:228
  43.6 10.8 %collective-permute-start.5 = (f32[64,256]{1,0:T(8,128)S(1)}, f32[64,256]{1,0:T(8,128)S(1)}, u32[]{:S(2)}, u32[]{:S(2)}) collective-permute-start(f32[64,256]{1,0:T(8,128)S(1)} %slice_add_fusion), channel_id=1, source_target_pairs={{0,4},{1,5},{2,6},{3,7},{4,8},{5,9},{6,10},{7,11},{8,12},{9,13},{1... | collective-permute-start | bytes 196616 | tf_op jit(solution)/shard_map/ppermute | solution.py:228
  71.6 26.3 %collective-permute-start.6 = (f32[256,256]{1,0:T(8,128)S(1)}, f32[256,256]{1,0:T(8,128)}, u32[]{:S(2)}, u32[]{:S(2)}) collective-permute-start(f32[256,256]{1,0:T(8,128)S(1)} %all_gather.3.quarter_ref.refs_3_), channel_id=1, source_target_pairs={{0,2},{1,3},{2,0},{3,1},{4,6},{5,7},{6,4},{7,5},{8,10},{9,11},{10,... | collective-permute-start | bytes 786440 | tf_op jit(solution)/shard_map/ppermute | solution.py:222
  98.6 10.1 %all-to-all-start.1 = ((f32[4,8,256]{2,1,0:T(8,128)}), f32[4,8,256]{2,1,0:T(8,128)S(1)}, u32[]{:S(2)}, u32[]{:S(2)}) async-start(f32[4,8,256]{2,1,0:T(8,128)} %sum_and_repeat.1), calls=%async_computation.1 | async-start | bytes 65536 | tf_op jit(solution)/shard_map/all_to_all | solution.py:236
  104.1 13.7 %collective-permute-start.7 = (f32[256,256]{1,0:T(8,128)}, f32[256,256]{1,0:T(8,128)}, u32[]{:S(2)}, u32[]{:S(2)}) collective-permute-start(f32[256,256]{1,0:T(8,128)} %collective-permute-done.6.refs_2_), channel_id=1, source_target_pairs={{0,1},{1,0},{2,3},{3,2},{4,5},{5,4},{6,7},{7,6},{8,9},{9,8},{10,11... | collective-permute-start | bytes 786440 | tf_op jit(solution)/shard_map/ppermute | solution.py:222
  108.6 18.3 %collective-permute-start.8 = (f32[256,256]{1,0:T(8,128)S(1)}, f32[256,256]{1,0:T(8,128)}, u32[]{:S(2)}, u32[]{:S(2)}) collective-permute-start(f32[256,256]{1,0:T(8,128)S(1)} %all_gather.3.quarter_ref.refs_3_), channel_id=1, source_target_pairs={{0,1},{1,0},{2,3},{3,2},{4,5},{5,4},{6,7},{7,6},{8,9},{9,8},{10,11... | collective-permute-start | bytes 786440 | tf_op jit(solution)/shard_map/ppermute | solution.py:222
  111.4 15.6 %all-to-all-start.2 = ((f32[32,8,256]{2,1,0:T(8,128)}), f32[32,8,256]{2,1,0:T(8,128)}, u32[]{:S(2)}, u32[]{:S(2)}) async-start(f32[32,8,256]{2,1,0:T(8,128)} %broadcast_in_dim.3), calls=%async_computation.2 | async-start | bytes 524288 | tf_op jit(solution)/shard_map/all_to_all | solution.py:236
  190.7 4.2 %collective-permute-start.9 = (f32[16,8,1536]{2,1,0:T(8,128)S(1)}, f32[16,8,1536]{2,1,0:T(8,128)S(1)}, u32[]{:S(2)}, u32[]{:S(2)}) collective-permute-start(f32[16,8,1536]{2,1,0:T(8,128)S(1)} %get-tuple-element.33), channel_id=1, source_target_pairs={{0,16},{16,0},{1,17},{17,1},{2,18},{18,2},{3,19},{19,3},{4,20},{20... | collective-permute-start | bytes 2359304 | tf_op jit(solution)/shard_map/ppermute | solution.py:232

commit v15 on v13

--- a/solution.py
+++ b/solution.py
@@ -89,7 +89,7 @@
     return dot(a_high, b_high, contract) + (dot(a_high, b_low, contract) + dot(a_low, b_high, contract))
 
 
-def tile_kernel(tex_ref, light_ref, sketch_ref, *refs, order, step=128):
+def tile_kernel(tex_ref, light_ref, sketch_ref, *refs, order, step=256, span=512):
     tile_ref, part_ref = refs[-2:]
     rows, groups = part_ref.shape[0], lax.axis_size(FAR)
     share = rows // groups
@@ -103,9 +103,12 @@
     onward = 1 - 2 * lax.axis_index("core")
     for at in range(0, rows, step):
         tex = tex_ref[pl.ds(pl.multiple_of(first + at, step), step), :]
-        tile = sine(dot(tex, light_ref[...], (1, 1))).astype(BF16)
-        tile_ref[order * rows + at : order * rows + at + step, :] = tile
-        part = dot(tile, sketch_ref[...], (1, 0))
+        part = None
+        for to in range(0, light_ref.shape[0], span):
+            tile = sine(dot(tex, light_ref[to : to + span, :], (1, 1))).astype(BF16)
+            tile_ref[order * rows + at : order * rows + at + step, to : to + span] = tile
+            product = dot(tile, sketch_ref[to : to + span, :], (1, 0))
+            part = product if part is None else part + product
         for i in range(step // share):
             turn = (onward * (at // share + i - holder) + groups) % groups
             part_ref[pl.ds(pl.multiple_of(turn * share, share), share), :] = part[i * share : (i + 1) * share, :]

time: 211 us -> 210 us (level)
  no operation moved by 1% of the time
where the time goes in v15:
time: 210 us; the launch traced here: 209 us
  Pallas kernels  70.5 us (34%)
  blocking collectives  58.6 us (28%)
  starting transfers between devices  51.9 us (25%)
  waiting for transfers between devices  21.3 us (10%)
  local copies, waits for them, and re-layouts  4.5 us (2%)
    pallas_call x7, Pallas kernels, on_core(): pl.pallas_call(kernel, out_shape=out_shape, in_specs=[VMEM] * len(operand...  70.5 us
    all_to_all x2, blocking collectives, each_to_each(): return lax.all_to_all(parts, axes, 0, 0, tiled=True)  41 us
    ppermute x6, starting transfers between devices, across(): lax.ppermute(value, ('core', *LIGHT), light_pairs(lax.axis_size(LIGHT), r...  26.1 us
    all_gather x1, blocking collectives, on_device(): quarter = lax.all_gather(share, FAR, axis=0, tiled=True)  17.6 us
    ppermute x3, starting transfers between devices, onward(): return lax.ppermute(value, ('core', *LIGHT), pairs)  15.4 us
    all_to_all x2, waiting for transfers between devices, each_to_each(): return lax.all_to_all(parts, axes, 0, 0, tiled=True)  8.74 us
    all_to_all x2, starting transfers between devices, each_to_each(): return lax.all_to_all(parts, axes, 0, 0, tiled=True)  8.35 us
    ppermute x6, waiting for transfers between devices, across(): lax.ppermute(value, ('core', *LIGHT), light_pairs(lax.axis_size(LIGHT), r...  6.02 us
  transfers between devices with their start and end apart: 12, of which 5 were waited for; matrix products, arithmetic and copies ran while one was open for 0% of the time, Pallas kernels for 2%

profile of v15, /device:TPU:1, one launch (start us, length us, event | category | flops | bytes accessed | tf_op | source)
XLA Modules:
  0.0 208.6 jit_solution(709615765644032827)
XLA Ops:
  0.6 1.4 copy-done
  2.0 1.2 copy-done.1
  3.3 1.1 copy-done.2
  4.4 1.4 tile_quarter.4
  5.8 12.0 %collective-permute-start.1 = (f32[256,256]{1,0:T(8,128)S(1)}, f32[256,256]{1,0:T(8,128)S(1)}, u32[]{:S(2)}, u32[]{:S(2)}) collective-permute-start(f32[256,256]{1,0:T(8,128)S(1)} %get-tuple-element.22), channel_id=1, source_target_pairs={{0,1},{1,0},{2,3},{3,2},{4,5},{5,4},{6,7},{7,6},{8,9},{9,8},{10,11... | collective-permute-start | bytes 786440 | tf_op jit(solution)/shard_map/ppermute | solution.py:225
  17.8 1.4 tile_quarter.5
  19.2 1.4 tile_quarter.6
  20.6 1.9 collective-permute-start
  22.6 3.8 %collective-permute-start.2 = (f32[256,256]{1,0:T(8,128)S(1)}, f32[256,256]{1,0:T(8,128)S(1)}, u32[]{:S(2)}, u32[]{:S(2)}) collective-permute-start(f32[256,256]{1,0:T(8,128)S(1)} %add.22), channel_id=1, source_target_pairs={{0,2},{1,3},{2,0},{3,1},{4,6},{5,7},{6,4},{7,5},{8,10},{9,11},{10,... | collective-permute-start | bytes 786440 | tf_op jit(solution)/shard_map/ppermute | solution.py:225
  26.4 1.4 tile_quarter.7
  27.8 1.3 collective-permute-done
  29.1 4.7 %collective-permute-done.2 = f32[256,256]{1,0:T(8,128)S(1)} collective-permute-done((f32[256,256]{1,0:T(8,128)S(1)}, f32[256,256]{1,0:T(8,128)S(1)}, u32[]{:S(2)}, u32[]{:S(2)}) %collective-permute-start.2) | collective-permute-done | bytes 262176 | tf_op jit(solution)/shard_map/ppermute | solution.py:225
  33.9 6.2 %collective-permute-start.4 = (f32[64,256]{1,0:T(8,128)S(1)}, f32[64,256]{1,0:T(8,128)S(1)}, u32[]{:S(2)}, u32[]{:S(2)}) collective-permute-start(f32[64,256]{1,0:T(8,128)S(1)} %get-tuple-element.31), channel_id=1, source_target_pairs={{0,4},{1,5},{2,6},{3,7},{4,8},{5,9},{6,10},{7,11},{8,12},{9,13},{1... | collective-permute-start | bytes 196616 | tf_op jit(solution)/shard_map/ppermute | solution.py:231
  40.1 3.0 %collective-permute-start.3 = (f32[64,256]{1,0:T(8,128)S(1)}, f32[64,256]{1,0:T(8,128)S(1)}, u32[]{:S(2)}, u32[]{:S(2)}) collective-permute-start(f32[64,256]{1,0:T(8,128)S(1)} %get-tuple-element.30), channel_id=1, source_target_pairs={{0,12},{1,13},{2,14},{3,15},{4,0},{5,1},{6,2},{7,3},{8,4},{9,5},{1... | collective-permute-start | bytes 196616 | tf_op jit(solution)/shard_map/ppermute | solution.py:231
  43.1 6.2 %collective-permute-start.5 = (f32[64,256]{1,0:T(8,128)S(1)}, f32[64,256]{1,0:T(8,128)S(1)}, u32[]{:S(2)}, u32[]{:S(2)}) collective-permute-start(f32[64,256]{1,0:T(8,128)S(1)} %slice_add_fusion), channel_id=1, source_target_pairs={{0,4},{1,5},{2,6},{3,7},{4,8},{5,9},{6,10},{7,11},{8,12},{9,13},{1... | collective-permute-start | bytes 196616 | tf_op jit(solution)/shard_map/ppermute | solution.py:231
  49.4 4.5 %collective-permute-done.5 = f32[64,256]{1,0:T(8,128)S(1)} collective-permute-done((f32[64,256]{1,0:T(8,128)S(1)}, f32[64,256]{1,0:T(8,128)S(1)}, u32[]{:S(2)}, u32[]{:S(2)}) %collective-permute-start.5) | collective-permute-done | bytes 65568 | tf_op jit(solution)/shard_map/ppermute | solution.py:231
  53.9 17.6 %all_gather.3.quarter_ref.refs_3_ = f32[256,256]{1,0:T(8,128)S(1)} all-gather(f32[64,256]{1,0:T(8,128)S(1)} %fusion), channel_id=1, replica_groups=mesh['x'=4,'y'=4,'core'=2,'z3'=2,'z2'=2,'z1'=2,'z0'=2] {'z3','z2'}, dimensions={0}, use_global_device_ids=true | all-gather | bytes 327680 | tf_op jit(solution)/shard_map/all_gather | solution.py:272
  71.5 1.9 collective-permute-start.6
  73.5 0.4 gram_part.1
  73.9 24.9 %all_to_all.20.parts_ref = f32[32,8,256]{2,1,0:T(8,128)S(1)} all-to-all(f32[32,8,256]{2,1,0:T(8,128)S(1)} %bitcast.3), channel_id=1, replica_groups=mesh['x'=4,'y'=4,'core'=2,'z3'=2,'z2'=2,'z1'=2,'z0'=2] {'x','y','core'}, dimensions={0} | all-to-all | bytes 524288 | tf_op jit(solution)/shard_map/all_to_all | solution.py:239
  98.9 0.7 sum_and_repeat.1
  99.5 4.0 %all-to-all-start.1 = ((f32[4,8,256]{2,1,0:T(8,128)}), f32[4,8,256]{2,1,0:T(8,128)S(1)}, u32[]{:S(2)}, u32[]{:S(2)}) async-start(f32[4,8,256]{2,1,0:T(8,128)} %sum_and_repeat.1), calls=%async_computation.1 | async-start | bytes 65536 | tf_op jit(solution)/shard_map/all_to_all | solution.py:239
  103.5 2.7 %collective-permute-start.7 = (f32[256,256]{1,0:T(8,128)}, f32[256,256]{1,0:T(8,128)}, u32[]{:S(2)}, u32[]{:S(2)}) collective-permute-start(f32[256,256]{1,0:T(8,128)} %collective-permute-done.6.refs_2_), channel_id=1, source_target_pairs={{0,1},{1,0},{2,3},{3,2},{4,5},{5,4},{6,7},{7,6},{8,9},{9,8},{10,11... | collective-permute-start | bytes 786440 | tf_op jit(solution)/shard_map/ppermute | solution.py:225
  106.2 3.7 %collective-permute-start.8 = (f32[256,256]{1,0:T(8,128)S(1)}, f32[256,256]{1,0:T(8,128)}, u32[]{:S(2)}, u32[]{:S(2)}) collective-permute-start(f32[256,256]{1,0:T(8,128)S(1)} %all_gather.3.quarter_ref.refs_3_), channel_id=1, source_target_pairs={{0,1},{1,0},{2,3},{3,2},{4,5},{5,4},{6,7},{7,6},{8,9},{9,8},{10,11... | collective-permute-start | bytes 786440 | tf_op jit(solution)/shard_map/ppermute | solution.py:225
  110.0 0.7 broadcast_in_dim.3
  110.7 4.4 %all-to-all-start.2 = ((f32[32,8,256]{2,1,0:T(8,128)}), f32[32,8,256]{2,1,0:T(8,128)}, u32[]{:S(2)}, u32[]{:S(2)}) async-start(f32[32,8,256]{2,1,0:T(8,128)} %broadcast_in_dim.3), calls=%async_computation.2 | async-start | bytes 524288 | tf_op jit(solution)/shard_map/all_to_all | solution.py:239
  115.1 8.7 %all-to-all-done.2 = f32[32,8,256]{2,1,0:T(8,128)} async-done(((f32[32,8,256]{2,1,0:T(8,128)}), f32[32,8,256]{2,1,0:T(8,128)}, u32[]{:S(2)}, u32[]{:S(2)}) %all-to-all-start.2) | async-done | bytes 262176 | tf_op jit(solution)/shard_map/all_to_all | solution.py:239
  123.9 63.7 %basis_and_coeffs.1 = (f32[1024,256]{1,0:T(8,128)}, f32[16,8,1536]{2,1,0:T(8,128)S(1)}, f32[16,8,1536]{2,1,0:T(8,128)S(1)}) custom-call(s32[1,32]{1,0:T(1,128)S(1)} %bitcast.5, f32[256,256]{1,0:T(8,128)} %bitcast.2.gram_ref, f32[256,256]{1,0:T(8,128)} %collective-permute-done.7.refs_0_, f32[256,256]{1,0:T(8,128)} %collective-permute-done.8.refs_1_, ...), custom_call_target="tpu_custom_call" | custom-call | flops 1000000000 | bytes 1048576 | tf_op jit(solution)/shard_map/basis_and_coeffs/pallas_call | solution.py:56
  187.6 2.1 collective-permute-start.9
  189.7 2.1 collective-permute-done.9
  191.9 16.1 %all_to_all.21 = f32[16,8,1536]{2,1,0:T(8,128)S(1)} all-to-all(f32[16,8,1536]{2,1,0:T(8,128)S(1)} %add.27), channel_id=1, replica_groups=mesh['x'=4,'y'=4,'core'=2,'z3'=2,'z2'=2,'z1'=2,'z0'=2] {'x','y'}, dimensions={0} | all-to-all | bytes 1572864 | tf_op jit(solution)/shard_map/all_to_all | solution.py:239
  208.0 0.7 reduce_sum.19
  (19 shorter events, 0.3 us)
Async XLA Ops:
  0.6 1.4 copy-start
  2.0 1.2 copy-start.1
  3.3 1.1 copy-start.2
  5.8 16.7 %collective-permute-start.1 = (f32[256,256]{1,0:T(8,128)S(1)}, f32[256,256]{1,0:T(8,128)S(1)}, u32[]{:S(2)}, u32[]{:S(2)}) collective-permute-start(f32[256,256]{1,0:T(8,128)S(1)} %get-tuple-element.22), channel_id=1, source_target_pairs={{0,1},{1,0},{2,3},{3,2},{4,5},{5,4},{6,7},{7,6},{8,9},{9,8},{10,11... | collective-permute-start | bytes 786440 | tf_op jit(solution)/shard_map/ppermute | solution.py:225
  20.6 8.5 %collective-permute-start = (f32[256,256]{1,0:T(8,128)S(1)}, f32[256,256]{1,0:T(8,128)S(1)}, u32[]{:S(2)}, u32[]{:S(2)}) collective-permute-start(f32[256,256]{1,0:T(8,128)S(1)} %get-tuple-element.20), channel_id=1, source_target_pairs={{0,1},{1,0},{2,3},{3,2},{4,5},{5,4},{6,7},{7,6},{8,9},{9,8},{10,11... | collective-permute-start | bytes 786440 | tf_op jit(solution)/shard_map/ppermute | solution.py:225
  22.6 11.2 %collective-permute-start.2 = (f32[256,256]{1,0:T(8,128)S(1)}, f32[256,256]{1,0:T(8,128)S(1)}, u32[]{:S(2)}, u32[]{:S(2)}) collective-permute-start(f32[256,256]{1,0:T(8,128)S(1)} %add.22), channel_id=1, source_target_pairs={{0,2},{1,3},{2,0},{3,1},{4,6},{5,7},{6,4},{7,5},{8,10},{9,11},{10,... | collective-permute-start | bytes 786440 | tf_op jit(solution)/shard_map/ppermute | solution.py:225
  26.4 47.1 %copy-start.3 = (s32[32]{0:T(128)S(1)}, s32[32]{0:T(128)}, u32[]{:S(2)}) copy-start(s32[32]{0:T(128)} %param.7) | copy-start | bytes 388
  33.9 9.2 %collective-permute-start.4 = (f32[64,256]{1,0:T(8,128)S(1)}, f32[64,256]{1,0:T(8,128)S(1)}, u32[]{:S(2)}, u32[]{:S(2)}) collective-permute-start(f32[64,256]{1,0:T(8,128)S(1)} %get-tuple-element.31), channel_id=1, source_target_pairs={{0,4},{1,5},{2,6},{3,7},{4,8},{5,9},{6,10},{7,11},{8,12},{9,13},{1... | collective-permute-start | bytes 196616 | tf_op jit(solution)/shard_map/ppermute | solution.py:231
  40.1 9.3 %collective-permute-start.3 = (f32[64,256]{1,0:T(8,128)S(1)}, f32[64,256]{1,0:T(8,128)S(1)}, u32[]{:S(2)}, u32[]{:S(2)}) collective-permute-start(f32[64,256]{1,0:T(8,128)S(1)} %get-tuple-element.30), channel_id=1, source_target_pairs={{0,12},{1,13},{2,14},{3,15},{4,0},{5,1},{6,2},{7,3},{8,4},{9,5},{1... | collective-permute-start | bytes 196616 | tf_op jit(solution)/shard_map/ppermute | solution.py:231
  43.1 10.7 %collective-permute-start.5 = (f32[64,256]{1,0:T(8,128)S(1)}, f32[64,256]{1,0:T(8,128)S(1)}, u32[]{:S(2)}, u32[]{:S(2)}) collective-permute-start(f32[64,256]{1,0:T(8,128)S(1)} %slice_add_fusion), channel_id=1, source_target_pairs={{0,4},{1,5},{2,6},{3,7},{4,8},{5,9},{6,10},{7,11},{8,12},{9,13},{1... | collective-permute-start | bytes 196616 | tf_op jit(solution)/shard_map/ppermute | solution.py:231
  71.5 27.3 %collective-permute-start.6 = (f32[256,256]{1,0:T(8,128)S(1)}, f32[256,256]{1,0:T(8,128)}, u32[]{:S(2)}, u32[]{:S(2)}) collective-permute-start(f32[256,256]{1,0:T(8,128)S(1)} %all_gather.3.quarter_ref.refs_3_), channel_id=1, source_target_pairs={{0,2},{1,3},{2,0},{3,1},{4,6},{5,7},{6,4},{7,5},{8,10},{9,11},{10,... | collective-permute-start | bytes 786440 | tf_op jit(solution)/shard_map/ppermute | solution.py:225
  99.5 10.5 %all-to-all-start.1 = ((f32[4,8,256]{2,1,0:T(8,128)}), f32[4,8,256]{2,1,0:T(8,128)S(1)}, u32[]{:S(2)}, u32[]{:S(2)}) async-start(f32[4,8,256]{2,1,0:T(8,128)} %sum_and_repeat.1), calls=%async_computation.1 | async-start | bytes 65536 | tf_op jit(solution)/shard_map/all_to_all | solution.py:239
  103.5 11.6 %collective-permute-start.7 = (f32[256,256]{1,0:T(8,128)}, f32[256,256]{1,0:T(8,128)}, u32[]{:S(2)}, u32[]{:S(2)}) collective-permute-start(f32[256,256]{1,0:T(8,128)} %collective-permute-done.6.refs_2_), channel_id=1, source_target_pairs={{0,1},{1,0},{2,3},{3,2},{4,5},{5,4},{6,7},{7,6},{8,9},{9,8},{10,11... | collective-permute-start | bytes 786440 | tf_op jit(solution)/shard_map/ppermute | solution.py:225
  106.2 8.9 %collective-permute-start.8 = (f32[256,256]{1,0:T(8,128)S(1)}, f32[256,256]{1,0:T(8,128)}, u32[]{:S(2)}, u32[]{:S(2)}) collective-permute-start(f32[256,256]{1,0:T(8,128)S(1)} %all_gather.3.quarter_ref.refs_3_), channel_id=1, source_target_pairs={{0,1},{1,0},{2,3},{3,2},{4,5},{5,4},{6,7},{7,6},{8,9},{9,8},{10,11... | collective-permute-start | bytes 786440 | tf_op jit(solution)/shard_map/ppermute | solution.py:225
  110.7 13.2 %all-to-all-start.2 = ((f32[32,8,256]{2,1,0:T(8,128)}), f32[32,8,256]{2,1,0:T(8,128)}, u32[]{:S(2)}, u32[]{:S(2)}) async-start(f32[32,8,256]{2,1,0:T(8,128)} %broadcast_in_dim.3), calls=%async_computation.2 | async-start | bytes 524288 | tf_op jit(solution)/shard_map/all_to_all | solution.py:239
  187.6 4.2 %collective-permute-start.9 = (f32[16,8,1536]{2,1,0:T(8,128)S(1)}, f32[16,8,1536]{2,1,0:T(8,128)S(1)}, u32[]{:S(2)}, u32[]{:S(2)}) collective-permute-start(f32[16,8,1536]{2,1,0:T(8,128)S(1)} %get-tuple-element.29), channel_id=1, source_target_pairs={{0,16},{16,0},{1,17},{17,1},{2,18},{18,2},{3,19},{19,3},{4,20},{20... | collective-permute-start | bytes 2359304 | tf_op jit(solution)/shard_map/ppermute | solution.py:235
